TPU v7x, 32 devices: a whole 2x2x4 slice. The times are simulated.
32 devices in a mesh: ctx: 8 (over z, core), tp: 4 (over y, x).
Axes of the slice: x: 2, y: 2, z: 4, core: 2. Of those that a mesh axis runs over, the one named last changes fastest.
Arguments:
- inputs: bfloat16 [2, 2, 2048, 2048], P(None, None, 'ctx'), may hold values from -6 to 6
- segments: int32 [2, 2, 2048], replicated, may hold values from 0 to 15, as said below
- keep_mask: int32 [2, 2, 2048], replicated, may hold values 0 or 1
- first_gain: float32 [2048], replicated, may hold values from 0.25 to 1.75
- first_shift: float32 [2048], replicated, may hold values from -4 to 4
- proj_weight: bfloat16 [2048, 3, 2048], P(None, None, 'tp'), may hold values from -0.125 to 0.125
- proj_bias: float32 [2, 2048], P(None, 'tp'), may hold values from -4 to 4
- mixer_weight: bfloat16 [2048, 2048], P('tp'), may hold values from -0.75 to 0.75
- mixer_bias: float32 [2048], replicated, may hold values from -4 to 4
- second_gain: float32 [2048], replicated, may hold values from 0.25 to 1.75
- second_shift: float32 [2048], replicated, may hold values from -4 to 4
- up_weight: bfloat16 [2048, 8192], P(None, 'tp'), may hold values from -0.125 to 0.125
- up_bias: float32 [8192], P('tp'), may hold values from -4 to 4
- down_weight: bfloat16 [8192, 2048], P('tp'), may hold values from -0.1875 to 0.1875
- down_bias: float32 [2048], replicated, may hold values from -4 to 4
- out_cotangent: bfloat16 [2, 2, 2048, 2048], P(None, None, 'ctx'), may hold values from -6 to 6
Outputs:
- outputs: bfloat16 [2, 2, 2048, 2048], P(None, None, 'ctx')
- input_grad: float32 [2, 2, 2048, 2048], P(None, None, 'ctx')
- first_gain_grad: float32 [2048], P('ctx')
- first_shift_grad: float32 [2048], P('ctx')
- proj_weight_grad: float32 [2048, 3, 2048], P('ctx', None, 'tp')
- proj_bias_grad: float32 [2, 2048], P(None, ('tp', 'ctx'))
- mixer_weight_grad: float32 [2048, 2048], P('tp', 'ctx')
- mixer_bias_grad: float32 [2048], P('ctx')
- second_gain_grad: float32 [2048], P('ctx')
- second_shift_grad: float32 [2048], P('ctx')
- up_weight_grad: float32 [2048, 8192], P('ctx', 'tp')
- up_bias_grad: float32 [8192], P(('tp', 'ctx'))
- down_weight_grad: float32 [8192, 2048], P('tp', 'ctx')
- down_bias_grad: float32 [2048], P('ctx')
Inputs may be any that keep to these rules, and one draw needn't show every extreme that they name: `segments`: document numbers never fall along a sequence; document 0 starts at position 0 and covers at least the first half of each sequence; the last position holds 15.
All inputs are finite; a program needn't handle non-finite values.
Results may differ from a plain program's by a relative error of at most 0.03.
Values may be sent and summed in bfloat16 or wider, within the bound.
No kernel may reach another device: no remote copies, remote signals or barrier semaphores. Data moves between devices by JAX's collectives and lax.ppermute only.
A program may use at most 256 MiB of HBM per device.

v0:
```python
import math

import jax
import jax.numpy as jnp
from jax import lax
from jax.sharding import PartitionSpec as P

HD = 128


def storage_order(values, part_count):
    leading = values.shape[:-1]
    blocks = values.reshape(leading + (2 * part_count, -1))
    front_half = blocks[..., :part_count, :]
    back_half = jnp.flip(blocks[..., part_count:, :], axis=-2)
    return jnp.stack([front_half, back_half], axis=-2).reshape(leading + (-1,))


def layer_norm(values, norm_gain, norm_shift):
    center = values - jnp.mean(values, axis=-1, keepdims=True)
    spread = jnp.mean(center * center, axis=-1, keepdims=True)
    return center * lax.rsqrt(spread + 1e-05) * norm_gain + norm_shift


def gelu_exact(values):
    return jax.nn.gelu(values, approximate=False)


def split_heads(rows, heads_here):
    return rows.reshape(rows.shape[0], rows.shape[1], heads_here, -1)


def scores_of(queries, key_all, allowed, heads_here, scaler):
    raw = (
        jnp.einsum(
            "sqhd,skhd->shqk",
            split_heads(queries, heads_here),
            split_heads(key_all, heads_here),
            preferred_element_type=jnp.float32,
        )
        * scaler
    )
    return jnp.where(allowed[:, None], raw, -1000000000.0)


def attend(queries, key_all, value_all, allowed, heads_here, scaler):
    masked = scores_of(queries, key_all, allowed, heads_here, scaler)
    top = jnp.max(masked, axis=-1, keepdims=True)
    raised = jnp.exp(masked - top)
    totals = jnp.sum(raised, axis=-1, keepdims=True)
    probs = raised / totals
    mixed = jnp.einsum(
        "shqk,skhd->sqhd",
        probs.astype(jnp.bfloat16),
        split_heads(value_all, heads_here),
        preferred_element_type=jnp.float32,
    )
    return (mixed.reshape(queries.shape), top + jnp.log(totals))


def attend_back(queries, key_all, value_all, allowed, log_total, grad_heads, heads_here, scaler):
    masked = scores_of(queries, key_all, allowed, heads_here, scaler)
    probs = jnp.exp(masked - log_total)
    grad_four = split_heads(grad_heads, heads_here)
    grad_value = jnp.einsum(
        "shqk,sqhd->skhd", probs.astype(jnp.bfloat16), grad_four, preferred_element_type=jnp.float32
    )
    grad_probs = jnp.einsum(
        "sqhd,skhd->shqk",
        grad_four,
        split_heads(value_all, heads_here),
        preferred_element_type=jnp.float32,
    )
    inner_sum = jnp.sum(probs * grad_probs, axis=-1, keepdims=True)
    grad_scores = (probs * (grad_probs - inner_sum)).astype(jnp.bfloat16)
    grad_query = (
        jnp.einsum(
            "shqk,skhd->sqhd",
            grad_scores,
            split_heads(key_all, heads_here),
            preferred_element_type=jnp.float32,
        )
        * scaler
    )
    grad_key = (
        jnp.einsum(
            "shqk,sqhd->skhd",
            grad_scores,
            split_heads(queries, heads_here),
            preferred_element_type=jnp.float32,
        )
        * scaler
    )
    return (
        grad_query.reshape(queries.shape),
        grad_key.reshape(key_all.shape),
        grad_value.reshape(value_all.shape),
    )


def reduce_grads(grads):
    return (
        lax.psum_scatter(
            grads[0].astype(jnp.bfloat16), "ctx", scatter_dimension=0, tiled=True
        ).astype(jnp.float32),
        lax.psum_scatter(
            grads[1].astype(jnp.bfloat16), "ctx", scatter_dimension=0, tiled=True
        ).astype(jnp.float32),
        lax.psum_scatter(
            grads[2].astype(jnp.bfloat16), "ctx", scatter_dimension=0, tiled=True
        ).astype(jnp.float32),
        lax.psum_scatter(
            grads[3].astype(jnp.bfloat16), "ctx", scatter_dimension=1, tiled=True
        ).astype(jnp.float32),
        lax.psum_scatter(
            grads[4].astype(jnp.bfloat16), "ctx", scatter_dimension=1, tiled=True
        ).astype(jnp.float32),
        lax.psum_scatter(
            grads[5].astype(jnp.bfloat16), "ctx", scatter_dimension=0, tiled=True
        ).astype(jnp.float32),
        lax.psum_scatter(
            grads[6].astype(jnp.bfloat16), "ctx", scatter_dimension=0, tiled=True
        ).astype(jnp.float32),
        lax.psum_scatter(
            grads[7].astype(jnp.bfloat16), "ctx", scatter_dimension=0, tiled=True
        ).astype(jnp.float32),
        lax.psum_scatter(
            grads[8].astype(jnp.bfloat16), "ctx", scatter_dimension=0, tiled=True
        ).astype(jnp.float32),
        lax.psum_scatter(
            grads[9].astype(jnp.bfloat16), "ctx", scatter_dimension=0, tiled=True
        ).astype(jnp.float32),
        lax.psum_scatter(
            grads[10].astype(jnp.bfloat16), "ctx", scatter_dimension=1, tiled=True
        ).astype(jnp.float32),
        lax.psum_scatter(
            grads[11].astype(jnp.bfloat16), "ctx", scatter_dimension=0, tiled=True
        ).astype(jnp.float32),
    )


def per_device(
    inputs,
    segments,
    keep_mask,
    first_gain,
    first_shift,
    proj_weight,
    proj_bias,
    mixer_weight,
    mixer_bias,
    second_gain,
    second_shift,
    up_weight,
    up_bias,
    down_weight,
    down_bias,
    out_cotangent,
):
    ctx_count = lax.axis_size("ctx")
    micro_count, seq_count, tok_len, model_width = inputs.shape
    inner_width = proj_bias.shape[1]
    heads_here = inner_width // HD
    scaler = 1.0 / math.sqrt(HD)
    seq_len = tok_len * ctx_count
    places = storage_order(jnp.arange(seq_len, dtype=jnp.int32), ctx_count)
    offset = lax.axis_index("ctx") * tok_len
    my_places = lax.dynamic_slice_in_dim(places, offset, tok_len, 0)
    seg_store = storage_order(segments, ctx_count)
    keep_store = storage_order(keep_mask, ctx_count)
    proj_flat = proj_weight.reshape(model_width, 3 * inner_width)
    bias_three = jnp.stack([proj_bias[0], jnp.zeros_like(proj_bias[0]), proj_bias[1]])
    causal = places[None, :] <= my_places[:, None]
    itself = places[None, :] == my_places[:, None]
    shaped_like = (
        first_gain,
        first_shift,
        proj_weight,
        proj_bias,
        mixer_weight,
        mixer_bias,
        second_gain,
        second_shift,
        up_weight,
        up_bias,
        down_weight,
        down_bias,
    )
    running = tuple((jnp.zeros(item.shape, jnp.float32) for item in shaped_like))
    out_list = []
    grad_list = []
    for micro_index in range(micro_count):
        x_now = inputs[micro_index].astype(jnp.float32)
        seg_keys = seg_store[micro_index]
        seg_mine = lax.dynamic_slice_in_dim(seg_keys, offset, tok_len, 1)
        visible = (keep_store[micro_index] > 0)[:, None, :] | itself[None]
        allowed = causal[None] & (seg_keys[:, None, :] == seg_mine[:, :, None]) & visible
        normed_one = layer_norm(x_now, first_gain, first_shift).astype(jnp.bfloat16)
        projected = jnp.einsum(
            "std,dc->stc", normed_one, proj_flat, preferred_element_type=jnp.float32
        )
        projected = (projected.reshape(seq_count, tok_len, 3, inner_width) + bias_three).astype(
            jnp.bfloat16
        )
        queries = projected[:, :, 0]
        key_here = projected[:, :, 1]
        value_here = projected[:, :, 2]
        key_all, value_all = (
            lax.all_gather(key_here, "ctx", axis=1, tiled=True),
            lax.all_gather(value_here, "ctx", axis=1, tiled=True),
        )
        heads_out, log_total = attend(queries, key_all, value_all, allowed, heads_here, scaler)
        heads_low = heads_out.astype(jnp.bfloat16)
        mixed_part = jnp.einsum(
            "stn,nd->std", heads_low, mixer_weight, preferred_element_type=jnp.float32
        )
        resid = (
            x_now + lax.psum(mixed_part.astype(jnp.bfloat16), "tp").astype(jnp.float32) + mixer_bias
        )
        normed_two = layer_norm(resid, second_gain, second_shift).astype(jnp.bfloat16)
        pre_act = (
            jnp.einsum("std,df->stf", normed_two, up_weight, preferred_element_type=jnp.float32)
            + up_bias
        )
        act_low = gelu_exact(pre_act).astype(jnp.bfloat16)
        feed_part = jnp.einsum(
            "stf,fd->std", act_low, down_weight, preferred_element_type=jnp.float32
        )
        feed = lax.psum(feed_part.astype(jnp.bfloat16), "tp").astype(jnp.float32) + down_bias
        out_list.append((resid + feed).astype(jnp.bfloat16))
        cot_low = out_cotangent[micro_index]
        cot_full = cot_low.astype(jnp.float32)
        down_bias_part = jnp.sum(cot_full, axis=(0, 1))
        down_part = jnp.einsum("stf,std->fd", act_low, cot_low, preferred_element_type=jnp.float32)
        grad_act = jnp.einsum(
            "std,fd->stf", cot_low, down_weight, preferred_element_type=jnp.float32
        )
        grad_pre = jax.vjp(gelu_exact, pre_act)[1](grad_act)[0].astype(jnp.bfloat16)
        up_part = jnp.einsum(
            "std,stf->df", normed_two, grad_pre, preferred_element_type=jnp.float32
        )
        up_bias_part = jnp.sum(grad_pre.astype(jnp.float32), axis=(0, 1))
        grad_two_part = jnp.einsum(
            "stf,df->std", grad_pre, up_weight, preferred_element_type=jnp.float32
        )
        grad_two = lax.psum(grad_two_part.astype(jnp.bfloat16), "tp").astype(jnp.float32)
        resid_part, second_gain_part, second_shift_part = jax.vjp(
            layer_norm, resid, second_gain, second_shift
        )[1](grad_two)
        grad_resid = cot_full + resid_part
        grad_mix = grad_resid.astype(jnp.bfloat16)
        mixer_bias_part = jnp.sum(grad_mix.astype(jnp.float32), axis=(0, 1))
        mixer_part = jnp.einsum(
            "stn,std->nd", heads_low, grad_mix, preferred_element_type=jnp.float32
        )
        grad_heads = jnp.einsum(
            "std,nd->stn", grad_mix, mixer_weight, preferred_element_type=jnp.float32
        ).astype(jnp.bfloat16)
        key_back, value_back = (key_all, value_all)
        grad_query, grad_key, grad_value = attend_back(
            queries, key_back, value_back, allowed, log_total, grad_heads, heads_here, scaler
        )
        key_share, value_share = (
            lax.psum_scatter(
                grad_key.astype(jnp.bfloat16), "ctx", scatter_dimension=1, tiled=True
            ).astype(jnp.float32),
            lax.psum_scatter(
                grad_value.astype(jnp.bfloat16), "ctx", scatter_dimension=1, tiled=True
            ).astype(jnp.float32),
        )
        grad_proj = jnp.stack([grad_query, key_share, value_share], axis=2).astype(jnp.bfloat16)
        proj_part = jnp.einsum(
            "std,stcn->dcn", normed_one, grad_proj, preferred_element_type=jnp.float32
        )
        proj_sums = jnp.sum(grad_proj.astype(jnp.float32), axis=(0, 1))
        proj_bias_part = jnp.stack([proj_sums[0], proj_sums[2]])
        grad_one_part = jnp.einsum(
            "stc,dc->std",
            grad_proj.reshape(seq_count, tok_len, 3 * inner_width),
            proj_flat,
            preferred_element_type=jnp.float32,
        )
        grad_one = lax.psum(grad_one_part.astype(jnp.bfloat16), "tp").astype(jnp.float32)
        input_part, first_gain_part, first_shift_part = jax.vjp(
            layer_norm, x_now, first_gain, first_shift
        )[1](grad_one)
        grad_list.append(grad_resid + input_part)
        batch_grads = (
            first_gain_part,
            first_shift_part,
            proj_part,
            proj_bias_part,
            mixer_part,
            mixer_bias_part,
            second_gain_part,
            second_shift_part,
            up_part,
            up_bias_part,
            down_part,
            down_bias_part,
        )
        running = tuple((earlier + adding for earlier, adding in zip(running, batch_grads)))
    final = reduce_grads(running)
    return (
        jnp.stack(out_list),
        jnp.stack(grad_list),
        final[0],
        final[1],
        final[2],
        final[3],
        final[4],
        final[5],
        final[6],
        final[7],
        final[8],
        final[9],
        final[10],
        final[11],
    )


def solution(mesh):
    in_specs = (
        P(None, None, "ctx", None),
        P(),
        P(),
        P(),
        P(),
        P(None, None, "tp"),
        P(None, "tp"),
        P("tp", None),
        P(),
        P(),
        P(),
        P(None, "tp"),
        P("tp"),
        P("tp", None),
        P(),
        P(None, None, "ctx", None),
    )
    out_specs = (
        P(None, None, "ctx", None),
        P(None, None, "ctx", None),
        P("ctx"),
        P("ctx"),
        P("ctx", None, "tp"),
        P(None, ("tp", "ctx")),
        P("tp", "ctx"),
        P("ctx"),
        P("ctx"),
        P("ctx"),
        P("ctx", "tp"),
        P(("tp", "ctx")),
        P("tp", "ctx"),
        P("ctx"),
    )
    return jax.shard_map(
        per_device, mesh=mesh, in_specs=in_specs, out_specs=out_specs, check_vma=False
    )
```

profile of v0, /device:TPU:0, one launch (start us, length us, event | category | flops | bytes accessed | tf_op | source)
XLA Modules:
  0.0 1380.3 jit_solution(7033520012287488483)
XLA Ops:
  34.3 44.3 %all-gather.11.cloned.1.call-done = bf16[2,2048,1,512]{3,1,2,0:T(8,128)(2,1)} async-done(((bf16[2,256,1,512]{3,1,2,0:T(8,128)(2,1)}), bf16[2,2048,1,512]{3,1,2,0:T(8,128)(2,1)}) %all-gather.11.cloned.1.call-update) | async-done | bytes 4194320 | tf_op jit(solution)/shard_map/all_gather | solution.py:209
  103.7 23.0 %all-gather.9.cloned.1.call-done = bf16[2,2048,1,512]{3,1,2,0:T(8,128)(2,1)} async-done(((bf16[2,256,1,512]{3,1,2,0:T(8,128)(2,1)}), bf16[2,2048,1,512]{3,1,2,0:T(8,128)(2,1)}) %all-gather.9.cloned.1.call-update) | async-done | bytes 4194320 | tf_op jit(solution)/shard_map/all_gather | solution.py:210
  147.4 68.0 %all-reduce.15.cloned.1.call-done = bf16[2,256,2048]{2,1,0:T(8,128)(2,1)} async-done(((bf16[2,256,2048]{2,1,0:T(8,128)(2,1)}), bf16[2,256,2048]{2,1,0:T(8,128)(2,1)}) %all-reduce.15.cloned.1.call-update) | async-done | bytes 2097168 | tf_op jit(solution)/shard_map/psum | solution.py:218
  228.1 46.5 %all-gather.15.cloned.1.call-done = bf16[2,2048,1,512]{3,1,2,0:T(8,128)(2,1)} async-done(((bf16[2,256,1,512]{3,1,2,0:T(8,128)(2,1)}), bf16[2,2048,1,512]{3,1,2,0:T(8,128)(2,1)}) %all-gather.15.cloned.1.call-update) | async-done | bytes 4194320 | tf_op jit(solution)/shard_map/all_gather | solution.py:209
  299.8 22.9 %all-gather.13.cloned.1.call-done = bf16[2,2048,1,512]{3,1,2,0:T(8,128)(2,1)} async-done(((bf16[2,256,1,512]{3,1,2,0:T(8,128)(2,1)}), bf16[2,2048,1,512]{3,1,2,0:T(8,128)(2,1)}) %all-gather.13.cloned.1.call-update) | async-done | bytes 4194320 | tf_op jit(solution)/shard_map/all_gather | solution.py:210
  343.1 68.2 %all-reduce.17.cloned.1.call-done = bf16[2,256,2048]{2,1,0:T(8,128)(2,1)} async-done(((bf16[2,256,2048]{2,1,0:T(8,128)(2,1)}), bf16[2,256,2048]{2,1,0:T(8,128)(2,1)}) %all-reduce.17.cloned.1.call-update) | async-done | bytes 2097168 | tf_op jit(solution)/shard_map/psum | solution.py:218
  425.4 14.1 %fusion.202 = (u8[256,2048]{1,0:T(8,128)(4,1)S(1)}, u8[256,2048]{1,0:T(8,128)(4,1)S(1)}, u8[256,2048]{1,0:T(8,128)(4,1)S(1)}, u8[256,2048]{1,0:T(8,128)(4,1)}, f32[2,256,2048]{2,1,0:T(8,128)}) fusion(f32[2048]{0:T(1024)S(1)} %copy-done.93, f32[2,256,2048]{2,1,0:T(8,128)S(1)} %fusion.23, bf16[2048,2048]{1,0:T(8,128)(2,1)} %param.27, ...), kind=kOutput, calls=%fused_computation.263 | convolution fusion | flops 4331667456 | bytes 23105536 | tf_op jit(solution)/shard_map/std,df->stf/dot_general | solution.py:222
  439.4 22.5 %multiply_convert_fusion.5 = (bf16[2,256,2048]{2,1,0:T(8,128)(2,1)}, f32[2,256,2048]{2,1,0:T(8,128)}, bf16[2,256,2048]{2,1,0:T(8,128)(2,1)}, f32[2,256,2048]{2,1,0:T(8,128)}) fusion(f32[2,256,2048]{2,1,0:T(8,128)} %get-tuple-element.107, f32[2048]{0:T(1024)S(1)} %copy-done.93, u8[256,2048]{1,0:T(8,128)(4,1)S(1)} %get-tuple-element.31, ...), kind=kLoop, calls=%fused_computation.168 | loop fusion | flops 147849216 | bytes 23076864 | tf_op jit(solution)/shard_map/convert_element_type | solution.py:225
  462.0 12.4 convert_reduce_fusion.9
  474.3 11.7 convert_reduce_fusion.8
  505.8 104.2 %all-reduce.21.cloned.1.call-done = (bf16[2,256,2048]{2,1,0:T(8,128)(2,1)}, bf16[2,256,2048]{2,1,0:T(8,128)(2,1)}) async-done(((bf16[2,256,2048]{2,1,0:T(8,128)(2,1)}, bf16[2,256,2048]{2,1,0:T(8,128)(2,1)}), (bf16[2,256,2048]{2,1,0:T(8,128)(2,1)}, bf16[2,256,2048]{2,1,0:T(8,128)(2,1)})) %all-reduce.21.cloned.1.call-update) | async-done | bytes 4194320 | tf_op jit(solution)/shard_map/psum | solution.py:246
  635.2 12.7 multiply_reduce_fusion
  647.9 11.8 multiply_convert_fusion
  691.6 13.0 multiply_reduce_fusion.1
  704.7 12.2 multiply_convert_fusion.1
  751.0 13.3 fusion.213
  782.1 39.6 %reduce-scatter.12.cloned.1.call-done = bf16[2,256,512]{2,1,0:T(8,128)(2,1)} async-done(((bf16[2,2048,512]{2,1,0:T(8,128)(2,1)}), bf16[2,256,512]{2,1,0:T(8,128)(2,1)}) %reduce-scatter.12.cloned.1.call-update) | async-done | bytes 524304 | tf_op jit(solution)/shard_map/reduce_scatter | solution.py:264
  821.8 50.6 %reduce-scatter.14.cloned.1.call-done = bf16[2,256,512]{2,1,0:T(8,128)(2,1)} async-done(((bf16[2,2048,512]{2,1,0:T(8,128)(2,1)}), bf16[2,256,512]{2,1,0:T(8,128)(2,1)}) %reduce-scatter.14.cloned.1.call-update) | async-done | bytes 524304 | tf_op jit(solution)/shard_map/reduce_scatter | solution.py:267
  875.0 15.7 %fusion.1 = bf16[2048,2048]{1,0:T(8,128)(2,1)} fusion(f32[2048,2048,1]{1,0,2:T(8,128)} %fusion.213, bf16[2,256,2048]{2,1,0:T(8,128)(2,1)} %get-tuple-element.115, f32[2,256]{1,0:T(2,128)S(1)} %fusion.212, f32[2048]{0:T(1024)S(1)} %copy-done.97, f32[2048]{0:T(1024)S(1)} %copy-done.48, f32[2,256]{1,0:T(2,128)S(1)} %broadcast_multiply_fusion, ...), kind=kOutput, calls=%fused_computation.3 | convolution fusion | flops 4312793088 | bytes 31485952 | tf_op jit(solution)/shard_map/std,stf->df/dot_general | solution.py:239
  890.8 12.7 fusion.149
  969.8 61.1 %reduce-scatter.24.cloned.1.call-done = bf16[256,2048]{1,0:T(8,128)(2,1)} async-done(((bf16[2048,2048]{1,0:T(8,128)(2,1)}), bf16[256,2048]{1,0:T(8,128)(2,1)}) %reduce-scatter.24.cloned.1.call-update) | async-done | bytes 1048592 | tf_op jit(solution)/shard_map/reduce_scatter | solution.py:127
  1033.6 87.3 %reduce-scatter.26.cloned.1.call-done = bf16[2048,256]{1,0:T(8,128)(2,1)} async-done(((bf16[2048,2048]{1,0:T(8,128)(2,1)}), bf16[2048,256]{1,0:T(8,128)(2,1)}) %reduce-scatter.26.cloned.1.call-update) | async-done | bytes 1048592 | tf_op jit(solution)/shard_map/reduce_scatter | solution.py:133
  1123.7 173.7 %all-reduce.19.cloned.1.call-done = (bf16[2,256,2048]{2,1,0:T(8,128)(2,1)}, bf16[2,256,2048]{2,1,0:T(8,128)(2,1)}, bf16[2,256,2048]{2,1,0:T(8,128)(2,1)}, bf16[2,256,2048]{2,1,0:T(8,128)(2,1)}) async-done(((bf16[2,256,2048]{2,1,0:T(8,128)(2,1)}, bf16[2,256,2048]{2,1,0:T(8,128)(2,1)}, bf16[2,256,2048]{2,1,0:T(8,128)(2,1)}, bf16[2,256,2048]{2,1,0:T(8,128)(2,1)}), (bf16[2,256,2048]{2,1,0:T(8,128)(2,1)}, ...) | async-done | bytes 8388624 | tf_op jit(solution)/shard_map/psum | solution.py:229
  1307.5 30.8 %all-reduce.7 = (bf16[2048]{0:T(1024)(128)(2,1)S(1)}, bf16[2048]{0:T(1024)(128)(2,1)S(1)}, bf16[2048]{0:T(1024)(128)(2,1)S(1)}, bf16[2048]{0:T(1024)(128)(2,1)S(...) all-reduce(bf16[2048]{0:T(1024)(128)(2,1)S(1)} %add_convert_fusion., ...), channel_id=10, replica_groups=mesh['ctx'=8,'tp'=4] {'ctx'}, use_global_device_ids=true, to_apply=%region_36.37.clone | all-reduce | flops 14336 | bytes 57344
  (377 shorter events, 391.6 us)
Async XLA Ops:
  7.2 137.1 %copy-start = (bf16[512,2048]{1,0:T(8,128)(2,1)S(1)}, bf16[512,2048]{1,0:T(8,128)(2,1)}, u32[]{:S(2)}) copy-start(bf16[512,2048]{1,0:T(8,128)(2,1)} %param.23) | copy-start | bytes 6291460
  7.2 71.4 %all-gather.11.cloned.1.call-start = ((), (), s32[]{:S(2)}) async-start(), calls=%async_computation.20 | async-start | bytes 4718592 | tf_op jit(solution)/shard_map/all_gather | solution.py:209
  10.3 209.4 %copy-start.58 = (f32[2,256]{1,0:T(2,128)}, f32[2,256]{1,0:T(2,128)S(1)}, u32[]{:S(2)}) copy-start(f32[2,256]{1,0:T(2,128)S(1)} %get-tuple-element.116) | copy-start | bytes 6148
  28.6 98.1 %all-gather.9.cloned.1.call-start = ((), (), s32[]{:S(2)}) async-start(), calls=%async_computation.19 | async-start | bytes 4718592 | tf_op jit(solution)/shard_map/all_gather | solution.py:210
  29.3 186.1 %all-reduce.15.cloned.1.call-start = ((), (), s32[]{:S(2)}) async-start(), calls=%async_computation.9 | async-start | bytes 4194304 | tf_op jit(solution)/shard_map/psum | solution.py:218
  146.9 127.6 %all-gather.15.cloned.1.call-start = ((), (), s32[]{:S(2)}) async-start(), calls=%async_computation.22 | async-start | bytes 4718592 | tf_op jit(solution)/shard_map/all_gather | solution.py:209
  227.2 95.4 %all-gather.13.cloned.1.call-start = ((), (), s32[]{:S(2)}) async-start(), calls=%async_computation.21 | async-start | bytes 4718592 | tf_op jit(solution)/shard_map/all_gather | solution.py:210
  227.8 183.4 %all-reduce.17.cloned.1.call-start = ((), (), s32[]{:S(2)}) async-start(), calls=%async_computation.10 | async-start | bytes 4194304 | tf_op jit(solution)/shard_map/psum | solution.py:218
  342.8 267.2 %all-reduce.21.cloned.1.call-start = ((), (), s32[]{:S(2)}) async-start(), calls=%async_computation.25 | async-start | bytes 8388608 | tf_op jit(solution)/shard_map/psum | solution.py:246
  343.1 407.9 %copy-start.56 = (f32[2,256]{1,0:T(2,128)}, f32[2,256]{1,0:T(2,128)S(1)}, u32[]{:S(2)}) copy-start(f32[2,256]{1,0:T(2,128)S(1)} %broadcast_multiply_fusion.2) | copy-start | bytes 6148
  416.6 458.3 %copy-start.54 = (f32[2,256]{1,0:T(2,128)}, f32[2,256]{1,0:T(2,128)S(1)}, u32[]{:S(2)}) copy-start(f32[2,256]{1,0:T(2,128)S(1)} %broadcast_multiply_fusion) | copy-start | bytes 6148
  417.7 457.3 %copy-start.77 = (f32[2,256]{1,0:T(2,128)}, f32[2,256]{1,0:T(2,128)S(1)}, u32[]{:S(2)}) copy-start(f32[2,256]{1,0:T(2,128)S(1)} %fusion.212) | copy-start | bytes 6148
  417.7 333.2 %copy-start.79 = (f32[2,256]{1,0:T(2,128)}, f32[2,256]{1,0:T(2,128)S(1)}, u32[]{:S(2)}) copy-start(f32[2,256]{1,0:T(2,128)S(1)} %fusion.210) | copy-start | bytes 6148
  505.7 275.0 %reduce-scatter.16.cloned.1.call-start = ((), (), s32[]{:S(2)}) async-start(), calls=%async_computation.13 | async-start | bytes 4718592 | tf_op jit(solution)/shard_map/reduce_scatter | solution.py:264
  670.6 110.1 %reduce-scatter.18.cloned.1.call-start = ((), (), s32[]{:S(2)}) async-start(), calls=%async_computation.14 | async-start | bytes 4718592 | tf_op jit(solution)/shard_map/reduce_scatter | solution.py:267
  687.8 133.9 %reduce-scatter.12.cloned.1.call-start = ((), (), s32[]{:S(2)}) async-start(), calls=%async_computation.11 | async-start | bytes 4718592 | tf_op jit(solution)/shard_map/reduce_scatter | solution.py:264
  727.8 144.6 %reduce-scatter.14.cloned.1.call-start = ((), (), s32[]{:S(2)}) async-start(), calls=%async_computation.12 | async-start | bytes 4718592 | tf_op jit(solution)/shard_map/reduce_scatter | solution.py:267
  744.9 221.7 %reduce-scatter.22.cloned.1.call-start = ((), (), s32[]{:S(2)}) async-start(), calls=%async_computation.16 | async-start | bytes 2359296 | tf_op jit(solution)/shard_map/reduce_scatter | solution.py:115
  750.9 217.5 %reduce-scatter.28.cloned.1.call-start = ((), (), s32[]{:S(2)}) async-start(), calls=%async_computation.23 | async-start | bytes 147456
  779.2 95.7 %copy-start.13 = (bf16[2,256,2048]{2,1,0:T(8,128)(2,1)S(1)}, bf16[2,256,2048]{2,1,0:T(8,128)(2,1)}, u32[]{:S(2)}) copy-start(bf16[2,256,2048]{2,1,0:T(8,128)(2,1)} %all-reduce.17.cloned.1.call-done) | copy-start | bytes 6291460
  874.7 156.2 %reduce-scatter.24.cloned.1.call-start = ((), (), s32[]{:S(2)}) async-start(), calls=%async_computation.17 | async-start | bytes 9437184 | tf_op jit(solution)/shard_map/reduce_scatter | solution.py:127
  890.7 230.3 %reduce-scatter.26.cloned.1.call-start = ((), (), s32[]{:S(2)}) async-start(), calls=%async_computation.18 | async-start | bytes 9437184 | tf_op jit(solution)/shard_map/reduce_scatter | solution.py:133
  913.9 383.5 %all-reduce.19.cloned.1.call-start = ((), (), s32[]{:S(2)}) async-start(), calls=%async_computation.24 | async-start | bytes 16777216 | tf_op jit(solution)/shard_map/psum | solution.py:229
  943.0 427.9 %reduce-scatter.20.cloned.1.call-start = ((), (), s32[]{:S(2)}) async-start(), calls=%async_computation.15 | async-start | bytes 7077888 | tf_op jit(solution)/shard_map/reduce_scatter | solution.py:109
  (97 other events, 1014.2 us)
Sparse Core Ops, SparseCore 0:
  28.7 49.8 all-gather.10
  80.7 45.8 all-gather.8
  147.0 68.3 all-reduce.14
  227.3 47.1 all-gather.14
  276.6 45.9 all-gather.12
  342.9 68.2 all-reduce.16
  505.8 104.1 all-reduce.20
  670.7 49.9 reduce-scatter.15
  723.1 48.1 reduce-scatter.17
  773.6 48.1 reduce-scatter.11
  824.2 48.1 reduce-scatter.13
  874.6 33.9 reduce-scatter.21
  911.5 28.7 reduce-scatter.27
  943.0 87.8 reduce-scatter.23
  1033.0 87.9 reduce-scatter.25
  1125.4 172.0 all-reduce.18
  1299.7 71.0 reduce-scatter.19
where the time goes:
time: 1390 us; the launch traced here: 1380 us
  waiting for transfers between devices  798 us (57%)
  matrix products  302 us (22%)
  other arithmetic  149 us (11%)
  local copies, waits for them, and re-layouts  82 us (6%)
  blocking collectives  30.8 us (2%)
  between operations  16.5 us (1%)
    psum x1, waiting for transfers between devices, per_device(): lax.psum(feed_part.astype(jnp.bfloat16), 'tp').astype(jnp.float32)  174 us
    psum x2, waiting for transfers between devices, per_device(): lax.psum(mixed_part.astype(jnp.bfloat16), 'tp').astype(jnp.float32)  136 us
    psum x1, waiting for transfers between devices, per_device(): lax.psum(grad_two_part.astype(jnp.bfloat16), 'tp').astype(jnp.float32)  104 us
    all_gather x2, waiting for transfers between devices, per_device(): lax.all_gather(key_here, 'ctx', axis=1, tiled=True)  90.7 us
    reduce_scatter x1, waiting for transfers between devices, reduce_grads(): lax.psum_scatter(grads[10].astype(jnp.bfloat16), 'ctx', scatter_dimension...  87.3 us
    reduce_scatter x1, waiting for transfers between devices, reduce_grads(): lax.psum_scatter(grads[8].astype(jnp.bfloat16), 'ctx', scatter_dimension=...  61.1 us
    reduce_scatter x2, waiting for transfers between devices, per_device(): lax.psum_scatter(grad_value.astype(jnp.bfloat16), 'ctx', scatter_dimensio...  50.6 us
    all_gather x2, waiting for transfers between devices, per_device(): lax.all_gather(value_here, 'ctx', axis=1, tiled=True)  45.8 us
  transfers between devices with their start and end apart: 17, of which 13 were waited for; matrix products, arithmetic and copies ran while one was open for 21% of the time, Pallas kernels for 0%

commit v1 on v0

--- a/solution.py
+++ b/solution.py
@@ -3,6 +3,8 @@
 import jax
 import jax.numpy as jnp
 from jax import lax
+from jax.experimental import pallas as pl
+from jax.experimental.pallas import tpu as pltpu
 from jax.sharding import PartitionSpec as P
 
 HD = 128
@@ -319,6 +321,889 @@
     )
 
 
+BF = jnp.bfloat16
+F32 = jnp.float32
+LOG2E = 1.4426950408889634
+LOW = -1e30
+ORDERS = ((1, 2), (2, 1))
+
+
+def xor_permute(values, axis, step):
+    count = lax.axis_size(axis)
+    return lax.ppermute(values, axis, [(i, i ^ step) for i in range(count)])
+
+
+def sds(shape, dtype=BF):
+    return jax.ShapeDtypeStruct(tuple(shape), dtype)
+
+
+def run_kernel(body, outs, args, flops=0, exps=0, scratch=(), limit=48, name=None):
+    specs = []
+    moved = 0
+    for arg in args:
+        if arg.dtype == jnp.int32 and arg.size <= 8:
+            specs.append(pl.BlockSpec(memory_space=pltpu.SMEM))
+        else:
+            specs.append(pl.BlockSpec(memory_space=pltpu.VMEM))
+            moved += arg.size * arg.dtype.itemsize
+    moved += sum(math.prod(o.shape) * o.dtype.itemsize for o in outs)
+    return pl.pallas_call(
+        body,
+        out_shape=tuple(outs),
+        in_specs=specs,
+        out_specs=tuple(pl.BlockSpec(memory_space=pltpu.VMEM) for _ in outs),
+        scratch_shapes=list(scratch),
+        compiler_params=pltpu.CompilerParams(vmem_limit_bytes=limit << 20),
+        cost_estimate=pl.CostEstimate(
+            flops=flops, bytes_accessed=moved, transcendentals=exps
+        ),
+        name=name,
+    )(*args)
+
+
+def rows_at(start, count):
+    return pl.ds(pl.multiple_of(start, count), count)
+
+
+def shard_reduce(messages):
+    sums = []
+    for part, (first, second) in enumerate(ORDERS):
+        send, keep = messages[2 * part], messages[2 * part + 1]
+        got = xor_permute(send, "tp", first)
+        middle = (keep[1].astype(F32) + got[1].astype(F32)).astype(BF)
+        sums += [keep, got, xor_permute(middle, "tp", second)]
+    return sums
+
+
+def shard_gather(halves):
+    pieces = []
+    for part, (first, second) in enumerate(ORDERS):
+        near = xor_permute(halves[part], "tp", first)
+        far = xor_permute(jnp.stack([halves[part], near]), "tp", second)
+        pieces += [halves[part], near, far]
+    return pieces
+
+
+def total_of(refs):
+    halves = []
+    for part in range(2):
+        keep, got, late = refs[3 * part : 3 * part + 3]
+        halves.append(
+            keep[0].astype(F32) + got[0].astype(F32) + late[...].astype(F32)
+        )
+    return jnp.concatenate(halves, axis=0)
+
+
+def place_gathered(store, tp_here, refs, size):
+    half = size // 2
+    for part, (first, second) in enumerate(ORDERS):
+        mine, near, far = refs[3 * part : 3 * part + 3]
+        parts = ((0, mine[...]), (first, near[...]), (second, far[0]), (first | second, far[1]))
+        for step, value in parts:
+            store(rows_at((tp_here ^ step) * size + part * half, half), value)
+
+
+def emit_messages(load, tp_here, refs, size):
+    half = size // 2
+    for part, (first, second) in enumerate(ORDERS):
+        send, keep = refs[2 * part], refs[2 * part + 1]
+        for ref, steps in ((send, (first, first | second)), (keep, (0, second))):
+            for place, step in enumerate(steps):
+                ref[place] = load(rows_at((tp_here ^ step) * size + part * half, half))
+
+
+def message_shapes(half, width):
+    return [sds((2, half, width)) for _ in range(4)]
+
+
+def exchange(local, cross, first, second, third):
+    got = [
+        xor_permute(item, "ctx", 2 * (place + 1))
+        for place, item in enumerate((first, second, third))
+    ]
+    packed = jnp.stack([cross] + [item[1] for item in got])
+    return [local] + got + [xor_permute(packed, "ctx", 1)]
+
+
+def exchanged(refs, here):
+    local, first, second, third, packed = refs
+    return (
+        (here, local[...]),
+        (here ^ 1, packed[0]),
+        (here ^ 2, first[0]),
+        (here ^ 3, packed[1]),
+        (here ^ 4, second[0]),
+        (here ^ 5, packed[2]),
+        (here ^ 6, third[0]),
+        (here ^ 7, packed[3]),
+    )
+
+
+def emit_exchange(load, here, refs):
+    local, cross, first, second, third = refs
+    local[...] = load(here)
+    cross[...] = load(here ^ 1)
+    for place, ref in enumerate((first, second, third)):
+        other = here ^ (2 * (place + 1))
+        ref[0] = load(other)
+        ref[1] = load(other ^ 1)
+
+
+def exchange_shapes(rows, width):
+    return [sds((rows, width)), sds((rows, width))] + [sds((2, rows, width))] * 3
+
+
+def normalized(values):
+    center = values - jnp.mean(values, axis=-1, keepdims=True)
+    spread = jnp.mean(center * center, axis=-1, keepdims=True)
+    root = lax.rsqrt(spread + 1e-05)
+    return center * root, root
+
+
+def norm_back(values, gain, grad):
+    unit, root = normalized(values)
+    scaled = grad * gain
+    back = root * (
+        scaled
+        - jnp.mean(scaled, axis=-1, keepdims=True)
+        - unit * jnp.mean(scaled * unit, axis=-1, keepdims=True)
+    )
+    gain_sum = jnp.sum(grad * unit, axis=0, keepdims=True)
+    shift_sum = jnp.sum(grad, axis=0, keepdims=True)
+    return back, gain_sum, shift_sum
+
+
+def dot(left, right):
+    return jnp.dot(left, right, preferred_element_type=F32)
+
+
+def dot_nt(left, right):
+    return lax.dot_general(left, right, (((1,), (1,)), ((), ())), preferred_element_type=F32)
+
+
+def dot_tn(left, right):
+    return lax.dot_general(left, right, (((0,), (0,)), ((), ())), preferred_element_type=F32)
+
+
+def project(here, x_rows, gain, shift, weight, bias, tok_len):
+    rows, width = x_rows.shape
+    inner = weight.shape[2]
+    heads = inner // HD
+
+    def body(here_ref, x_ref, gain_ref, shift_ref, weight_ref, bias_ref, *rest):
+        norm_ref, outs, held = rest[0], rest[1:6], rest[6]
+        unit, _ = normalized(x_ref[...].astype(F32))
+        norm_ref[...] = (unit * gain_ref[...] + shift_ref[...]).astype(BF)
+        for part in range(3):
+            value = dot(norm_ref[...], weight_ref[part]) + bias_ref[part : part + 1]
+            value = value.astype(BF)
+            for head in range(heads):
+                held[head, :, part * HD : (part + 1) * HD] = value[:, head * HD : (head + 1) * HD]
+
+        def load(unit_id):
+            return held[unit_id % heads, rows_at(unit_id // heads * tok_len, tok_len), :]
+
+        emit_exchange(load, here_ref[0], outs)
+
+    return run_kernel(
+        body,
+        [sds((rows, width))] + exchange_shapes(tok_len, 3 * HD),
+        [here, x_rows, gain, shift, weight, bias],
+        flops=6 * rows * width * inner,
+        scratch=[pltpu.VMEM((heads, rows, 3 * HD), BF)],
+        name="project",
+    )
+
+
+def rows_of_device(device, block, blocks):
+    return (
+        rows_at(device * block, block),
+        rows_at((blocks - 1 - device) * block, block),
+    )
+
+
+def attention(here, received, seg_column, key_row, heads):
+    tok_len = received[0].shape[0]
+    block = tok_len // 2
+    seq_len = seg_column.shape[1]
+    blocks = seq_len // block
+    step = 256
+    factor = LOG2E / math.sqrt(HD)
+
+    def body(here_ref, *rest):
+        refs, seg_ref, key_ref = rest[:5], rest[5], rest[6]
+        outs, lse_ref = rest[7:12], rest[12]
+        q_all, k_turned, v_all, mixed = rest[13:]
+        me = here_ref[0]
+        seq = me // heads
+        for device, value in exchanged(refs, me):
+            for half, place in enumerate(rows_of_device(device, block, blocks)):
+                rows = value[half * block : (half + 1) * block]
+                q_all[place] = rows[:, :HD]
+                k_turned[:, place] = rows[:, HD : 2 * HD].T
+                v_all[place] = rows[:, 2 * HD :]
+        for number in range(seq_len // step):
+            start, stop = number * step, (number + 1) * step
+            segs = seg_ref[seq, start:stop]
+            scores = dot(q_all[start:stop], k_turned[:, :stop]) * factor
+            scores = masked(scores, segs, key_ref, seq, start, stop)
+            top = jnp.max(scores, axis=-1, keepdims=True)
+            raised = jnp.exp2(scores - top)
+            total = jnp.sum(raised, axis=-1, keepdims=True)
+            out = dot(raised.astype(BF), v_all[:stop]) / total
+            mixed[start:stop] = out.astype(BF)
+            lse_ref[start:stop] = top + jnp.log2(total)
+
+        def load(device):
+            return jnp.concatenate(
+                [mixed[place] for place in rows_of_device(device, block, blocks)], axis=0
+            )
+
+        emit_exchange(load, me, outs)
+
+    return run_kernel(
+        body,
+        exchange_shapes(tok_len, HD) + [sds((seq_len, 1), F32)],
+        [here] + list(received) + [seg_column, key_row],
+        flops=2 * 2 * seq_len * seq_len * HD,
+        exps=seq_len * seq_len // 2,
+        scratch=[
+            pltpu.VMEM((seq_len, HD), BF),
+            pltpu.VMEM((HD, seq_len), BF),
+            pltpu.VMEM((seq_len, HD), BF),
+            pltpu.VMEM((seq_len, HD), BF),
+        ],
+        name="attention",
+    )
+
+
+def masked(scores, segs, key_ref, seq, start, stop):
+    size = stop - start
+    row = lax.broadcasted_iota(jnp.int32, (size, size), 0)
+    column = lax.broadcasted_iota(jnp.int32, (size, size), 1)
+    same = segs == key_ref[seq, :, start:stop]
+    seen = (same & (column < row)) | (column == row)
+    corner = jnp.where(seen, scores[:, start:], LOW)
+    if start == 0:
+        return corner
+    left = jnp.where(segs == key_ref[seq, :, :start], scores[:, :start], LOW)
+    return jnp.concatenate([left, corner], axis=1)
+
+
+def attention_back(here, received, grads, seg_column, key_row, lse, heads):
+    tok_len = received[0].shape[0]
+    block = tok_len // 2
+    seq_len = seg_column.shape[1]
+    blocks = seq_len // block
+    step = 256
+    scaler = 1.0 / math.sqrt(HD)
+
+    def body(here_ref, *rest):
+        refs, grad_refs = rest[:5], rest[5:10]
+        seg_ref, key_ref, lse_ref = rest[10:13]
+        outs = rest[13:18]
+        q_all, k_all, k_turned, v_turned, g_all, result, dk_turned, dv_turned = rest[18:]
+        me = here_ref[0]
+        seq = me // heads
+        for device, value in exchanged(refs, me):
+            for half, place in enumerate(rows_of_device(device, block, blocks)):
+                rows = value[half * block : (half + 1) * block]
+                q_all[place] = rows[:, :HD]
+                k_all[place] = rows[:, HD : 2 * HD]
+                k_turned[:, place] = rows[:, HD : 2 * HD].T
+                v_turned[:, place] = rows[:, 2 * HD :].T
+        for device, value in exchanged(grad_refs, me):
+            for half, place in enumerate(rows_of_device(device, block, blocks)):
+                g_all[place] = value[half * block : (half + 1) * block]
+        last = seq_len // step - 1
+        for number in range(last, -1, -1):
+            start, stop = number * step, (number + 1) * step
+            segs = seg_ref[seq, start:stop]
+            query, grad = q_all[start:stop], g_all[start:stop]
+            scores = dot(query, k_turned[:, :stop]) * (scaler * LOG2E)
+            scores = masked(scores, segs, key_ref, seq, start, stop)
+            probs = jnp.exp2(scores - lse_ref[start:stop])
+            grad_probs = dot(grad, v_turned[:, :stop])
+            inner = jnp.sum(probs * grad_probs, axis=-1, keepdims=True)
+            grad_scores = (probs * (grad_probs - inner)).astype(BF)
+            dv_part = dot_tn(grad, probs.astype(BF))
+            dk_part = dot_tn(query, grad_scores)
+            if number == last:
+                dv_turned[...] = dv_part
+                dk_turned[...] = dk_part
+            else:
+                dv_turned[:, :stop] += dv_part
+                dk_turned[:, :stop] += dk_part
+            dq = dot(grad_scores, k_all[:stop]) * scaler
+            result[start:stop, :HD] = dq.astype(BF)
+        for number in range(last + 1):
+            start, stop = number * step, (number + 1) * step
+            result[start:stop, HD : 2 * HD] = (dk_turned[:, start:stop] * scaler).T.astype(BF)
+            result[start:stop, 2 * HD :] = dv_turned[:, start:stop].T.astype(BF)
+
+        def load(device):
+            return jnp.concatenate(
+                [result[place] for place in rows_of_device(device, block, blocks)], axis=0
+            )
+
+        emit_exchange(load, me, outs)
+
+    return run_kernel(
+        body,
+        exchange_shapes(tok_len, 3 * HD),
+        [here] + list(received) + list(grads) + [seg_column, key_row, lse],
+        flops=5 * 2 * seq_len * seq_len * HD // 2,
+        exps=seq_len * seq_len // 2,
+        scratch=[
+            pltpu.VMEM((seq_len, HD), BF),
+            pltpu.VMEM((seq_len, HD), BF),
+            pltpu.VMEM((HD, seq_len), BF),
+            pltpu.VMEM((HD, seq_len), BF),
+            pltpu.VMEM((seq_len, HD), BF),
+            pltpu.VMEM((seq_len, 3 * HD), BF),
+            pltpu.VMEM((HD, seq_len), F32),
+            pltpu.VMEM((HD, seq_len), F32),
+        ],
+        name="attention_back",
+    )
+
+
+def mix_heads(here, tp_here, received, weight, heads):
+    tok_len = received[0].shape[0]
+    inner, width = weight.shape
+    rows = len_units(received) * tok_len // heads
+    size = rows // 4
+
+    def body(here_ref, tp_ref, *rest):
+        refs, weight_ref = rest[:5], rest[5]
+        heads_ref, outs, held = rest[6], rest[7:11], rest[11]
+        for unit_id, value in exchanged(refs, here_ref[0]):
+            column = pl.multiple_of(unit_id % heads * HD, HD)
+            heads_ref[rows_at(unit_id // heads * tok_len, tok_len), pl.ds(column, HD)] = value
+        for start in range(0, width, 512):
+            held[:, start : start + 512] = dot(
+                heads_ref[...], weight_ref[:, start : start + 512]
+            ).astype(BF)
+        emit_messages(lambda place: held[place, :], tp_ref[0], outs, size)
+
+    return run_kernel(
+        body,
+        [sds((rows, inner))] + message_shapes(size // 2, width),
+        [here, tp_here] + list(received) + [weight],
+        flops=2 * rows * inner * width,
+        scratch=[pltpu.VMEM((rows, width), BF)],
+        name="mix_heads",
+    )
+
+
+def len_units(received):
+    return 2 * received[-1].shape[0]
+
+
+def second_norm(tp_here, sums, x_rows, mixer_bias, gain, shift):
+    rows, width = x_rows.shape
+    size = rows // 4
+
+    def body(tp_ref, *rest):
+        refs, x_ref, bias_ref, gain_ref, shift_ref = rest[:6], *rest[6:10]
+        resid_ref, low_ref, high_ref = rest[10:]
+        mine = x_ref[rows_at(tp_ref[0] * size, size), :].astype(F32)
+        resid = mine + total_of(refs) + bias_ref[...]
+        resid_ref[...] = resid
+        unit, _ = normalized(resid)
+        value = (unit * gain_ref[...] + shift_ref[...]).astype(BF)
+        low_ref[...] = value[: size // 2]
+        high_ref[...] = value[size // 2 :]
+
+    return run_kernel(
+        body,
+        [sds((size, width), F32)] + [sds((size // 2, width))] * 2,
+        [tp_here] + list(sums) + [x_rows, mixer_bias, gain, shift],
+        name="second_norm",
+    )
+
+
+def erf_of(value):
+    return lax.erf(value)
+
+
+def feed_forward(tp_here, pieces, cot, up_weight, up_bias, down_weight):
+    rows, width = cot.shape
+    hidden = up_weight.shape[1]
+    size = rows // 4
+    step = 256
+    count = hidden // step
+
+    def body(tp_ref, *rest):
+        refs, cot_ref, up_ref, bias_ref, down_ref = rest[:6], *rest[6:10]
+        norm_ref, act_ref, pre_ref, sum_ref = rest[10:14]
+        feed_outs, grad_outs = rest[14:18], rest[18:22]
+        feed, grad = rest[22:]
+        number = pl.program_id(0)
+
+        @pl.when(number == 0)
+        def _():
+            def store(place, value):
+                norm_ref[place, :] = value
+
+            place_gathered(store, tp_ref[0], refs, size)
+
+        pre = dot(norm_ref[...], up_ref[...]) + bias_ref[...]
+        grad_act = dot_nt(cot_ref[...], down_ref[...])
+        spread = 0.5 + 0.5 * erf_of(pre * math.sqrt(0.5))
+        dense = jnp.exp(-0.5 * pre * pre) * (1.0 / math.sqrt(2.0 * math.pi))
+        act = (pre * spread).astype(BF)
+        grad_pre = (grad_act * (spread + pre * dense)).astype(BF)
+        act_ref[...] = act
+        pre_ref[...] = grad_pre
+        sum_ref[...] = jnp.sum(grad_pre.astype(F32), axis=0, keepdims=True)
+        feed_part = dot(act, down_ref[...])
+        grad_part = dot_nt(grad_pre, up_ref[...])
+
+        @pl.when(number == 0)
+        def _():
+            feed[...] = feed_part
+            grad[...] = grad_part
+
+        @pl.when(number > 0)
+        def _():
+            feed[...] += feed_part
+            grad[...] += grad_part
+
+        @pl.when(number == count - 1)
+        def _():
+            emit_messages(lambda at: feed[at, :].astype(BF), tp_ref[0], feed_outs, size)
+            emit_messages(lambda at: grad[at, :].astype(BF), tp_ref[0], grad_outs, size)
+
+    whole = lambda *shape: pl.BlockSpec(shape, lambda i: (0,) * len(shape))
+    in_specs = (
+        [pl.BlockSpec(memory_space=pltpu.SMEM)]
+        + [whole(*piece.shape) for piece in pieces]
+        + [
+            whole(rows, width),
+            pl.BlockSpec((width, step), lambda i: (0, i)),
+            pl.BlockSpec((1, step), lambda i: (0, i)),
+            pl.BlockSpec((step, width), lambda i: (i, 0)),
+        ]
+    )
+    out_specs = (
+        [
+            whole(rows, width),
+            pl.BlockSpec((rows, step), lambda i: (0, i)),
+            pl.BlockSpec((rows, step), lambda i: (0, i)),
+            pl.BlockSpec((1, step), lambda i: (0, i)),
+        ]
+        + [whole(2, size // 2, width)] * 8
+    )
+    outs = (
+        [sds((rows, width)), sds((rows, hidden)), sds((rows, hidden)), sds((1, hidden), F32)]
+        + message_shapes(size // 2, width)
+        + message_shapes(size // 2, width)
+    )
+    return pl.pallas_call(
+        body,
+        grid=(count,),
+        out_shape=tuple(outs),
+        in_specs=in_specs,
+        out_specs=tuple(out_specs),
+        scratch_shapes=[pltpu.VMEM((rows, width), F32), pltpu.VMEM((rows, width), F32)],
+        compiler_params=pltpu.CompilerParams(vmem_limit_bytes=56 << 20),
+        cost_estimate=pl.CostEstimate(
+            flops=8 * rows * width * hidden,
+            bytes_accessed=4 * width * hidden + 20 * rows * width,
+            transcendentals=2 * rows * hidden,
+        ),
+        name="feed_forward",
+    )(tp_here, *pieces, cot, up_weight, up_bias, down_weight)
+
+
+def second_norm_back(tp_here, sums, resid, cot, gain):
+    size, width = resid.shape
+
+    def body(tp_ref, *rest):
+        refs, resid_ref, cot_ref, gain_ref = rest[:6], *rest[6:9]
+        grad_ref, low_ref, high_ref, gain_out, shift_out = rest[9:]
+        back, gain_sum, shift_sum = norm_back(resid_ref[...], gain_ref[...], total_of(refs))
+        grad = back + cot_ref[rows_at(tp_ref[0] * size, size), :].astype(F32)
+        grad_ref[...] = grad
+        low = grad.astype(BF)
+        low_ref[...] = low[: size // 2]
+        high_ref[...] = low[size // 2 :]
+        gain_out[...] = gain_sum
+        shift_out[...] = shift_sum
+
+    return run_kernel(
+        body,
+        [sds((size, width), F32)]
+        + [sds((size // 2, width))] * 2
+        + [sds((1, width), F32)] * 2,
+        [tp_here] + list(sums) + [resid, cot, gain],
+        name="second_norm_back",
+    )
+
+
+def first_norm_back(tp_here, sums, x_rows, grad_resid, gain):
+    size, width = grad_resid.shape
+
+    def body(tp_ref, *rest):
+        refs, x_ref, grad_ref, gain_ref = rest[:6], *rest[6:9]
+        low_ref, high_ref, gain_out, shift_out = rest[9:]
+        mine = x_ref[rows_at(tp_ref[0] * size, size), :].astype(F32)
+        back, gain_sum, shift_sum = norm_back(mine, gain_ref[...], total_of(refs))
+        low = (back + grad_ref[...]).astype(BF)
+        low_ref[...] = low[: size // 2]
+        high_ref[...] = low[size // 2 :]
+        gain_out[...] = gain_sum
+        shift_out[...] = shift_sum
+
+    return run_kernel(
+        body,
+        [sds((size // 2, width))] * 2 + [sds((1, width), F32)] * 2,
+        [tp_here] + list(sums) + [x_rows, grad_resid, gain],
+        name="first_norm_back",
+    )
+
+
+def finish_output(sums, resid, bias):
+    size, width = resid.shape
+
+    def body(*rest):
+        refs, resid_ref, bias_ref, low_ref, high_ref = rest[:6], *rest[6:]
+        value = (resid_ref[...] + total_of(refs) + bias_ref[...]).astype(BF)
+        low_ref[...] = value[: size // 2]
+        high_ref[...] = value[size // 2 :]
+
+    return run_kernel(
+        body,
+        [sds((size // 2, width))] * 2,
+        list(sums) + [resid, bias],
+        name="finish_output",
+    )
+
+
+def heads_back(here, tp_here, pieces, weight, tok_len):
+    inner, width = weight.shape
+    heads = inner // HD
+    size = 2 * pieces[0].shape[0]
+    rows = 4 * size
+
+    def body(here_ref, tp_ref, *rest):
+        refs, weight_ref = rest[:6], rest[6]
+        mix_ref, sum_ref, outs, held = rest[7], rest[8], rest[9:14], rest[14]
+
+        def store(place, value):
+            mix_ref[place, :] = value
+
+        place_gathered(store, tp_ref[0], refs, size)
+        sum_ref[...] = jnp.sum(mix_ref[...].astype(F32), axis=0, keepdims=True)
+        value = dot_nt(mix_ref[...], weight_ref[...]).astype(BF)
+        for head in range(heads):
+            held[head] = value[:, head * HD : (head + 1) * HD]
+
+        def load(unit_id):
+            return held[unit_id % heads, rows_at(unit_id // heads * tok_len, tok_len), :]
+
+        emit_exchange(load, here_ref[0], outs)
+
+    return run_kernel(
+        body,
+        [sds((rows, width)), sds((1, width), F32)] + exchange_shapes(tok_len, HD),
+        [here, tp_here] + list(pieces) + [weight],
+        flops=2 * rows * inner * width,
+        scratch=[pltpu.VMEM((heads, rows, HD), BF)],
+        name="heads_back",
+    )
+
+
+def project_back(here, tp_here, received, weight):
+    tok_len = received[0].shape[0]
+    _, width, inner = weight.shape
+    heads = inner // HD
+    rows = len_units(received) * tok_len // heads
+    size = rows // 4
+
+    def body(here_ref, tp_ref, *rest):
+        refs, weight_ref = rest[:5], rest[5]
+        proj_ref, sum_ref, outs, held = rest[6], rest[7], rest[8:12], rest[12]
+        for unit_id, value in exchanged(refs, here_ref[0]):
+            place = rows_at(unit_id // heads * tok_len, tok_len)
+            for part in range(3):
+                column = pl.multiple_of(part * inner + unit_id % heads * HD, HD)
+                proj_ref[place, pl.ds(column, HD)] = value[:, part * HD : (part + 1) * HD]
+        sum_ref[...] = jnp.sum(proj_ref[...].astype(F32), axis=0, keepdims=True)
+        for start in range(0, width, 512):
+            value = dot_nt(proj_ref[:, :inner], weight_ref[0, start : start + 512])
+            for part in range(1, 3):
+                value += dot_nt(
+                    proj_ref[:, part * inner : (part + 1) * inner],
+                    weight_ref[part, start : start + 512],
+                )
+            held[:, start : start + 512] = value.astype(BF)
+        emit_messages(lambda place: held[place, :], tp_ref[0], outs, size)
+
+    return run_kernel(
+        body,
+        [sds((rows, 3 * inner)), sds((1, 3 * inner), F32)] + message_shapes(size // 2, width),
+        [here, tp_here] + list(received) + [weight],
+        flops=6 * rows * inner * width,
+        scratch=[pltpu.VMEM((rows, width), BF)],
+        name="project_back",
+    )
+
+
+def assemble(tp_here, pieces, earlier, index, count, dtype):
+    half, width = pieces[0].shape
+    size = 2 * half
+    rows = 4 * size
+
+    def body(tp_ref, *rest):
+        refs, out_ref = rest[:6], rest[-1]
+
+        def store(place, value):
+            out_ref[0, place, :] = value.astype(dtype)
+
+        place_gathered(store, tp_ref[0], refs, size)
+
+    args = [tp_here] + list(pieces)
+    in_specs = [pl.BlockSpec(memory_space=pltpu.SMEM)] + [
+        pl.BlockSpec(piece.shape, lambda i, n=piece.ndim: (0,) * n) for piece in pieces
+    ]
+    aliases = {}
+    if earlier is not None:
+        aliases = {len(args): 0}
+        args.append(earlier)
+        in_specs.append(pl.BlockSpec(memory_space=pl.ANY))
+    return pl.pallas_call(
+        body,
+        grid=(1,),
+        out_shape=sds((count, rows, width), dtype),
+        in_specs=in_specs,
+        out_specs=pl.BlockSpec((1, rows, width), lambda i: (index, 0, 0)),
+        input_output_aliases=aliases,
+        compiler_params=pltpu.CompilerParams(vmem_limit_bytes=32 << 20),
+        cost_estimate=pl.CostEstimate(
+            flops=0, bytes_accessed=rows * width * 6, transcendentals=0
+        ),
+        name="assemble",
+    )(*args)
+
+
+def weight_grad(lefts, rights, step=512):
+    count = len(lefts)
+    rows, tall = lefts[0].shape
+    wide = rights[0].shape[1]
+    step = min(step, tall)
+
+    def body(*rest):
+        left_refs, right_refs, out_ref = rest[:count], rest[count : 2 * count], rest[-1]
+        value = dot_tn(left_refs[0][...], right_refs[0][...])
+        for place in range(1, count):
+            value += dot_tn(left_refs[place][...], right_refs[place][...])
+        out_ref[...] = value.astype(BF)
+
+    return pl.pallas_call(
+        body,
+        grid=(tall // step,),
+        out_shape=sds((tall, wide)),
+        in_specs=[pl.BlockSpec((rows, step), lambda i: (0, i))] * count
+        + [pl.BlockSpec((rows, wide), lambda i: (0, 0))] * count,
+        out_specs=pl.BlockSpec((step, wide), lambda i: (i, 0)),
+        compiler_params=pltpu.CompilerParams(vmem_limit_bytes=48 << 20),
+        cost_estimate=pl.CostEstimate(
+            flops=2 * count * rows * tall * wide,
+            bytes_accessed=2 * (count * rows * (tall + wide) + tall * wide),
+            transcendentals=0,
+        ),
+        name="weight_grad",
+    )(*lefts, *rights)
+
+
+def small_sums(values):
+    here = lax.axis_index("ctx")
+    step = values.shape[0] // 2
+    while step:
+        pair = values.reshape((2, step) + values.shape[1:])
+        bit = (here // step) % 2
+        keep = lax.dynamic_index_in_dim(pair, bit, 0, False)
+        send = lax.dynamic_index_in_dim(pair, 1 - bit, 0, False)
+        values = keep + xor_permute(send, "ctx", step)
+        step //= 2
+    return values[0]
+
+
+def per_device_exchanged(
+    inputs,
+    segments,
+    keep_mask,
+    first_gain,
+    first_shift,
+    proj_weight,
+    proj_bias,
+    mixer_weight,
+    mixer_bias,
+    second_gain,
+    second_shift,
+    up_weight,
+    up_bias,
+    down_weight,
+    down_bias,
+    out_cotangent,
+):
+    ctx_count = lax.axis_size("ctx")
+    micro_count, seq_count, tok_len, width = inputs.shape
+    inner = proj_bias.shape[1]
+    heads = inner // HD
+    rows = seq_count * tok_len
+    here = lax.axis_index("ctx").astype(jnp.int32).reshape(1)
+    tp_here = lax.axis_index("tp").astype(jnp.int32).reshape(1)
+    weight_three = jnp.transpose(proj_weight, (1, 0, 2))
+    bias_three = jnp.stack([proj_bias[0], jnp.zeros_like(proj_bias[0]), proj_bias[1]])
+    x_all = inputs.reshape(micro_count, rows, width)
+    cot_all = out_cotangent.reshape(micro_count, rows, width)
+    key_rows = jnp.where(keep_mask > 0, segments, -1)[:, :, None, :]
+    seg_columns = segments[:, :, :, None]
+    gain_one, shift_one = first_gain[None], first_shift[None]
+    gain_two, shift_two = second_gain[None], second_shift[None]
+    mix_bias, low_bias, high_bias = mixer_bias[None], down_bias[None], up_bias[None]
+    micro = range(micro_count)
+
+    norm_one, received, lses, heads_low, resids = [], [], [], [], []
+    for index in micro:
+        normed, *sent = project(
+            here, x_all[index], gain_one, shift_one, weight_three, bias_three, tok_len
+        )
+        norm_one.append(normed)
+        received.append(exchange(*sent))
+    gathered_two = []
+    for index in micro:
+        *sent, lse = attention(here, received[index], seg_columns[index], key_rows[index], heads)
+        lses.append(lse)
+        mixed, *messages = mix_heads(here, tp_here, exchange(*sent), mixer_weight, heads)
+        heads_low.append(mixed)
+        resid, low, high = second_norm(
+            tp_here, shard_reduce(messages), x_all[index], mix_bias, gain_two, shift_two
+        )
+        resids.append(resid)
+        gathered_two.append(shard_gather((low, high)))
+    norm_two, acts, grad_pres, up_sums, feeds, grad_twos = [], [], [], [], [], []
+    for index in micro:
+        normed, act, grad_pre, up_sum, *messages = feed_forward(
+            tp_here, gathered_two[index], cot_all[index], up_weight, high_bias, down_weight
+        )
+        norm_two.append(normed)
+        acts.append(act)
+        grad_pres.append(grad_pre)
+        up_sums.append(up_sum)
+        feeds.append(messages[:4])
+        grad_twos.append(messages[4:])
+    grad_resids, gain_twos, shift_twos, gathered_mix = [], [], [], []
+    for index in micro:
+        grad_resid, low, high, gain_sum, shift_sum = second_norm_back(
+            tp_here, shard_reduce(grad_twos[index]), resids[index], cot_all[index], gain_two
+        )
+        grad_resids.append(grad_resid)
+        gain_twos.append(gain_sum)
+        shift_twos.append(shift_sum)
+        gathered_mix.append(shard_gather((low, high)))
+
+    def scattered(part, dim):
+        return lax.psum_scatter(part, "ctx", scatter_dimension=dim, tiled=True).astype(F32)
+
+    cots = [cot_all[index] for index in micro]
+    down_grad = scattered(weight_grad(acts, cots), 1)
+    up_grad = scattered(weight_grad(norm_two, grad_pres), 0)
+
+    grad_mixes, mix_sums, grad_projs, proj_sums, gain_ones, shift_ones = [], [], [], [], [], []
+    input_grad = None
+    outputs = None
+    for index in micro:
+        grad_mix, mix_sum, *sent = heads_back(
+            here, tp_here, gathered_mix[index], mixer_weight, tok_len
+        )
+        grad_mixes.append(grad_mix)
+        mix_sums.append(mix_sum)
+        sent = attention_back(
+            here,
+            received[index],
+            exchange(*sent),
+            seg_columns[index],
+            key_rows[index],
+            lses[index],
+            heads,
+        )
+        grad_proj, proj_sum, *messages = project_back(
+            here, tp_here, exchange(*sent), weight_three
+        )
+        grad_projs.append(grad_proj)
+        proj_sums.append(proj_sum)
+        low, high, gain_sum, shift_sum = first_norm_back(
+            tp_here, shard_reduce(messages), x_all[index], grad_resids[index], gain_one
+        )
+        gain_ones.append(gain_sum)
+        shift_ones.append(shift_sum)
+        input_grad = assemble(
+            tp_here, shard_gather((low, high)), input_grad, index, micro_count, F32
+        )
+    for index in micro:
+        halves = finish_output(shard_reduce(feeds[index]), resids[index], low_bias)
+        outputs = assemble(tp_here, shard_gather(halves), outputs, index, micro_count, BF)
+    mixer_grad = scattered(weight_grad(heads_low, grad_mixes), 1)
+    proj_grad = scattered(weight_grad(norm_one, grad_projs), 0)
+
+    def over_micro(items):
+        return sum(items[1:], items[0]).reshape(ctx_count, -1)
+
+    cot_sum = jnp.sum(out_cotangent.astype(F32), axis=(0, 1, 2)).reshape(ctx_count, -1)
+    proj_sum = sum(proj_sums[1:], proj_sums[0]).reshape(3, ctx_count, -1)
+    pair_sum = jnp.concatenate([proj_sum[0], proj_sum[2]], axis=1)
+    share = cot_sum.shape[1]
+    pair_sum = jnp.pad(pair_sum, ((0, 0), (0, share - pair_sum.shape[1])))
+    kinds = [
+        over_micro(gain_ones),
+        over_micro(shift_ones),
+        over_micro(gain_twos),
+        over_micro(shift_twos),
+        over_micro(mix_sums),
+        cot_sum,
+        over_micro(up_sums),
+        pair_sum,
+    ]
+    small = small_sums(jnp.stack(kinds, axis=1))
+    norms = small[:4]
+    for step in (1, 2):
+        norms = norms + xor_permute(norms, "tp", step)
+    proj_bias_grad = small[7, : 2 * inner // ctx_count].reshape(2, -1)
+    return (
+        outputs.reshape(inputs.shape),
+        input_grad.reshape(inputs.shape),
+        norms[0],
+        norms[1],
+        proj_grad.reshape(width // ctx_count, 3, inner),
+        proj_bias_grad,
+        mixer_grad,
+        small[4],
+        norms[2],
+        norms[3],
+        up_grad,
+        small[6],
+        down_grad,
+        small[5],
+    )
+
+
+def plan_for(mesh):
+    sizes = dict(mesh.shape)
+
+    def chosen(*args):
+        seq_count, width = args[0].shape[1], args[0].shape[3]
+        units = seq_count * args[6].shape[1] // HD
+        fits = sizes["ctx"] == 8 and sizes["tp"] == 4 and units == sizes["ctx"]
+        fits = fits and args[12].shape[0] == width
+        return (per_device_exchanged if fits else per_device)(*args)
+
+    return chosen
+
+
 def solution(mesh):
     in_specs = (
         P(None, None, "ctx", None),
@@ -355,5 +1240,5 @@
         P("ctx"),
     )
     return jax.shard_map(
-        per_device, mesh=mesh, in_specs=in_specs, out_specs=out_specs, check_vma=False
-    )
+        plan_for(mesh), mesh=mesh, in_specs=in_specs, out_specs=out_specs, check_vma=False
+    )

time: 1390 us -> 775 us (0.56)
  waiting for transfers between devices: 798 us -> 309 us
  matrix products: 302 us -> 0 us
  Pallas kernels: 0 us -> 213 us
  starting transfers between devices: 2.71 us -> 138 us
  other arithmetic: 149 us -> 30.5 us
  blocking collectives: 30.8 us -> 0 us
  local copies, waits for them, and re-layouts: 82 us -> 58.6 us
    psum x4 -> x0, waiting for transfers between devices: 414 us -> none  [the longest x1 174 us: per_device(): lax.psum(feed_part.astype(jnp.bfloat16), 'tp').astype(jnp.float32)]
    dot_general x36 -> x0, matrix products: 302 us -> none  [the longest x2 29 us: per_device(): jnp.einsum('std,stf->df', normed_two, grad_pre, preferred_element_type=jn...]
    ppermute x0 -> x101, waiting for transfers between devices: none -> 253 us  [xor_permute(): return lax.ppermute(values, axis, [(i, i ^ step) for i in range(count)])]
    pallas_call x0 -> x30, Pallas kernels: none -> 213 us  [the longest x20 95 us: run_kernel(): pl.pallas_call(body, out_shape=tuple(outs), in_specs=specs, out_specs=tup...]
    reduce_scatter x8 -> x4, waiting for transfers between devices: 246 us -> 55.9 us  [scattered(): lax.psum_scatter(part, 'ctx', scatter_dimension=dim, tiled=True).astype(F32)]
    ppermute x0 -> x101, starting transfers between devices: none -> 138 us  [xor_permute(): return lax.ppermute(values, axis, [(i, i ^ step) for i in range(count)])]
    all_gather x4 -> x0, waiting for transfers between devices: 137 us -> none  [the longest x2 90.7 us: per_device(): lax.all_gather(key_here, 'ctx', axis=1, tiled=True)]
    reduce_sum x15 -> x1, other arithmetic: 63.5 us -> 0.65 us  [per_device_exchanged(): jnp.sum(out_cotangent.astype(F32), axis=(0, 1, 2)).reshape(ctx_count, -1)]
  transfers between devices with their start and end apart: 17 -> 105, of which waited for: 13 -> 49; matrix products, arithmetic and copies ran while one was open for 21% -> 6% of each run, Pallas kernels for 0% -> 26%
where the time goes in v1:
time: 775 us; the launch traced here: 765 us
  waiting for transfers between devices  309 us (40%)
  Pallas kernels  213 us (27%)
  starting transfers between devices  138 us (18%)
  local copies, waits for them, and re-layouts  58.6 us (8%)
  other arithmetic  30.5 us (4%)
  between operations  15.8 us (2%)
    ppermute x101, waiting for transfers between devices, xor_permute(): return lax.ppermute(values, axis, [(i, i ^ step) for i in range(count)])  253 us
    ppermute x101, starting transfers between devices, xor_permute(): return lax.ppermute(values, axis, [(i, i ^ step) for i in range(count)])  138 us
    pallas_call x20, Pallas kernels, run_kernel(): pl.pallas_call(body, out_shape=tuple(outs), in_specs=specs, out_specs=tup...  95 us
    pallas_call x2, Pallas kernels, feed_forward(): pl.pallas_call(body, grid=(count,), out_shape=tuple(outs), in_specs=in_sp...  66.1 us
    reduce_scatter x4, waiting for transfers between devices, scattered(): lax.psum_scatter(part, 'ctx', scatter_dimension=dim, tiled=True).astype(F32)  55.9 us
    unnamed x283, local copies, waits for them, and re-layouts  41.4 us
    pallas_call x4, Pallas kernels, weight_grad(): pl.pallas_call(body, grid=(tall // step,), out_shape=sds((tall, wide)), i...  40.3 us
  transfers between devices with their start and end apart: 105, of which 49 were waited for; matrix products, arithmetic and copies ran while one was open for 6% of the time, Pallas kernels for 26%

profile of v1, /device:TPU:0, one launch (start us, length us, event | category | flops | bytes accessed | tf_op | source)
XLA Modules:
  0.0 765.0 jit_solution(6766963956535428828)
XLA Ops:
  11.0 8.7 %project.2 = (bf16[512,2048]{1,0:T(8,128)(2,1)S(1)}, bf16[256,384]{1,0:T(8,128)(2,1)S(1)}, bf16[256,384]{1,0:T(8,128)(2,1)S(1)}, bf16[2,256,384]{2,1,0:T(8,128)(...) custom-call(s32[1]{0:T(128)} %bitcast.1.here_ref, bf16[512,2048]{1,0:T(8,128)(2,1)S(1)} %bitcast.129, ...), custom_call_target="tpu_custom_call" | custom-call | flops 3221225472 | bytes 12081152 | tf_op jit(solution)/shard_map/project/pallas_call | solution.py:350
  26.7 8.3 %project.3 = (bf16[512,2048]{1,0:T(8,128)(2,1)S(1)}, bf16[256,384]{1,0:T(8,128)(2,1)S(1)}, bf16[256,384]{1,0:T(8,128)(2,1)S(1)}, bf16[2,256,384]{2,1,0:T(8,128)(...) custom-call(s32[1]{0:T(128)} %bitcast.1.here_ref, bf16[512,2048]{1,0:T(8,128)(2,1)S(1)} %bitcast.126, ...), custom_call_target="tpu_custom_call" | custom-call | flops 3221225472 | bytes 12081152 | tf_op jit(solution)/shard_map/project/pallas_call | solution.py:350
  46.3 7.6 collective-permute-done.1.rest_2_
  59.1 28.5 %collective-permute-done.25.rest_2_ = bf16[2,256,384]{2,1,0:T(8,128)(2,1)S(1)} collective-permute-done((bf16[2,256,384]{2,1,0:T(8,128)(2,1)}, bf16[2,256,384]{2,1,0:T(8,128)(2,1)S(1)}, u32[]{:S(2)}, u32[]{:S(2)}) %collective-permute-start.25) | collective-permute-done | bytes 393248 | tf_op jit(solution)/shard_map/ppermute | solution.py:333
  199.6 9.5 %collective-permute-done.13.rest_2_ = bf16[2,64,2048]{2,1,0:T(8,128)(2,1)S(1)} collective-permute-done((bf16[2,64,2048]{2,1,0:T(8,128)(2,1)S(1)}, bf16[2,64,2048]{2,1,0:T(8,128)(2,1)S(1)}, u32[]{:S(2)}, u32[]{:S(2)}) %collective-permute-start.13) | collective-permute-done | bytes 524320 | tf_op jit(solution)/shard_map/ppermute | solution.py:333
  210.1 32.9 %feed_forward.2 = (bf16[512,2048]{1,0:T(8,128)(2,1)}, bf16[512,2048]{1,0:T(8,128)(2,1)}, bf16[512,2048]{1,0:T(8,128)(2,1)}, f32[1,2048]{1,0:T(1,128)}, bf16[2,64...) custom-call(s32[1]{0:T(128)} %bitcast.tp_ref, ...), custom_call_target="tpu_custom_call" | custom-call | flops 17179869184 | bytes 37748736 | tf_op jit(solution)/shard_map/feed_forward/pallas_call | solution.py:803
  245.7 33.2 %feed_forward.3 = (bf16[512,2048]{1,0:T(8,128)(2,1)}, bf16[512,2048]{1,0:T(8,128)(2,1)}, bf16[512,2048]{1,0:T(8,128)(2,1)}, f32[1,2048]{1,0:T(1,128)}, bf16[2,64...) custom-call(s32[1]{0:T(128)} %bitcast.tp_ref, ...), custom_call_target="tpu_custom_call" | custom-call | flops 17179869184 | bytes 37748736 | tf_op jit(solution)/shard_map/feed_forward/pallas_call | solution.py:803
  283.3 10.7 %collective-permute-done.72.rest_1_ = bf16[2,64,2048]{2,1,0:T(8,128)(2,1)S(1)} collective-permute-done((bf16[2,64,2048]{2,1,0:T(8,128)(2,1)}, bf16[2,64,2048]{2,1,0:T(8,128)(2,1)S(1)}, u32[]{:S(2)}, u32[]{:S(2)}) %collective-permute-start.72) | collective-permute-done | bytes 524320 | tf_op jit(solution)/shard_map/ppermute | solution.py:333
  320.0 10.6 %collective-permute-done.53.rest_2_ = bf16[2,64,2048]{2,1,0:T(8,128)(2,1)S(1)} collective-permute-done((bf16[2,64,2048]{2,1,0:T(8,128)(2,1)S(1)}, bf16[2,64,2048]{2,1,0:T(8,128)(2,1)S(1)}, u32[]{:S(2)}, u32[]{:S(2)}) %collective-permute-start.53) | collective-permute-done | bytes 524320 | tf_op jit(solution)/shard_map/ppermute | solution.py:333
  368.8 7.9 %collective-permute-done.80.rest_6_ = bf16[2,256,128]{2,1,0:T(8,128)(2,1)S(1)} collective-permute-done((bf16[2,256,128]{2,1,0:T(8,128)(2,1)S(1)}, bf16[2,256,128]{2,1,0:T(8,128)(2,1)S(1)}, u32[]{:S(2)}, u32[]{:S(2)}) %collective-permute-start.80) | collective-permute-done | bytes 131104 | tf_op jit(solution)/shard_map/ppermute | solution.py:333
  378.0 7.8 %collective-permute-done.82.rest_8_ = bf16[2,256,128]{2,1,0:T(8,128)(2,1)S(1)} collective-permute-done((bf16[2,256,128]{2,1,0:T(8,128)(2,1)S(1)}, bf16[2,256,128]{2,1,0:T(8,128)(2,1)S(1)}, u32[]{:S(2)}, u32[]{:S(2)}) %collective-permute-start.82) | collective-permute-done | bytes 131104 | tf_op jit(solution)/shard_map/ppermute | solution.py:333
  391.6 9.6 %attention_back.2 = (bf16[256,384]{1,0:T(8,128)(2,1)S(1)}, bf16[256,384]{1,0:T(8,128)(2,1)S(1)}, bf16[2,256,384]{2,1,0:T(8,128)(2,1)S(1)}, bf16[2,256,384]{2,1,0:T(8,128)(2,1)S(1)}, bf16[2,256,384]{2,1,0:T(8,128)(2,1)S(1)}) custom-call(s32[1]{0:T(128)} %bitcast.1.here_ref, bf16[256,384]{1,0:T(8,128)(2,1)S(1)} %copy-done.122, ...), custom_call_target="tpu_custom_call" | custom-call | flops 2684354560 | bytes 4497408 | tf_op jit(solution)/shard_map/attention_back/pallas_call | solution.py:350
  407.5 9.9 %attention_back.3 = (bf16[256,384]{1,0:T(8,128)(2,1)S(1)}, bf16[256,384]{1,0:T(8,128)(2,1)S(1)}, bf16[2,256,384]{2,1,0:T(8,128)(2,1)S(1)}, bf16[2,256,384]{2,1,0:T(8,128)(2,1)S(1)}, bf16[2,256,384]{2,1,0:T(8,128)(2,1)S(1)}) custom-call(s32[1]{0:T(128)} %bitcast.1.here_ref, bf16[256,384]{1,0:T(8,128)(2,1)S(1)} %copy-done.120, ...), custom_call_target="tpu_custom_call" | custom-call | flops 2684354560 | bytes 4497408 | tf_op jit(solution)/shard_map/attention_back/pallas_call | solution.py:350
  424.3 10.1 %collective-permute-done.61.rest_2_ = bf16[2,256,384]{2,1,0:T(8,128)(2,1)S(1)} collective-permute-done((bf16[2,256,384]{2,1,0:T(8,128)(2,1)S(1)}, bf16[2,256,384]{2,1,0:T(8,128)(2,1)S(1)}, u32[]{:S(2)}, u32[]{:S(2)}) %collective-permute-start.61) | collective-permute-done | bytes 393248 | tf_op jit(solution)/shard_map/ppermute | solution.py:333
  439.7 28.4 %collective-permute-done.85.rest_2_ = bf16[2,256,384]{2,1,0:T(8,128)(2,1)S(1)} collective-permute-done((bf16[2,256,384]{2,1,0:T(8,128)(2,1)S(1)}, bf16[2,256,384]{2,1,0:T(8,128)(2,1)S(1)}, u32[]{:S(2)}, u32[]{:S(2)}) %collective-permute-start.85) | collective-permute-done | bytes 393248 | tf_op jit(solution)/shard_map/ppermute | solution.py:333
  468.4 7.5 project_back.2
  488.3 9.7 %weight_grad.4 = bf16[2048,1536]{1,0:T(8,128)(2,1)} custom-call(bf16[512,2048]{1,0:T(8,128)(2,1)S(1)} %copy-done.111, bf16[512,2048]{1,0:T(8,128)(2,1)} %copy-done.109, bf16[512,1536]{1,0:T(8,128)(2,1)S(1)} %get-tuple-element.246.rest_2_, bf16[512,1536]{1,0:T(8,128)(2,1)S(1)} %get-tuple-element.247.rest_3_), custom_call_target="tpu_custom_call" | custom-call | flops 6442450944 | bytes 13631488 | tf_op jit(solution)/shard_map/weight_grad/pallas_call | solution.py:1004
  501.5 13.3 %weight_grad.7 = bf16[2048,2048]{1,0:T(8,128)(2,1)} custom-call(bf16[512,2048]{1,0:T(8,128)(2,1)S(1)} %copy-done.126, bf16[512,2048]{1,0:T(8,128)(2,1)S(1)} %copy-done.124, bf16[512,2048]{1,0:T(8,128)(2,1)} %bitcast.183, bf16[512,2048]{1,0:T(8,128)(2,1)} %bitcast.186), custom_call_target="tpu_custom_call" | custom-call | flops 8589934592 | bytes 16777216 | tf_op jit(solution)/shard_map/weight_grad/pallas_call | solution.py:1004
  518.1 13.4 %weight_grad.6 = bf16[2048,2048]{1,0:T(8,128)(2,1)} custom-call(bf16[512,2048]{1,0:T(8,128)(2,1)S(1)} %copy-done.125, bf16[512,2048]{1,0:T(8,128)(2,1)S(1)} %copy-done.123, bf16[512,2048]{1,0:T(8,128)(2,1)} %get-tuple-element.254.rest_2_, bf16[512,2048]{1,0:T(8,128)(2,1)} %get-tuple-element.255.rest_3_), custom_call_target="tpu_custom_call" | custom-call | flops 8589934592 | bytes 16777216 | tf_op jit(solution)/shard_map/weight_grad/pallas_call | solution.py:1004
  535.6 10.9 %collective-permute-done.16.rest_1_ = bf16[2,64,2048]{2,1,0:T(8,128)(2,1)S(1)} collective-permute-done((bf16[2,64,2048]{2,1,0:T(8,128)(2,1)}, bf16[2,64,2048]{2,1,0:T(8,128)(2,1)S(1)}, u32[]{:S(2)}, u32[]{:S(2)}) %collective-permute-start.16) | collective-permute-done | bytes 524320 | tf_op jit(solution)/shard_map/ppermute | solution.py:333
  549.9 7.8 %collective-permute-done.40.rest_1_ = bf16[2,64,2048]{2,1,0:T(8,128)(2,1)S(1)} collective-permute-done((bf16[2,64,2048]{2,1,0:T(8,128)(2,1)}, bf16[2,64,2048]{2,1,0:T(8,128)(2,1)S(1)}, u32[]{:S(2)}, u32[]{:S(2)}) %collective-permute-start.40) | collective-permute-done | bytes 524320 | tf_op jit(solution)/shard_map/ppermute | solution.py:333
  624.4 10.0 %collective-permute-start.96 = (f32[4,8,256]{2,1,0:T(8,128)S(1)}, f32[4,8,256]{2,1,0:T(8,128)S(1)}, u32[]{:S(2)}, u32[]{:S(2)}) collective-permute-start(f32[4,8,256]{2,1,0:T(8,128)S(1)} %dynamic-slice_bitcast_fusion), channel_id=1, source_target_pairs={{0,16},{4,20},{8,24},{12,28},{16,0},{20,4},{24,8},{28,12},{1,17},{... | collective-permute-start | bytes 98312 | tf_op jit(solution)/shard_map/ppermute | solution.py:333
  670.6 14.9 %collective-permute-done.100 = f32[4,256]{1,0:T(4,128)S(1)} collective-permute-done((f32[4,256]{1,0:T(4,128)S(1)}, f32[4,256]{1,0:T(4,128)S(1)}, u32[]{:S(2)}, u32[]{:S(2)}) %collective-permute-start.100) | collective-permute-done | bytes 4128 | tf_op jit(solution)/shard_map/ppermute | solution.py:333
  699.4 55.9 %reduce-scatter.9.cloned.1.call-done = bf16[256,2048]{1,0:T(8,128)(2,1)} async-done(((bf16[2048,2048]{1,0:T(8,128)(2,1)}), bf16[256,2048]{1,0:T(8,128)(2,1)}) %reduce-scatter.9.cloned.1.call-update) | async-done | bytes 1048592 | tf_op jit(solution)/shard_map/reduce_scatter | solution.py:1110
  (608 shorter events, 382.2 us)
Async XLA Ops:
  7.2 684.7 %reduce-scatter.7.cloned.1.call-start = ((), (), s32[]{:S(2)}) async-start(), calls=%async_computation.5 | async-start | bytes 2359296 | tf_op jit(solution)/shard_map/reduce_scatter | solution.py:1110
  24.1 29.8 %collective-permute-start.1 = (bf16[2,256,384]{2,1,0:T(8,128)(2,1)S(1)}, bf16[2,256,384]{2,1,0:T(8,128)(2,1)S(1)}, u32[]{:S(2)}, u32[]{:S(2)}) collective-permute-start(bf16[2,256,384]{2,1,0:T(8,128)(2,1)S(1)} %get-tuple-element.138), channel_id=1, source_target_pairs={{0,16},{4,20},{8,24},{12,28},{16,0},{20,4},{24,8},{28,12},{1,17},{... | collective-permute-start | bytes 1179656 | tf_op jit(solution)/shard_map/ppermute | solution.py:333
  26.7 27.3 %collective-permute-start.2 = (bf16[2,256,384]{2,1,0:T(8,128)(2,1)S(1)}, bf16[2,256,384]{2,1,0:T(8,128)(2,1)S(1)}, u32[]{:S(2)}, u32[]{:S(2)}) collective-permute-start(bf16[2,256,384]{2,1,0:T(8,128)(2,1)S(1)} %get-tuple-element.139), channel_id=1, source_target_pairs={{0,24},{4,28},{8,16},{12,20},{16,8},{20,12},{24,0},{28,4},{1,25},{... | collective-permute-start | bytes 1179656 | tf_op jit(solution)/shard_map/ppermute | solution.py:333
  37.2 50.4 %collective-permute-start.25 = (bf16[2,256,384]{2,1,0:T(8,128)(2,1)}, bf16[2,256,384]{2,1,0:T(8,128)(2,1)S(1)}, u32[]{:S(2)}, u32[]{:S(2)}) collective-permute-start(bf16[2,256,384]{2,1,0:T(8,128)(2,1)} %get-tuple-element.161), channel_id=1, source_target_pairs={{0,16},{4,20},{8,24},{12,28},{16,0},{20,4},{24,8},{28,12},{1,17},{... | collective-permute-start | bytes 1179656 | tf_op jit(solution)/shard_map/ppermute | solution.py:333
  41.7 46.7 %collective-permute-start.26 = (bf16[2,256,384]{2,1,0:T(8,128)(2,1)}, bf16[2,256,384]{2,1,0:T(8,128)(2,1)}, u32[]{:S(2)}, u32[]{:S(2)}) collective-permute-start(bf16[2,256,384]{2,1,0:T(8,128)(2,1)} %get-tuple-element.162), channel_id=1, source_target_pairs={{0,24},{4,28},{8,16},{12,20},{16,8},{20,12},{24,0},{28,4},{1,25},{... | collective-permute-start | bytes 1179656 | tf_op jit(solution)/shard_map/ppermute | solution.py:333
  55.1 36.0 %collective-permute-start.3 = (bf16[4,256,384]{2,1,0:T(8,128)(2,1)}, bf16[4,256,384]{2,1,0:T(8,128)(2,1)}, u32[]{:S(2)}, u32[]{:S(2)}) collective-permute-start(bf16[4,256,384]{2,1,0:T(8,128)(2,1)} %pad_maximum_fusion), channel_id=1, source_target_pairs={{0,4},{4,0},{8,12},{12,8},{16,20},{20,16},{24,28},{28,24},{1,5},{5... | collective-permute-start | bytes 2359304 | tf_op jit(solution)/shard_map/ppermute | solution.py:333
  90.4 31.0 %collective-permute-start.27 = (bf16[4,256,384]{2,1,0:T(8,128)(2,1)}, bf16[4,256,384]{2,1,0:T(8,128)(2,1)}, u32[]{:S(2)}, u32[]{:S(2)}) collective-permute-start(bf16[4,256,384]{2,1,0:T(8,128)(2,1)} %pad_maximum_fusion.1), channel_id=1, source_target_pairs={{0,4},{4,0},{8,12},{12,8},{16,20},{20,16},{24,28},{28,24},{1,5},{5... | collective-permute-start | bytes 2359304 | tf_op jit(solution)/shard_map/ppermute | solution.py:333
  197.2 47.5 %collective-permute-start.37 = (bf16[2,64,2048]{2,1,0:T(8,128)(2,1)S(1)}, bf16[2,64,2048]{2,1,0:T(8,128)(2,1)S(1)}, u32[]{:S(2)}, u32[]{:S(2)}) collective-permute-start(bf16[2,64,2048]{2,1,0:T(8,128)(2,1)S(1)} %pad_maximum_fusion.8), channel_id=1, source_target_pairs={{0,2},{1,3},{2,0},{3,1},{4,6},{5,7},{6,4},{7,5},{8,10},{9,11},{10,... | collective-permute-start | bytes 1572872 | tf_op jit(solution)/shard_map/ppermute | solution.py:333
  198.8 45.9 %collective-permute-start.39 = (bf16[2,64,2048]{2,1,0:T(8,128)(2,1)S(1)}, bf16[2,64,2048]{2,1,0:T(8,128)(2,1)S(1)}, u32[]{:S(2)}, u32[]{:S(2)}) collective-permute-start(bf16[2,64,2048]{2,1,0:T(8,128)(2,1)S(1)} %pad_maximum_fusion.9), channel_id=1, source_target_pairs={{0,1},{1,0},{2,3},{3,2},{4,5},{5,4},{6,7},{7,6},{8,9},{9,8},{10,11... | collective-permute-start | bytes 1572872 | tf_op jit(solution)/shard_map/ppermute | solution.py:333
  243.0 38.4 %collective-permute-start.48 = (bf16[2,64,2048]{2,1,0:T(8,128)(2,1)}, bf16[2,64,2048]{2,1,0:T(8,128)(2,1)S(1)}, u32[]{:S(2)}, u32[]{:S(2)}) collective-permute-start(bf16[2,64,2048]{2,1,0:T(8,128)(2,1)} %get-tuple-element.183), channel_id=1, source_target_pairs={{0,1},{1,0},{2,3},{3,2},{4,5},{5,4},{6,7},{7,6},{8,9},{9,8},{10,11... | collective-permute-start | bytes 1572872 | tf_op jit(solution)/shard_map/ppermute | solution.py:333
  243.4 39.6 %collective-permute-start.50 = (bf16[2,64,2048]{2,1,0:T(8,128)(2,1)}, bf16[2,64,2048]{2,1,0:T(8,128)(2,1)S(1)}, u32[]{:S(2)}, u32[]{:S(2)}) collective-permute-start(bf16[2,64,2048]{2,1,0:T(8,128)(2,1)} %get-tuple-element.185), channel_id=1, source_target_pairs={{0,2},{1,3},{2,0},{3,1},{4,6},{5,7},{6,4},{7,5},{8,10},{9,11},{10,... | collective-permute-start | bytes 1572872 | tf_op jit(solution)/shard_map/ppermute | solution.py:333
  346.4 347.3 %reduce-scatter.5.cloned.1.call-start = ((), (), s32[]{:S(2)}) async-start(), calls=%async_computation.4 | async-start | bytes 7077888 | tf_op jit(solution)/shard_map/reduce_scatter | solution.py:1110
  404.6 29.8 %collective-permute-start.61 = (bf16[2,256,384]{2,1,0:T(8,128)(2,1)S(1)}, bf16[2,256,384]{2,1,0:T(8,128)(2,1)S(1)}, u32[]{:S(2)}, u32[]{:S(2)}) collective-permute-start(bf16[2,256,384]{2,1,0:T(8,128)(2,1)S(1)} %get-tuple-element.196), channel_id=1, source_target_pairs={{0,16},{4,20},{8,24},{12,28},{16,0},{20,4},{24,8},{28,12},{1,17},{... | collective-permute-start | bytes 1179656 | tf_op jit(solution)/shard_map/ppermute | solution.py:333
  406.0 28.4 %collective-permute-start.62 = (bf16[2,256,384]{2,1,0:T(8,128)(2,1)S(1)}, bf16[2,256,384]{2,1,0:T(8,128)(2,1)S(1)}, u32[]{:S(2)}, u32[]{:S(2)}) collective-permute-start(bf16[2,256,384]{2,1,0:T(8,128)(2,1)S(1)} %get-tuple-element.197), channel_id=1, source_target_pairs={{0,24},{4,28},{8,16},{12,20},{16,8},{20,12},{24,0},{28,4},{1,25},{... | collective-permute-start | bytes 1179656 | tf_op jit(solution)/shard_map/ppermute | solution.py:333
  418.0 50.0 %collective-permute-start.85 = (bf16[2,256,384]{2,1,0:T(8,128)(2,1)S(1)}, bf16[2,256,384]{2,1,0:T(8,128)(2,1)S(1)}, u32[]{:S(2)}, u32[]{:S(2)}) collective-permute-start(bf16[2,256,384]{2,1,0:T(8,128)(2,1)S(1)} %get-tuple-element.220), channel_id=1, source_target_pairs={{0,16},{4,20},{8,24},{12,28},{16,0},{20,4},{24,8},{28,12},{1,17},{... | collective-permute-start | bytes 1179656 | tf_op jit(solution)/shard_map/ppermute | solution.py:333
  422.7 45.4 %collective-permute-start.86 = (bf16[2,256,384]{2,1,0:T(8,128)(2,1)S(1)}, bf16[2,256,384]{2,1,0:T(8,128)(2,1)S(1)}, u32[]{:S(2)}, u32[]{:S(2)}) collective-permute-start(bf16[2,256,384]{2,1,0:T(8,128)(2,1)S(1)} %get-tuple-element.221), channel_id=1, source_target_pairs={{0,24},{4,28},{8,16},{12,20},{16,8},{20,12},{24,0},{28,4},{1,25},{... | collective-permute-start | bytes 1179656 | tf_op jit(solution)/shard_map/ppermute | solution.py:333
  434.6 33.8 %collective-permute-start.63 = (bf16[4,256,384]{2,1,0:T(8,128)(2,1)S(1)}, bf16[4,256,384]{2,1,0:T(8,128)(2,1)S(1)}, u32[]{:S(2)}, u32[]{:S(2)}) collective-permute-start(bf16[4,256,384]{2,1,0:T(8,128)(2,1)S(1)} %pad_maximum_fusion.2), channel_id=1, source_target_pairs={{0,4},{4,0},{8,12},{12,8},{16,20},{20,16},{24,28},{28,24},{1,5},{5... | collective-permute-start | bytes 2359304 | tf_op jit(solution)/shard_map/ppermute | solution.py:333
  498.0 198.7 %reduce-scatter.11.cloned.1.call-start = ((), (), s32[]{:S(2)}) async-start(), calls=%async_computation.7 | async-start | bytes 9437184 | tf_op jit(solution)/shard_map/reduce_scatter | solution.py:1110
  514.8 240.5 %reduce-scatter.9.cloned.1.call-start = ((), (), s32[]{:S(2)}) async-start(), calls=%async_computation.6 | async-start | bytes 9437184 | tf_op jit(solution)/shard_map/reduce_scatter | solution.py:1110
  572.6 35.4 %collective-permute-start.44 = (bf16[64,2048]{1,0:T(8,128)(2,1)S(1)}, bf16[64,2048]{1,0:T(8,128)(2,1)S(1)}, u32[]{:S(2)}, u32[]{:S(2)}) collective-permute-start(bf16[64,2048]{1,0:T(8,128)(2,1)S(1)} %get-tuple-element.180.rest_0_), channel_id=1, source_target_pairs={{0,1},{1,0},{2,3},{3,2},{4,5},{5,4},{6,7},{7,6},{8,9},{9,8},{10,11... | collective-permute-start | bytes 786440 | tf_op jit(solution)/shard_map/ppermute | solution.py:333
  573.6 60.8 %collective-permute-start.46 = (bf16[64,2048]{1,0:T(8,128)(2,1)}, bf16[64,2048]{1,0:T(8,128)(2,1)}, u32[]{:S(2)}, u32[]{:S(2)}) collective-permute-start(bf16[64,2048]{1,0:T(8,128)(2,1)} %get-tuple-element.181.rest_3_), channel_id=1, source_target_pairs={{0,2},{1,3},{2,0},{3,1},{4,6},{5,7},{6,4},{7,5},{8,10},{9,11},{10,... | collective-permute-start | bytes 786440 | tf_op jit(solution)/shard_map/ppermute | solution.py:333
  611.0 36.8 %collective-permute-start.21 = (bf16[2,64,2048]{2,1,0:T(8,128)(2,1)}, bf16[2,64,2048]{2,1,0:T(8,128)(2,1)}, u32[]{:S(2)}, u32[]{:S(2)}) collective-permute-start(bf16[2,64,2048]{2,1,0:T(8,128)(2,1)} %pad_maximum_fusion.6), channel_id=1, source_target_pairs={{0,2},{1,3},{2,0},{3,1},{4,6},{5,7},{6,4},{7,5},{8,10},{9,11},{10,... | collective-permute-start | bytes 1572872 | tf_op jit(solution)/shard_map/ppermute | solution.py:333
  613.3 34.5 %collective-permute-start.23 = (bf16[2,64,2048]{2,1,0:T(8,128)(2,1)}, bf16[2,64,2048]{2,1,0:T(8,128)(2,1)}, u32[]{:S(2)}, u32[]{:S(2)}) collective-permute-start(bf16[2,64,2048]{2,1,0:T(8,128)(2,1)} %pad_maximum_fusion.7), channel_id=1, source_target_pairs={{0,1},{1,0},{2,3},{3,2},{4,5},{5,4},{6,7},{7,6},{8,9},{9,8},{10,11... | collective-permute-start | bytes 1572872 | tf_op jit(solution)/shard_map/ppermute | solution.py:333
  659.9 28.5 %collective-permute-start.69 = (bf16[2,64,2048]{2,1,0:T(8,128)(2,1)}, bf16[2,64,2048]{2,1,0:T(8,128)(2,1)}, u32[]{:S(2)}, u32[]{:S(2)}) collective-permute-start(bf16[2,64,2048]{2,1,0:T(8,128)(2,1)} %pad_maximum_fusion.14), channel_id=1, source_target_pairs={{0,2},{1,3},{2,0},{3,1},{4,6},{5,7},{6,4},{7,5},{8,10},{9,11},{10,... | collective-permute-start | bytes 1572872 | tf_op jit(solution)/shard_map/ppermute | solution.py:333
  (222 other events, 2875.1 us)
Sparse Core Ops, SparseCore 0:
  346.5 41.9 reduce-scatter.6
  498.1 75.5 reduce-scatter.4
  576.0 89.0 reduce-scatter.10
  667.2 87.9 reduce-scatter.8

commit v2 on v1

--- a/solution.py
+++ b/solution.py
@@ -326,6 +326,7 @@
 LOG2E = 1.4426950408889634
 LOW = -1e30
 ORDERS = ((1, 2), (2, 1))
+COST_SHARE = 1.0
 
 
 def xor_permute(values, axis, step):
@@ -337,54 +338,190 @@
     return jax.ShapeDtypeStruct(tuple(shape), dtype)
 
 
-def run_kernel(body, outs, args, flops=0, exps=0, scratch=(), limit=48, name=None):
+def cost(flops, moved, exps=0):
+    return pl.CostEstimate(
+        flops=int(flops * COST_SHARE),
+        bytes_accessed=int(moved * COST_SHARE),
+        transcendentals=int(exps * COST_SHARE),
+    )
+
+
+HBM = pltpu.MemorySpace.HBM
+
+
+def launch(
+    body, args, in_specs, outs, out_specs, scratch, limit, cost, name, after, grid=(), aliases=None
+):
+    first, last = len(after), len(after) + len(args) + len(outs)
+
+    def inner(*refs):
+        body(*refs[first:last], *refs[last + 1 :])
+
+    token = pl.BlockSpec(memory_space=HBM)
+    *results, done = pl.pallas_call(
+        inner,
+        grid=grid,
+        out_shape=(*outs, sds((8, 128), F32)),
+        in_specs=[token] * first + list(in_specs),
+        out_specs=(*out_specs, token),
+        scratch_shapes=list(scratch),
+        input_output_aliases={first + key: value for key, value in (aliases or {}).items()},
+        compiler_params=pltpu.CompilerParams(vmem_limit_bytes=limit),
+        cost_estimate=cost,
+        name=name,
+    )(*after, *args)
+    return results, (done,)
+
+
+class Part:
+    def __init__(self, array, index):
+        self.array, self.index = array, index
+        self.shape, self.dtype = array.shape[1:], array.dtype
+
+    def spec(self):
+        index, rest = self.index, (0,) * len(self.shape)
+        return pl.BlockSpec((None,) + self.shape, lambda *_: (index,) + rest)
+
+
+def operands_of(args):
+    arrays = [arg.array if isinstance(arg, Part) else arg for arg in args]
+    return [
+        array if array.dtype == jnp.int32 else pltpu.with_memory_space_constraint(array, HBM)
+        for array in arrays
+    ]
+
+
+class Part:
+    def __init__(self, array, index):
+        self.array, self.index = array, index
+        self.shape, self.dtype = array.shape[1:], array.dtype
+
+    def spec(self):
+        index, rest = self.index, (0,) * len(self.shape)
+        return pl.BlockSpec((None,) + self.shape, lambda *_: (index,) + rest)
+
+
+def operands_of(args):
+    arrays = [arg.array if isinstance(arg, Part) else arg for arg in args]
+    return [
+        array if array.dtype == jnp.int32 else pltpu.with_memory_space_constraint(array, HBM)
+        for array in arrays
+    ]
+
+
+def run_kernel(body, outs, args, flops=0, exps=0, scratch=(), limit=8, name=None, after=(), in_hbm=()):
     specs = []
     moved = 0
-    for arg in args:
-        if arg.dtype == jnp.int32 and arg.size <= 8:
+    for place, arg in enumerate(args):
+        if arg.dtype == jnp.int32 and math.prod(arg.shape) <= 8:
             specs.append(pl.BlockSpec(memory_space=pltpu.SMEM))
+        elif place in in_hbm:
+            specs.append(pl.BlockSpec(memory_space=pl.ANY))
         else:
             specs.append(pl.BlockSpec(memory_space=pltpu.VMEM))
-            moved += arg.size * arg.dtype.itemsize
+            moved += math.prod(arg.shape) * arg.dtype.itemsize
     moved += sum(math.prod(o.shape) * o.dtype.itemsize for o in outs)
-    return pl.pallas_call(
+    kept = [item for item in scratch if item.dtype in (BF, F32)]
+    held = moved + sum(math.prod(item.shape) * item.dtype.itemsize for item in kept)
+    return launch(
         body,
-        out_shape=tuple(outs),
-        in_specs=specs,
-        out_specs=tuple(pl.BlockSpec(memory_space=pltpu.VMEM) for _ in outs),
-        scratch_shapes=list(scratch),
-        compiler_params=pltpu.CompilerParams(vmem_limit_bytes=limit << 20),
-        cost_estimate=pl.CostEstimate(
-            flops=flops, bytes_accessed=moved, transcendentals=exps
-        ),
-        name=name,
-    )(*args)
+        args,
+        specs,
+        outs,
+        [pl.BlockSpec(memory_space=pltpu.VMEM) for _ in outs],
+        scratch,
+        held + (limit << 20),
+        cost(flops, moved, exps),
+        name,
+        after,
+    )
+
+
+def whole_of(shape):
+    return pl.BlockSpec(shape, lambda *_, n=len(shape): (0,) * n)
 
 
 def rows_at(start, count):
     return pl.ds(pl.multiple_of(start, count), count)
 
 
-def shard_reduce(messages):
+def held_until(items, after):
+    held, _ = lax.optimization_barrier((items, after))
+    return held, after
+
+
+def reduce_first(messages):
+    return [
+        (messages[2 * part + 1], xor_permute(messages[2 * part], "tp", first))
+        for part, (first, _) in enumerate(ORDERS)
+    ]
+
+
+def reduce_second(state, after=()):
+    middle_shape = state[0][0].shape[:-3] + state[0][0].shape[-2:]
+
+    def body(*refs):
+        for part in range(2):
+            keep, got = refs[2 * part : 2 * part + 2]
+            value = keep[..., 1, :, :].astype(F32) + got[..., 1, :, :].astype(F32)
+            refs[4 + part][...] = value.astype(BF)
+
+    middles, done = run_kernel(
+        body,
+        [sds(middle_shape)] * 2,
+        [item for pair in state for item in pair],
+        after=after,
+        name="reduce_middle",
+        limit=3,
+    )
     sums = []
-    for part, (first, second) in enumerate(ORDERS):
-        send, keep = messages[2 * part], messages[2 * part + 1]
-        got = xor_permute(send, "tp", first)
-        middle = (keep[1].astype(F32) + got[1].astype(F32)).astype(BF)
-        sums += [keep, got, xor_permute(middle, "tp", second)]
-    return sums
-
-
-def shard_gather(halves):
+    for part, (_, second) in enumerate(ORDERS):
+        sums += [*state[part], xor_permute(middles[part], "tp", second)]
+    return sums, done
+
+
+def reduce_direct(messages):
+    mine, *sent = messages
+    return [mine] + [xor_permute(item, "tp", 1 + step) for step, item in enumerate(sent)]
+
+
+def gather_first(halves):
+    return [
+        (halves[part], xor_permute(halves[part], "tp", first))
+        for part, (first, _) in enumerate(ORDERS)
+    ]
+
+
+def gather_second(state, after=()):
+    half = state[0][0].shape
+    pair_shape = half[:-2] + (2,) + half[-2:]
+
+    def body(*refs):
+        for part in range(2):
+            for place in range(2):
+                refs[4 + part][..., place, :, :] = refs[2 * part + place][...]
+
+    pairs, done = run_kernel(
+        body,
+        [sds(pair_shape)] * 2,
+        [item for pair in state for item in pair],
+        after=after,
+        name="gather_middle",
+        limit=3,
+    )
     pieces = []
-    for part, (first, second) in enumerate(ORDERS):
-        near = xor_permute(halves[part], "tp", first)
-        far = xor_permute(jnp.stack([halves[part], near]), "tp", second)
-        pieces += [halves[part], near, far]
-    return pieces
+    for part, (_, second) in enumerate(ORDERS):
+        pieces += [*state[part], xor_permute(pairs[part], "tp", second)]
+    return pieces, done
+
+
+def gather_direct(mine):
+    return [mine] + [xor_permute(mine, "tp", step) for step in (1, 2, 3)]
 
 
 def total_of(refs):
+    if len(refs) == 4:
+        return sum([ref[...].astype(F32) for ref in refs[1:]], refs[0][...].astype(F32))
     halves = []
     for part in range(2):
         keep, got, late = refs[3 * part : 3 * part + 3]
@@ -395,6 +532,10 @@
 
 
 def place_gathered(store, tp_here, refs, size):
+    if len(refs) == 4:
+        for step, ref in enumerate(refs):
+            store(rows_at((tp_here ^ step) * size, size), ref[...])
+        return
     half = size // 2
     for part, (first, second) in enumerate(ORDERS):
         mine, near, far = refs[3 * part : 3 * part + 3]
@@ -404,6 +545,10 @@
 
 
 def emit_messages(load, tp_here, refs, size):
+    if refs[0].shape[-2] == size:
+        for step, ref in enumerate(refs):
+            ref[...] = load(rows_at((tp_here ^ step) * size, size))
+        return
     half = size // 2
     for part, (first, second) in enumerate(ORDERS):
         send, keep = refs[2 * part], refs[2 * part + 1]
@@ -412,17 +557,42 @@
                 ref[place] = load(rows_at((tp_here ^ step) * size + part * half, half))
 
 
-def message_shapes(half, width):
-    return [sds((2, half, width)) for _ in range(4)]
-
-
-def exchange(local, cross, first, second, third):
+def emit_shard(value, refs):
+    rows = value.shape[0] // len(refs)
+    for place, ref in enumerate(refs):
+        ref[...] = value[place * rows : (place + 1) * rows]
+
+
+def shard_shapes(size, width, direct=False):
+    return [sds((size, width))] if direct else [sds((size // 2, width))] * 2
+
+
+def message_shapes(half, width, direct=False):
+    return [sds((2 * half, width) if direct else (2, half, width))] * 4
+
+
+def exchange_chips(local, cross, first, second, third):
     got = [
         xor_permute(item, "ctx", 2 * (place + 1))
         for place, item in enumerate((first, second, third))
     ]
-    packed = jnp.stack([cross] + [item[1] for item in got])
-    return [local] + got + [xor_permute(packed, "ctx", 1)]
+    return [local, cross] + got
+
+
+def exchange_cores(state, after):
+    local, cross, *got = state
+
+    lead = cross.shape[:-2]
+
+    def body(cross_ref, first_ref, second_ref, third_ref, out_ref):
+        out_ref[..., 0, :, :] = cross_ref[...]
+        for place, ref in enumerate((first_ref, second_ref, third_ref)):
+            out_ref[..., place + 1, :, :] = ref[..., 1, :, :]
+
+    (packed,), done = run_kernel(
+        body, [sds(lead + (4,) + cross.shape[-2:])], [cross] + got, after=after, limit=2, name="pack"
+    )
+    return [local] + got + [xor_permute(packed, "ctx", 1)], done
 
 
 def exchanged(refs, here):
@@ -485,16 +655,26 @@
     return lax.dot_general(left, right, (((0,), (0,)), ((), ())), preferred_element_type=F32)
 
 
-def project(here, x_rows, gain, shift, weight, bias, tok_len):
-    rows, width = x_rows.shape
+def project(here, x_all, index, gain, shift, weight, bias, tok_len, after=()):
+    _, rows, width = x_all.shape
     inner = weight.shape[2]
     heads = inner // HD
 
-    def body(here_ref, x_ref, gain_ref, shift_ref, weight_ref, bias_ref, *rest):
-        norm_ref, outs, held = rest[0], rest[1:6], rest[6]
-        unit, _ = normalized(x_ref[...].astype(F32))
+    def body(here_ref, x_ref, gain_ref, shift_ref, weight_hbm, bias_ref, *rest):
+        norm_ref, outs, (held, weight_ref, x_held, sems) = rest[0], rest[1:6], rest[6:]
+        fetch = pltpu.make_async_copy(x_ref.at[index], x_held, sems.at[3])
+        fetch.start()
+        copies = [
+            pltpu.make_async_copy(weight_hbm.at[part], weight_ref.at[part], sems.at[part])
+            for part in range(3)
+        ]
+        for copy in copies:
+            copy.start()
+        fetch.wait()
+        unit, _ = normalized(x_held[...].astype(F32))
         norm_ref[...] = (unit * gain_ref[...] + shift_ref[...]).astype(BF)
         for part in range(3):
+            copies[part].wait()
             value = dot(norm_ref[...], weight_ref[part]) + bias_ref[part : part + 1]
             value = value.astype(BF)
             for head in range(heads):
@@ -508,10 +688,18 @@
     return run_kernel(
         body,
         [sds((rows, width))] + exchange_shapes(tok_len, 3 * HD),
-        [here, x_rows, gain, shift, weight, bias],
+        [here, x_all, gain, shift, weight, bias],
         flops=6 * rows * width * inner,
-        scratch=[pltpu.VMEM((heads, rows, 3 * HD), BF)],
+        scratch=[
+            pltpu.VMEM((heads, rows, 3 * HD), BF),
+            pltpu.VMEM(weight.shape, BF),
+            pltpu.VMEM((rows, width), BF),
+            pltpu.SemaphoreType.DMA((4,)),
+        ],
         name="project",
+        limit=14,
+        after=after,
+        in_hbm=(1, 4),
     )
 
 
@@ -522,10 +710,10 @@
     )
 
 
-def attention(here, received, seg_column, key_row, heads):
+def attention(here, received, seg_row, key_row, heads, after=()):
     tok_len = received[0].shape[0]
     block = tok_len // 2
-    seq_len = seg_column.shape[1]
+    seq_len = seg_row.shape[2]
     blocks = seq_len // block
     step = 256
     factor = LOG2E / math.sqrt(HD)
@@ -544,7 +732,7 @@
                 v_all[place] = rows[:, 2 * HD :]
         for number in range(seq_len // step):
             start, stop = number * step, (number + 1) * step
-            segs = seg_ref[seq, start:stop]
+            segs = as_column(seg_ref[seq, :, start:stop])
             scores = dot(q_all[start:stop], k_turned[:, :stop]) * factor
             scores = masked(scores, segs, key_ref, seq, start, stop)
             top = jnp.max(scores, axis=-1, keepdims=True)
@@ -564,7 +752,7 @@
     return run_kernel(
         body,
         exchange_shapes(tok_len, HD) + [sds((seq_len, 1), F32)],
-        [here] + list(received) + [seg_column, key_row],
+        [here] + list(received) + [seg_row, key_row],
         flops=2 * 2 * seq_len * seq_len * HD,
         exps=seq_len * seq_len // 2,
         scratch=[
@@ -573,8 +761,14 @@
             pltpu.VMEM((seq_len, HD), BF),
             pltpu.VMEM((seq_len, HD), BF),
         ],
+        after=after,
         name="attention",
-    )
+        limit=16,
+    )
+
+
+def as_column(row):
+    return jnp.broadcast_to(row, (128, row.shape[1])).T[:, :1]
 
 
 def masked(scores, segs, key_ref, seq, start, stop):
@@ -590,10 +784,12 @@
     return jnp.concatenate([left, corner], axis=1)
 
 
-def attention_back(here, received, grads, seg_column, key_row, lse, heads):
+def attention_back(
+    here, received, grads, seg_row, key_row, lse, heads, earlier, index, count, after=()
+):
     tok_len = received[0].shape[0]
     block = tok_len // 2
-    seq_len = seg_column.shape[1]
+    seq_len = seg_row.shape[2]
     blocks = seq_len // block
     step = 256
     scaler = 1.0 / math.sqrt(HD)
@@ -601,8 +797,9 @@
     def body(here_ref, *rest):
         refs, grad_refs = rest[:5], rest[5:10]
         seg_ref, key_ref, lse_ref = rest[10:13]
-        outs = rest[13:18]
-        q_all, k_all, k_turned, v_turned, g_all, result, dk_turned, dv_turned = rest[18:]
+        rest = rest[13 + len(earlier) :]
+        outs = [ref.at[0] for ref in rest[:5]]
+        q_all, k_all, k_turned, v_turned, g_all, result, dk_turned, dv_turned = rest[5:]
         me = here_ref[0]
         seq = me // heads
         for device, value in exchanged(refs, me):
@@ -618,7 +815,7 @@
         last = seq_len // step - 1
         for number in range(last, -1, -1):
             start, stop = number * step, (number + 1) * step
-            segs = seg_ref[seq, start:stop]
+            segs = as_column(seg_ref[seq, :, start:stop])
             query, grad = q_all[start:stop], g_all[start:stop]
             scores = dot(query, k_turned[:, :stop]) * (scaler * LOG2E)
             scores = masked(scores, segs, key_ref, seq, start, stop)
@@ -648,13 +845,21 @@
 
         emit_exchange(load, me, outs)
 
-    return run_kernel(
+    shapes = exchange_shapes(tok_len, 3 * HD)
+    args = [here, *received, *grads, seg_row, key_row, lse, *earlier]
+    first = len(args) - len(earlier)
+    return launch(
         body,
-        exchange_shapes(tok_len, 3 * HD),
-        [here] + list(received) + list(grads) + [seg_column, key_row, lse],
-        flops=5 * 2 * seq_len * seq_len * HD // 2,
-        exps=seq_len * seq_len // 2,
-        scratch=[
+        operands_of(args),
+        [pl.BlockSpec(memory_space=pltpu.SMEM)]
+        + [whole_of(item.shape) for item in args[1:first]]
+        + [pl.BlockSpec(memory_space=pl.ANY) for _ in earlier],
+        [sds((count,) + item.shape) for item in shapes],
+        [
+            pl.BlockSpec((1,) + item.shape, lambda i, n=len(item.shape): (index,) + (0,) * n)
+            for item in shapes
+        ],
+        [
             pltpu.VMEM((seq_len, HD), BF),
             pltpu.VMEM((seq_len, HD), BF),
             pltpu.VMEM((HD, seq_len), BF),
@@ -664,11 +869,16 @@
             pltpu.VMEM((HD, seq_len), F32),
             pltpu.VMEM((HD, seq_len), F32),
         ],
-        name="attention_back",
-    )
-
-
-def mix_heads(here, tp_here, received, weight, heads):
+        36 << 20,
+        cost(5 * seq_len * seq_len * HD, 12 * seq_len * HD),
+        "attention_back",
+        after,
+        grid=(1,),
+        aliases={first + number: number for number in range(len(earlier))},
+    )
+
+
+def mix_heads(here, tp_here, received, weight, heads, direct, after=()):
     tok_len = received[0].shape[0]
     inner, width = weight.shape
     rows = len_units(received) * tok_len // heads
@@ -688,11 +898,13 @@
 
     return run_kernel(
         body,
-        [sds((rows, inner))] + message_shapes(size // 2, width),
+        [sds((rows, inner))] + message_shapes(size // 2, width, direct),
         [here, tp_here] + list(received) + [weight],
         flops=2 * rows * inner * width,
         scratch=[pltpu.VMEM((rows, width), BF)],
+        after=after,
         name="mix_heads",
+        limit=6,
     )
 
 
@@ -700,196 +912,283 @@
     return 2 * received[-1].shape[0]
 
 
-def second_norm(tp_here, sums, x_rows, mixer_bias, gain, shift):
-    rows, width = x_rows.shape
-    size = rows // 4
-
-    def body(tp_ref, *rest):
-        refs, x_ref, bias_ref, gain_ref, shift_ref = rest[:6], *rest[6:10]
-        resid_ref, low_ref, high_ref = rest[10:]
-        mine = x_ref[rows_at(tp_ref[0] * size, size), :].astype(F32)
-        resid = mine + total_of(refs) + bias_ref[...]
+def second_norm(sums, x_mine, mixer_bias, gain, shift, direct, after=()):
+    size, width = x_mine.shape
+    count = len(sums)
+
+    def body(*rest):
+        refs, (x_ref, bias_ref, gain_ref, shift_ref) = rest[:count], rest[count : count + 4]
+        resid_ref, outs = rest[count + 4], rest[count + 5 :]
+        resid = x_ref[...].astype(F32) + total_of(refs) + bias_ref[...]
         resid_ref[...] = resid
         unit, _ = normalized(resid)
-        value = (unit * gain_ref[...] + shift_ref[...]).astype(BF)
-        low_ref[...] = value[: size // 2]
-        high_ref[...] = value[size // 2 :]
+        emit_shard((unit * gain_ref[...] + shift_ref[...]).astype(BF), outs)
 
     return run_kernel(
         body,
-        [sds((size, width), F32)] + [sds((size // 2, width))] * 2,
-        [tp_here] + list(sums) + [x_rows, mixer_bias, gain, shift],
+        [sds((size, width), F32)] + shard_shapes(size, width, direct),
+        list(sums) + [x_mine, mixer_bias, gain, shift],
         name="second_norm",
-    )
-
-
-def erf_of(value):
-    return lax.erf(value)
-
-
-def feed_forward(tp_here, pieces, cot, up_weight, up_bias, down_weight):
+        limit=8,
+        after=after,
+    )
+
+
+def feed_forward(
+    tp_here, pieces, cot, up_weight, up_bias, down_weight, earlier, index, count, direct, after=()
+):
     rows, width = cot.shape
     hidden = up_weight.shape[1]
     size = rows // 4
-    step = 256
-    count = hidden // step
+    step = 512
+    blocks = hidden // step
 
     def body(tp_ref, *rest):
-        refs, cot_ref, up_ref, bias_ref, down_ref = rest[:6], *rest[6:10]
-        norm_ref, act_ref, pre_ref, sum_ref = rest[10:14]
-        feed_outs, grad_outs = rest[14:18], rest[18:22]
-        feed, grad = rest[22:]
-        number = pl.program_id(0)
-
-        @pl.when(number == 0)
-        def _():
-            def store(place, value):
-                norm_ref[place, :] = value
-
-            place_gathered(store, tp_ref[0], refs, size)
-
-        pre = dot(norm_ref[...], up_ref[...]) + bias_ref[...]
-        grad_act = dot_nt(cot_ref[...], down_ref[...])
-        spread = 0.5 + 0.5 * erf_of(pre * math.sqrt(0.5))
-        dense = jnp.exp(-0.5 * pre * pre) * (1.0 / math.sqrt(2.0 * math.pi))
-        act = (pre * spread).astype(BF)
-        grad_pre = (grad_act * (spread + pre * dense)).astype(BF)
-        act_ref[...] = act
-        pre_ref[...] = grad_pre
-        sum_ref[...] = jnp.sum(grad_pre.astype(F32), axis=0, keepdims=True)
-        feed_part = dot(act, down_ref[...])
-        grad_part = dot_nt(grad_pre, up_ref[...])
-
-        @pl.when(number == 0)
-        def _():
-            feed[...] = feed_part
-            grad[...] = grad_part
-
-        @pl.when(number > 0)
-        def _():
-            feed[...] += feed_part
-            grad[...] += grad_part
-
-        @pl.when(number == count - 1)
-        def _():
-            emit_messages(lambda at: feed[at, :].astype(BF), tp_ref[0], feed_outs, size)
-            emit_messages(lambda at: grad[at, :].astype(BF), tp_ref[0], grad_outs, size)
-
-    whole = lambda *shape: pl.BlockSpec(shape, lambda i: (0,) * len(shape))
-    in_specs = (
+        refs, rest = rest[: len(pieces)], rest[len(pieces) :]
+        cot_ref, up_hbm, bias_ref, down_hbm = rest[:4]
+        rest = rest[4 + len(earlier) :]
+        norm_ref, act_ref, pre_ref, sum_ref, cot_sum_ref = rest[:5]
+        feed_outs, grad_outs = rest[5:9], rest[9:13]
+        up, down, held, sems = rest[13:]
+
+        def part(number):
+            return pl.ds(pl.multiple_of(number * step, step), step)
+
+        def copies(number):
+            place = part(number)
+            return (
+                pltpu.make_async_copy(up_hbm.at[:, place], up.at[:, place], sems.at[0, number]),
+                pltpu.make_async_copy(down_hbm.at[place, :], down.at[place, :], sems.at[1, number]),
+            )
+
+        for number in range(blocks):
+            for copy in copies(number):
+                copy.start()
+
+        def store(place, value):
+            norm_ref[place, :] = value
+
+        place_gathered(store, tp_ref[0], refs, size)
+        cot_sum_ref[...] = jnp.sum(cot_ref[...].astype(F32), axis=0, keepdims=True)
+
+        @pl.loop(0, blocks)
+        def _(number):
+            for copy in copies(number):
+                copy.wait()
+            place = part(number)
+            pre = dot(norm_ref[...], up[:, place]) + bias_ref[:, place]
+            grad_act = dot_nt(cot_ref[...], down[place, :])
+            spread = 0.5 + 0.5 * lax.erf(pre * math.sqrt(0.5))
+            dense = jnp.exp(-0.5 * pre * pre) * (1.0 / math.sqrt(2.0 * math.pi))
+            act_ref[:, place] = (pre * spread).astype(BF)
+            grad_pre = (grad_act * (spread + pre * dense)).astype(BF)
+            pre_ref[:, place] = grad_pre
+            sum_ref[:, place] = jnp.sum(grad_pre.astype(F32), axis=0, keepdims=True)
+
+        @pl.loop(0, width // step)
+        def _(number):
+            place = part(number)
+            held[:, place] = dot_nt(pre_ref[...], up[place, :]).astype(BF)
+
+        emit_messages(lambda at: held[at, :], tp_ref[0], grad_outs, size)
+
+        @pl.loop(0, width // step)
+        def _(number):
+            place = part(number)
+            held[:, place] = dot(act_ref[...], down[:, place]).astype(BF)
+
+        emit_messages(lambda at: held[at, :], tp_ref[0], [ref.at[0] for ref in feed_outs], size)
+
+    message = (2, size // 2, width)
+    args = [tp_here, *pieces, cot, up_weight, up_bias, down_weight, *earlier]
+    first = len(args) - len(earlier)
+    outs = [
+        sds((rows, width)),
+        sds((rows, hidden)),
+        sds((rows, hidden)),
+        sds((1, hidden), F32),
+        sds((1, width), F32),
+    ]
+    messages = message_shapes(size // 2, width, direct)
+    return launch(
+        body,
+        operands_of(args),
         [pl.BlockSpec(memory_space=pltpu.SMEM)]
-        + [whole(*piece.shape) for piece in pieces]
-        + [
-            whole(rows, width),
-            pl.BlockSpec((width, step), lambda i: (0, i)),
-            pl.BlockSpec((1, step), lambda i: (0, i)),
-            pl.BlockSpec((step, width), lambda i: (i, 0)),
-        ]
-    )
-    out_specs = (
+        + [whole_of(piece.shape) for piece in pieces]
+        + [cot.spec(), pl.BlockSpec(memory_space=pl.ANY), whole_of(up_bias.shape)]
+        + [pl.BlockSpec(memory_space=pl.ANY)] * (1 + len(earlier)),
+        outs + [sds((count,) + message)] * 4 + messages,
+        [whole_of(item.shape) for item in outs]
+        + [pl.BlockSpec((1,) + message, lambda i: (index, 0, 0, 0))] * 4
+        + [whole_of(item.shape) for item in messages],
         [
-            whole(rows, width),
-            pl.BlockSpec((rows, step), lambda i: (0, i)),
-            pl.BlockSpec((rows, step), lambda i: (0, i)),
-            pl.BlockSpec((1, step), lambda i: (0, i)),
-        ]
-        + [whole(2, size // 2, width)] * 8
-    )
-    outs = (
-        [sds((rows, width)), sds((rows, hidden)), sds((rows, hidden)), sds((1, hidden), F32)]
-        + message_shapes(size // 2, width)
-        + message_shapes(size // 2, width)
-    )
-    return pl.pallas_call(
-        body,
-        grid=(count,),
-        out_shape=tuple(outs),
-        in_specs=in_specs,
-        out_specs=tuple(out_specs),
-        scratch_shapes=[pltpu.VMEM((rows, width), F32), pltpu.VMEM((rows, width), F32)],
-        compiler_params=pltpu.CompilerParams(vmem_limit_bytes=56 << 20),
-        cost_estimate=pl.CostEstimate(
-            flops=8 * rows * width * hidden,
-            bytes_accessed=4 * width * hidden + 20 * rows * width,
-            transcendentals=2 * rows * hidden,
-        ),
-        name="feed_forward",
-    )(tp_here, *pieces, cot, up_weight, up_bias, down_weight)
-
-
-def second_norm_back(tp_here, sums, resid, cot, gain):
+            pltpu.VMEM((width, hidden), BF),
+            pltpu.VMEM((hidden, width), BF),
+            pltpu.VMEM((rows, width), BF),
+            pltpu.SemaphoreType.DMA((2, blocks)),
+        ],
+        50 << 20,
+        cost(8 * rows * width * hidden, 4 * width * hidden + 20 * rows * width),
+        "feed_forward",
+        after,
+        grid=(1,),
+        aliases={first + number: 5 + number for number in range(len(earlier))},
+    )
+
+
+def second_norm_back(sums, resid, cot_mine, gain, direct, after=()):
     size, width = resid.shape
-
-    def body(tp_ref, *rest):
-        refs, resid_ref, cot_ref, gain_ref = rest[:6], *rest[6:9]
-        grad_ref, low_ref, high_ref, gain_out, shift_out = rest[9:]
+    count = len(sums)
+
+    def body(*rest):
+        refs, (resid_ref, cot_ref, gain_ref) = rest[:count], rest[count : count + 3]
+        grad_ref, gain_out, shift_out, *outs = rest[count + 3 :]
         back, gain_sum, shift_sum = norm_back(resid_ref[...], gain_ref[...], total_of(refs))
-        grad = back + cot_ref[rows_at(tp_ref[0] * size, size), :].astype(F32)
+        grad = back + cot_ref[...].astype(F32)
         grad_ref[...] = grad
-        low = grad.astype(BF)
-        low_ref[...] = low[: size // 2]
-        high_ref[...] = low[size // 2 :]
+        emit_shard(grad.astype(BF), outs)
         gain_out[...] = gain_sum
         shift_out[...] = shift_sum
 
     return run_kernel(
         body,
         [sds((size, width), F32)]
-        + [sds((size // 2, width))] * 2
-        + [sds((1, width), F32)] * 2,
-        [tp_here] + list(sums) + [resid, cot, gain],
+        + [sds((1, width), F32)] * 2
+        + shard_shapes(size, width, direct),
+        list(sums) + [resid, cot_mine, gain],
         name="second_norm_back",
-    )
-
-
-def first_norm_back(tp_here, sums, x_rows, grad_resid, gain):
-    size, width = grad_resid.shape
-
-    def body(tp_ref, *rest):
-        refs, x_ref, grad_ref, gain_ref = rest[:6], *rest[6:9]
-        low_ref, high_ref, gain_out, shift_out = rest[9:]
-        mine = x_ref[rows_at(tp_ref[0] * size, size), :].astype(F32)
-        back, gain_sum, shift_sum = norm_back(mine, gain_ref[...], total_of(refs))
-        low = (back + grad_ref[...]).astype(BF)
-        low_ref[...] = low[: size // 2]
-        high_ref[...] = low[size // 2 :]
-        gain_out[...] = gain_sum
-        shift_out[...] = shift_sum
+        limit=10,
+        after=after,
+    )
+
+
+def first_norm_back(sums, x_mine, grad_resids, gain, after=()):
+    count = len(x_mine)
+    size, width = grad_resids[0].shape
+
+    def body(*rest):
+        refs, rest = rest[:6], rest[6:]
+        x_refs, grad_refs, gain_ref = rest[:count], rest[count : 2 * count], rest[2 * count]
+        gain_out, shift_out, *outs = rest[2 * count + 1 :]
+        for index in range(count):
+            back, gain_sum, shift_sum = norm_back(
+                x_refs[index][...].astype(F32),
+                gain_ref[...],
+                total_of([ref.at[index] for ref in refs]),
+            )
+            emit_shard(
+                (back + grad_refs[index][...]).astype(BF), [ref.at[index] for ref in outs]
+            )
+            gain_out[...] = gain_sum if index == 0 else gain_out[...] + gain_sum
+            shift_out[...] = shift_sum if index == 0 else shift_out[...] + shift_sum
 
     return run_kernel(
         body,
-        [sds((size // 2, width))] * 2 + [sds((1, width), F32)] * 2,
-        [tp_here] + list(sums) + [x_rows, grad_resid, gain],
+        [sds((1, width), F32)] * 2
+        + [sds((count,) + item.shape) for item in shard_shapes(size, width)],
+        list(sums) + list(x_mine) + list(grad_resids) + [gain],
         name="first_norm_back",
-    )
-
-
-def finish_output(sums, resid, bias):
-    size, width = resid.shape
+        limit=10,
+        after=after,
+    )
+
+
+def finish_outputs(sums, resids, bias, after=()):
+    size, width = resids[0].shape
+    half = size // 2
+    count = len(resids)
 
     def body(*rest):
-        refs, resid_ref, bias_ref, low_ref, high_ref = rest[:6], *rest[6:]
-        value = (resid_ref[...] + total_of(refs) + bias_ref[...]).astype(BF)
-        low_ref[...] = value[: size // 2]
-        high_ref[...] = value[size // 2 :]
+        refs, resid_refs, bias_ref = rest[:6], rest[6 : 6 + count], rest[6 + count]
+        low_ref, high_ref = rest[7 + count :]
+        for index in range(count):
+            ours = [ref.at[index] for ref in refs]
+            value = (resid_refs[index][...] + total_of(ours) + bias_ref[...]).astype(BF)
+            low_ref[index] = value[:half]
+            high_ref[index] = value[half:]
 
     return run_kernel(
         body,
-        [sds((size // 2, width))] * 2,
-        list(sums) + [resid, bias],
-        name="finish_output",
-    )
-
-
-def heads_back(here, tp_here, pieces, weight, tok_len):
+        [sds((count, half, width))] * 2,
+        list(sums) + list(resids) + [bias],
+        after=after,
+        name="finish_outputs",
+        limit=8,
+    )
+
+
+def assemble_outputs(tp_here, pieces, dtype, after=()):
+    count, half, width = pieces[0].shape
+    size = 2 * half
+    rows = 4 * size
+
+    def block_of(shape):
+        return pl.BlockSpec((1,) + shape[1:], lambda i, n=len(shape) - 1: (i,) + (0,) * n)
+
+    def body(tp_ref, *rest):
+        refs, out_ref = rest[:6], rest[6]
+
+        def store(place, value):
+            out_ref[0, place, :] = value.astype(dtype)
+
+        place_gathered(store, tp_ref[0], [ref.at[0] for ref in refs], size)
+
+    results, done = launch(
+        body,
+        [tp_here] + list(pieces),
+        [pl.BlockSpec(memory_space=pltpu.SMEM)] + [block_of(piece.shape) for piece in pieces],
+        [HBM((count, rows, width), dtype)],
+        [block_of((count, rows, width))],
+        (),
+        24 << 20,
+        cost(0, count * rows * width * 6),
+        "assemble_outputs",
+        after,
+        grid=(count,),
+    )
+    return results[0], done
+
+
+def widen(part, turned, after=()):
+    rows, wide = part.shape
+
+    def body(part_ref, out_ref):
+        value = part_ref[...].astype(F32)
+        out_ref[...] = value.T if turned else value
+
+    shape = (wide, rows) if turned else (rows, wide)
+    return run_kernel(body, [sds(shape, F32)], [part], after=after, name="widen", limit=6)
+
+
+def widen_last(part, inner, after=()):
+    rows, _ = part.shape
+
+    def body(part_ref, proj_ref, mixer_ref):
+        for number in range(3):
+            place = slice(number * inner, (number + 1) * inner)
+            proj_ref[number] = part_ref[:, place].astype(F32)
+        mixer_ref[...] = part_ref[:, 3 * inner :].astype(F32).T
+
+    return run_kernel(
+        body,
+        [sds((3, rows, inner), F32), sds((inner, rows), F32)],
+        [part],
+        after=after,
+        name="widen",
+        limit=6,
+    )
+
+
+def heads_back(here, tp_here, pieces, weight, tok_len, after=()):
     inner, width = weight.shape
     heads = inner // HD
-    size = 2 * pieces[0].shape[0]
+    count = len(pieces)
+    size = pieces[0].shape[0] * (1 if count == 4 else 2)
     rows = 4 * size
 
     def body(here_ref, tp_ref, *rest):
-        refs, weight_ref = rest[:6], rest[6]
-        mix_ref, sum_ref, outs, held = rest[7], rest[8], rest[9:14], rest[14]
+        refs, weight_ref, rest = rest[:count], rest[count], rest[count + 1 :]
+        mix_ref, sum_ref, outs, held = rest[0], rest[1], rest[2:7], rest[7]
 
         def store(place, value):
             mix_ref[place, :] = value
@@ -911,111 +1210,103 @@
         [here, tp_here] + list(pieces) + [weight],
         flops=2 * rows * inner * width,
         scratch=[pltpu.VMEM((heads, rows, HD), BF)],
+        after=after,
         name="heads_back",
-    )
-
-
-def project_back(here, tp_here, received, weight):
-    tok_len = received[0].shape[0]
+        limit=8,
+    )
+
+
+def project_back(here, tp_here, received, weight, after=()):
+    count, tok_len, _ = received[0].shape
     _, width, inner = weight.shape
     heads = inner // HD
-    rows = len_units(received) * tok_len // heads
+    rows = 2 * received[-1].shape[1] * tok_len // heads
     size = rows // 4
 
     def body(here_ref, tp_ref, *rest):
-        refs, weight_ref = rest[:5], rest[5]
-        proj_ref, sum_ref, outs, held = rest[6], rest[7], rest[8:12], rest[12]
-        for unit_id, value in exchanged(refs, here_ref[0]):
-            place = rows_at(unit_id // heads * tok_len, tok_len)
-            for part in range(3):
-                column = pl.multiple_of(part * inner + unit_id % heads * HD, HD)
-                proj_ref[place, pl.ds(column, HD)] = value[:, part * HD : (part + 1) * HD]
-        sum_ref[...] = jnp.sum(proj_ref[...].astype(F32), axis=0, keepdims=True)
-        for start in range(0, width, 512):
-            value = dot_nt(proj_ref[:, :inner], weight_ref[0, start : start + 512])
-            for part in range(1, 3):
-                value += dot_nt(
-                    proj_ref[:, part * inner : (part + 1) * inner],
-                    weight_ref[part, start : start + 512],
-                )
-            held[:, start : start + 512] = value.astype(BF)
-        emit_messages(lambda place: held[place, :], tp_ref[0], outs, size)
+        refs, weight_ref, rest = rest[:5], rest[5], rest[6:]
+        proj_refs, sum_ref, outs, held = rest[:count], rest[count], rest[-5:-1], rest[-1]
+        for index, proj_ref in enumerate(proj_refs):
+            for unit_id, value in exchanged([ref.at[index] for ref in refs], here_ref[0]):
+                place = rows_at(unit_id // heads * tok_len, tok_len)
+                for part in range(3):
+                    column = pl.multiple_of(part * inner + unit_id % heads * HD, HD)
+                    proj_ref[place, pl.ds(column, HD)] = value[:, part * HD : (part + 1) * HD]
+            part_sum = jnp.sum(proj_ref[...].astype(F32), axis=0, keepdims=True)
+            sum_ref[...] = part_sum if index == 0 else sum_ref[...] + part_sum
+            for start in range(0, width, 512):
+                value = dot_nt(proj_ref[:, :inner], weight_ref[0, start : start + 512])
+                for part in range(1, 3):
+                    value += dot_nt(
+                        proj_ref[:, part * inner : (part + 1) * inner],
+                        weight_ref[part, start : start + 512],
+                    )
+                held[:, start : start + 512] = value.astype(BF)
+            emit_messages(
+                lambda place: held[place, :], tp_ref[0], [ref.at[index] for ref in outs], size
+            )
 
     return run_kernel(
         body,
-        [sds((rows, 3 * inner)), sds((1, 3 * inner), F32)] + message_shapes(size // 2, width),
+        [sds((rows, 3 * inner))] * count
+        + [sds((1, 3 * inner), F32)]
+        + [sds((count,) + item.shape) for item in message_shapes(size // 2, width)],
         [here, tp_here] + list(received) + [weight],
-        flops=6 * rows * inner * width,
+        flops=6 * count * rows * inner * width,
         scratch=[pltpu.VMEM((rows, width), BF)],
         name="project_back",
-    )
-
-
-def assemble(tp_here, pieces, earlier, index, count, dtype):
-    half, width = pieces[0].shape
-    size = 2 * half
-    rows = 4 * size
-
-    def body(tp_ref, *rest):
-        refs, out_ref = rest[:6], rest[-1]
-
-        def store(place, value):
-            out_ref[0, place, :] = value.astype(dtype)
-
-        place_gathered(store, tp_ref[0], refs, size)
-
-    args = [tp_here] + list(pieces)
-    in_specs = [pl.BlockSpec(memory_space=pltpu.SMEM)] + [
-        pl.BlockSpec(piece.shape, lambda i, n=piece.ndim: (0,) * n) for piece in pieces
-    ]
-    aliases = {}
-    if earlier is not None:
-        aliases = {len(args): 0}
-        args.append(earlier)
-        in_specs.append(pl.BlockSpec(memory_space=pl.ANY))
-    return pl.pallas_call(
+        limit=10,
+        after=after,
+    )
+
+
+def weight_grad(groups, step=512, after=()):
+    count = len(groups[0][0])
+    rows, tall = groups[0][0][0].shape
+    widths = [rights[0].shape[1] for _, rights in groups]
+    step = min(step, tall)
+
+    def body(*refs):
+        out_ref = refs[-1]
+        start = 0
+        for place, wide in enumerate(widths):
+            ours = refs[2 * count * place : 2 * count * (place + 1)]
+            value = dot_tn(ours[0][...], ours[count][...])
+            for number in range(1, count):
+                value += dot_tn(ours[number][...], ours[count + number][...])
+            out_ref[:, start : start + wide] = value.astype(BF)
+            start += wide
+
+    in_specs = []
+    args = []
+    for (lefts, rights), wide in zip(groups, widths):
+        for item in lefts:
+            if isinstance(item, Part):
+                in_specs.append(
+                    pl.BlockSpec((None, rows, step), lambda i, k=item.index: (k, 0, i))
+                )
+            else:
+                in_specs.append(pl.BlockSpec((rows, step), lambda i: (0, i)))
+        in_specs += [pl.BlockSpec((rows, wide), lambda i: (0, 0))] * count
+        args += list(lefts) + list(rights)
+    total = sum(widths)
+    results, done = launch(
         body,
-        grid=(1,),
-        out_shape=sds((count, rows, width), dtype),
-        in_specs=in_specs,
-        out_specs=pl.BlockSpec((1, rows, width), lambda i: (index, 0, 0)),
-        input_output_aliases=aliases,
-        compiler_params=pltpu.CompilerParams(vmem_limit_bytes=32 << 20),
-        cost_estimate=pl.CostEstimate(
-            flops=0, bytes_accessed=rows * width * 6, transcendentals=0
+        operands_of(args),
+        in_specs,
+        [HBM((tall, total), BF)],
+        [pl.BlockSpec((step, total), lambda i: (i, 0))],
+        (),
+        30 << 20,
+        cost(
+            2 * count * rows * tall * total,
+            2 * (count * rows * (tall * len(groups) + total) + tall * total),
         ),
-        name="assemble",
-    )(*args)
-
-
-def weight_grad(lefts, rights, step=512):
-    count = len(lefts)
-    rows, tall = lefts[0].shape
-    wide = rights[0].shape[1]
-    step = min(step, tall)
-
-    def body(*rest):
-        left_refs, right_refs, out_ref = rest[:count], rest[count : 2 * count], rest[-1]
-        value = dot_tn(left_refs[0][...], right_refs[0][...])
-        for place in range(1, count):
-            value += dot_tn(left_refs[place][...], right_refs[place][...])
-        out_ref[...] = value.astype(BF)
-
-    return pl.pallas_call(
-        body,
+        "weight_grad",
+        after,
         grid=(tall // step,),
-        out_shape=sds((tall, wide)),
-        in_specs=[pl.BlockSpec((rows, step), lambda i: (0, i))] * count
-        + [pl.BlockSpec((rows, wide), lambda i: (0, 0))] * count,
-        out_specs=pl.BlockSpec((step, wide), lambda i: (i, 0)),
-        compiler_params=pltpu.CompilerParams(vmem_limit_bytes=48 << 20),
-        cost_estimate=pl.CostEstimate(
-            flops=2 * count * rows * tall * wide,
-            bytes_accessed=2 * (count * rows * (tall + wide) + tall * wide),
-            transcendentals=0,
-        ),
-        name="weight_grad",
-    )(*lefts, *rights)
+    )
+    return results[0], done
 
 
 def small_sums(values):
@@ -1061,102 +1352,185 @@
     x_all = inputs.reshape(micro_count, rows, width)
     cot_all = out_cotangent.reshape(micro_count, rows, width)
     key_rows = jnp.where(keep_mask > 0, segments, -1)[:, :, None, :]
-    seg_columns = segments[:, :, :, None]
     gain_one, shift_one = first_gain[None], first_shift[None]
     gain_two, shift_two = second_gain[None], second_shift[None]
     mix_bias, low_bias, high_bias = mixer_bias[None], down_bias[None], up_bias[None]
     micro = range(micro_count)
 
+    key_rows = [key_rows[index] for index in micro]
+    seg_rows = [segments[index][:, None, :] for index in micro]
+    cots = [Part(cot_all, index) for index in micro]
+    size = rows // lax.axis_size("tp")
+    start = tp_here[0] * size
+    x_mine = [lax.dynamic_slice(x_all, (index, start, 0), (1, size, width))[0] for index in micro]
+    cot_mine = [
+        lax.dynamic_slice(cot_all, (index, start, 0), (1, size, width))[0] for index in micro
+    ]
+
+    def scattered(part):
+        return lax.psum_scatter(part, "ctx", scatter_dimension=0, tiled=True)
+
     norm_one, received, lses, heads_low, resids = [], [], [], [], []
-    for index in micro:
-        normed, *sent = project(
-            here, x_all[index], gain_one, shift_one, weight_three, bias_three, tok_len
+
+    def project_micro(index, done):
+        (normed, *sent), done = project(
+            here, x_all, index, gain_one, shift_one, weight_three, bias_three, tok_len, after=done
         )
         norm_one.append(normed)
-        received.append(exchange(*sent))
-    gathered_two = []
-    for index in micro:
-        *sent, lse = attention(here, received[index], seg_columns[index], key_rows[index], heads)
+        return exchange_chips(*sent), done
+
+    def attend_micro(index, got, done):
+        received.append(got)
+        (*sent, lse), done = attention(
+            here, got, seg_rows[index], key_rows[index], heads, after=done
+        )
         lses.append(lse)
-        mixed, *messages = mix_heads(here, tp_here, exchange(*sent), mixer_weight, heads)
+        return exchange_chips(*sent), done
+
+    def mix_micro(got, direct, done):
+        (mixed, *messages), done = mix_heads(
+            here, tp_here, got, mixer_weight, heads, direct, after=done
+        )
         heads_low.append(mixed)
-        resid, low, high = second_norm(
-            tp_here, shard_reduce(messages), x_all[index], mix_bias, gain_two, shift_two
+        return messages, done
+
+    def norm_micro(index, sums, direct, done):
+        (resid, *shard), done = second_norm(
+            sums, x_mine[index], mix_bias, gain_two, shift_two, direct, after=done
         )
         resids.append(resid)
-        gathered_two.append(shard_gather((low, high)))
-    norm_two, acts, grad_pres, up_sums, feeds, grad_twos = [], [], [], [], [], []
-    for index in micro:
-        normed, act, grad_pre, up_sum, *messages = feed_forward(
-            tp_here, gathered_two[index], cot_all[index], up_weight, high_bias, down_weight
+        return shard if direct else gather_first(shard), done
+
+    norm_two, acts, grad_pres, up_sums, cot_sums = [], [], [], [], []
+
+    def feed_micro(index, pieces, feeds, done):
+        (normed, act, grad_pre, up_sum, cot_sum, *messages), done = feed_forward(
+            tp_here,
+            pieces,
+            cots[index],
+            up_weight,
+            high_bias,
+            down_weight,
+            feeds,
+            index,
+            micro_count,
+            True,
+            after=done,
         )
         norm_two.append(normed)
         acts.append(act)
         grad_pres.append(grad_pre)
         up_sums.append(up_sum)
-        feeds.append(messages[:4])
-        grad_twos.append(messages[4:])
-    grad_resids, gain_twos, shift_twos, gathered_mix = [], [], [], []
-    for index in micro:
-        grad_resid, low, high, gain_sum, shift_sum = second_norm_back(
-            tp_here, shard_reduce(grad_twos[index]), resids[index], cot_all[index], gain_two
+        cot_sums.append(cot_sum)
+        return messages[:4], reduce_direct(messages[4:]), done
+
+    grad_resids, gain_twos, shift_twos = [], [], []
+    grad_mixes, mix_sums, states = [], [], []
+
+    def norm_back_micro(index, sums, done):
+        (grad_resid, gain_sum, shift_sum, *shard), done = second_norm_back(
+            sums, resids[index], cot_mine[index], gain_two, False, after=done
         )
         grad_resids.append(grad_resid)
         gain_twos.append(gain_sum)
         shift_twos.append(shift_sum)
-        gathered_mix.append(shard_gather((low, high)))
-
-    def scattered(part, dim):
-        return lax.psum_scatter(part, "ctx", scatter_dimension=dim, tiled=True).astype(F32)
-
-    cots = [cot_all[index] for index in micro]
-    down_grad = scattered(weight_grad(acts, cots), 1)
-    up_grad = scattered(weight_grad(norm_two, grad_pres), 0)
-
-    grad_mixes, mix_sums, grad_projs, proj_sums, gain_ones, shift_ones = [], [], [], [], [], []
-    input_grad = None
-    outputs = None
-    for index in micro:
-        grad_mix, mix_sum, *sent = heads_back(
-            here, tp_here, gathered_mix[index], mixer_weight, tok_len
+        return gather_first(shard), done
+
+    def heads_back_micro(index, pieces, done):
+        (grad_mix, mix_sum, *sent), done = heads_back(
+            here, tp_here, pieces, mixer_weight, tok_len, after=done
         )
         grad_mixes.append(grad_mix)
         mix_sums.append(mix_sum)
-        sent = attention_back(
+        states.append(exchange_chips(*sent))
+        return done
+
+    def attend_back_micro(index, got, earlier, done):
+        return attention_back(
             here,
             received[index],
-            exchange(*sent),
-            seg_columns[index],
+            got,
+            seg_rows[index],
             key_rows[index],
             lses[index],
             heads,
-        )
-        grad_proj, proj_sum, *messages = project_back(
-            here, tp_here, exchange(*sent), weight_three
-        )
-        grad_projs.append(grad_proj)
-        proj_sums.append(proj_sum)
-        low, high, gain_sum, shift_sum = first_norm_back(
-            tp_here, shard_reduce(messages), x_all[index], grad_resids[index], gain_one
-        )
-        gain_ones.append(gain_sum)
-        shift_ones.append(shift_sum)
-        input_grad = assemble(
-            tp_here, shard_gather((low, high)), input_grad, index, micro_count, F32
-        )
-    for index in micro:
-        halves = finish_output(shard_reduce(feeds[index]), resids[index], low_bias)
-        outputs = assemble(tp_here, shard_gather(halves), outputs, index, micro_count, BF)
-    mixer_grad = scattered(weight_grad(heads_low, grad_mixes), 1)
-    proj_grad = scattered(weight_grad(norm_one, grad_projs), 0)
+            earlier,
+            index,
+            micro_count,
+            after=done,
+        )
+
+    state_a, done = project_micro(0, ())
+    state_b, done = project_micro(1, done)
+    got, done = exchange_cores(state_a, done)
+    state_a, done = attend_micro(0, got, done)
+    got, done = exchange_cores(state_b, done)
+    state_b, done = attend_micro(1, got, done)
+    got, done = exchange_cores(state_a, done)
+    messages, done = mix_micro(got, False, done)
+    sums_a, done = reduce_second(reduce_first(messages), done)
+    state_a, done = norm_micro(0, sums_a, False, done)
+    got, done = exchange_cores(state_b, done)
+    messages, done = mix_micro(got, False, done)
+    state_b = reduce_first(messages)
+    pieces_a, done = gather_second(state_a, done)
+    sums_b, done = reduce_second(state_b, done)
+    state_b, done = norm_micro(1, sums_b, True, done)
+    pieces_b = gather_direct(state_b[0])
+    feeds, sums_a, done = feed_micro(0, pieces_a, [], done)
+    feeds, sums_b, done = feed_micro(1, pieces_b, feeds, done)
+    state_a, done = norm_back_micro(0, sums_a, done)
+    down_part, done = weight_grad([(cots, acts)], after=done)
+    pieces_a, done = gather_second(state_a, done)
+    (down_part,), done = held_until([down_part], done)
+    down_grad = scattered(down_part)
+    up_part, done = weight_grad([(norm_two, grad_pres)], after=done)
+    done = heads_back_micro(0, pieces_a, done)
+    state_b, done = norm_back_micro(1, sums_b, done)
+    got_a, done = exchange_cores(states[0], done)
+    pieces_b, done = gather_second(state_b, done)
+    done = heads_back_micro(1, pieces_b, done)
+    feeds, done = held_until(feeds, done)
+    state_feed = reduce_first(feeds)
+    sent, done = attend_back_micro(0, got_a, [], done)
+    got_b, done = exchange_cores(states[1], done)
+    sums_feed, done = reduce_second(state_feed, done)
+    sent, done = attend_back_micro(1, got_b, sent, done)
+    state_back = exchange_chips(*sent)
+    halves, done = finish_outputs(sums_feed, resids, low_bias, after=done)
+    state_out = gather_first(halves)
+    got, done = exchange_cores(state_back, done)
+    (up_part,), done = held_until([up_part], done)
+    up_grad = scattered(up_part)
+    (*grad_projs, proj_sum, first, second, third, fourth), done = project_back(
+        here, tp_here, got, weight_three, after=done
+    )
+    state_one = reduce_first((first, second, third, fourth))
+    last_part, done = weight_grad(
+        [(norm_one, grad_projs), (grad_mixes, heads_low)], after=done
+    )
+    pieces_out, done = gather_second(state_out, done)
+    (last_part,), done = held_until([last_part], done)
+    last_grad = scattered(last_part)
+    sums_one, done = reduce_second(state_one, done)
+    (gain_sum, shift_sum, *halves), done = first_norm_back(
+        sums_one, x_mine, grad_resids, gain_one, after=done
+    )
+    outputs, done = assemble_outputs(tp_here, pieces_out, BF, after=done)
+    gain_ones, shift_ones, proj_sums = [gain_sum], [shift_sum], [proj_sum]
+    pieces_in, done = gather_second(gather_first(halves), done)
+    input_grad, done = assemble_outputs(tp_here, pieces_in, F32, after=done)
+    (down_grad,), done = widen(down_grad, True, after=done)
+    (up_grad,), done = widen(up_grad, False, after=done)
+    (proj_grad, mixer_grad), done = widen_last(last_grad, inner, after=done)
+    proj_grad = jnp.transpose(proj_grad, (1, 0, 2))
 
     def over_micro(items):
         return sum(items[1:], items[0]).reshape(ctx_count, -1)
 
-    cot_sum = jnp.sum(out_cotangent.astype(F32), axis=(0, 1, 2)).reshape(ctx_count, -1)
     proj_sum = sum(proj_sums[1:], proj_sums[0]).reshape(3, ctx_count, -1)
     pair_sum = jnp.concatenate([proj_sum[0], proj_sum[2]], axis=1)
-    share = cot_sum.shape[1]
+    share = width // ctx_count
     pair_sum = jnp.pad(pair_sum, ((0, 0), (0, share - pair_sum.shape[1])))
     kinds = [
         over_micro(gain_ones),
@@ -1164,7 +1538,7 @@
         over_micro(gain_twos),
         over_micro(shift_twos),
         over_micro(mix_sums),
-        cot_sum,
+        over_micro(cot_sums),
         over_micro(up_sums),
         pair_sum,
     ]
@@ -1178,7 +1552,7 @@
         input_grad.reshape(inputs.shape),
         norms[0],
         norms[1],
-        proj_grad.reshape(width // ctx_count, 3, inner),
+        proj_grad,
         proj_bias_grad,
         mixer_grad,
         small[4],
@@ -1195,10 +1569,10 @@
     sizes = dict(mesh.shape)
 
     def chosen(*args):
-        seq_count, width = args[0].shape[1], args[0].shape[3]
+        micro, seq_count, _, width = args[0].shape
         units = seq_count * args[6].shape[1] // HD
         fits = sizes["ctx"] == 8 and sizes["tp"] == 4 and units == sizes["ctx"]
-        fits = fits and args[12].shape[0] == width
+        fits = fits and args[12].shape[0] == width and micro == 2
         return (per_device_exchanged if fits else per_device)(*args)
 
     return chosen

time: 775 us -> 666 us (0.86)
  waiting for transfers between devices: 309 us -> 277 us
  other arithmetic: 30.5 us -> 0.28 us
  Pallas kernels: 213 us -> 186 us
  starting transfers between devices: 138 us -> 121 us
    reduce_scatter x4 -> x3, waiting for transfers between devices: 55.9 us -> 27.7 us  [scattered(): return lax.psum_scatter(part, 'ctx', scatter_dimension=0, tiled=True)]
    pallas_call x30 -> x43, Pallas kernels: 213 us -> 186 us  [launch(): pl.pallas_call(inner, grid=grid, out_shape=(*outs, sds((8, 128), F32)), i...]
    ppermute x101 -> x78, starting transfers between devices: 138 us -> 121 us  [xor_permute(): return lax.ppermute(values, axis, [(i, i ^ step) for i in range(count)])]
    convert_element_type x19 -> x0, other arithmetic: 16.4 us -> none  [the longest x16 9.13 us: shard_reduce(): middle = (keep[1].astype(F32) + got[1].astype(F32)).astype(BF)]
    unnamed x283 -> x274, local copies, waits for them, and re-layouts: 41.4 us -> 55.2 us
    another operation x24 -> x0, other arithmetic: 12.6 us -> none  [the longest x16 9.4 us: shard_gather(): far = xor_permute(jnp.stack([halves[part], near]), 'tp', second)]
    slice x26 -> x0, local copies, waits for them, and re-layouts: 8.88 us -> none  [the longest x1 4.82 us: per_device_exchanged(): cot_all[index]]
    ppermute x101 -> x78, waiting for transfers between devices: 253 us -> 249 us  [xor_permute(): return lax.ppermute(values, axis, [(i, i ^ step) for i in range(count)])]
  transfers between devices with their start and end apart: 105 -> 81, of which waited for: 49 -> 37; matrix products, arithmetic and copies ran while one was open for 6% -> 1% of each run, Pallas kernels for 26% -> 26%
where the time goes in v2:
time: 666 us; the launch traced here: 661 us
  waiting for transfers between devices  277 us (42%)
  Pallas kernels  186 us (28%)
  starting transfers between devices  121 us (18%)
  local copies, waits for them, and re-layouts  61.7 us (9%)
  between operations  15.6 us (2%)
    ppermute x78, waiting for transfers between devices, xor_permute(): return lax.ppermute(values, axis, [(i, i ^ step) for i in range(count)])  249 us
    pallas_call x43, Pallas kernels, launch(): pl.pallas_call(inner, grid=grid, out_shape=(*outs, sds((8, 128), F32)), i...  186 us
    ppermute x78, starting transfers between devices, xor_permute(): return lax.ppermute(values, axis, [(i, i ^ step) for i in range(count)])  121 us
    unnamed x274, local copies, waits for them, and re-layouts  55.2 us
    reduce_scatter x3, waiting for transfers between devices, scattered(): return lax.psum_scatter(part, 'ctx', scatter_dimension=0, tiled=True)  27.7 us
  transfers between devices with their start and end apart: 81, of which 37 were waited for; matrix products, arithmetic and copies ran while one was open for 1% of the time, Pallas kernels for 26%

profile of v2, /device:TPU:0, one launch (start us, length us, event | category | flops | bytes accessed | tf_op | source)
XLA Modules:
  0.0 661.4 jit_solution(10981683137639033879)
XLA Ops:
  45.7 7.6 %collective-permute-done.1.refs_3_.refs_4_ = bf16[2,256,384]{2,1,0:T(8,128)(2,1)S(1)} collective-permute-done((bf16[2,256,384]{2,1,0:T(8,128)(2,1)S(1)}, bf16[2,256,384]{2,1,0:T(8,128)(2,1)S(1)}, u32[]{:S(2)}, u32[]{:S(2)}) %collective-permute-start.1) | collective-permute-done | bytes 393248 | tf_op jit(solution)/shard_map/ppermute | solution.py:334
  62.9 24.2 %collective-permute-done.5.refs_3_.refs_4_ = bf16[2,256,384]{2,1,0:T(8,128)(2,1)S(1)} collective-permute-done((bf16[2,256,384]{2,1,0:T(8,128)(2,1)S(1)}, bf16[2,256,384]{2,1,0:T(8,128)(2,1)S(1)}, u32[]{:S(2)}, u32[]{:S(2)}) %collective-permute-start.5) | collective-permute-done | bytes 393248 | tf_op jit(solution)/shard_map/ppermute | solution.py:334
  87.2 7.6 %collective-permute-start.8 = (bf16[2,256,128]{2,1,0:T(8,128)(2,1)S(1)}, bf16[2,256,128]{2,1,0:T(8,128)(2,1)S(1)}, u32[]{:S(2)}, u32[]{:S(2)}) collective-permute-start(bf16[2,256,128]{2,1,0:T(8,128)(2,1)S(1)} %get-tuple-element.228), channel_id=1, source_target_pairs={{0,8},{4,12},{8,0},{12,4},{16,24},{20,28},{24,16},{28,20},{1,9},{5... | collective-permute-start | bytes 393224 | tf_op jit(solution)/shard_map/ppermute | solution.py:334
  115.6 11.0 %collective-permute-done.12.refs_2_ = bf16[2,64,2048]{2,1,0:T(8,128)(2,1)S(1)} collective-permute-done((bf16[2,64,2048]{2,1,0:T(8,128)(2,1)S(1)}, bf16[2,64,2048]{2,1,0:T(8,128)(2,1)S(1)}, u32[]{:S(2)}, u32[]{:S(2)}) %collective-permute-start.12) | collective-permute-done | bytes 524320 | tf_op jit(solution)/shard_map/ppermute | solution.py:334
  154.0 15.5 %collective-permute-done.20.refs_2_.refs_3_ = bf16[64,2048]{1,0:T(8,128)(2,1)S(1)} collective-permute-done((bf16[64,2048]{1,0:T(8,128)(2,1)S(1)}, bf16[64,2048]{1,0:T(8,128)(2,1)S(1)}, u32[]{:S(2)}, u32[]{:S(2)}) %collective-permute-start.20) | collective-permute-done | bytes 262176 | tf_op jit(solution)/shard_map/ppermute | solution.py:334
  177.2 12.0 %collective-permute-done.24.refs_3_ = bf16[64,2048]{1,0:T(8,128)(2,1)S(1)} collective-permute-done((bf16[64,2048]{1,0:T(8,128)(2,1)S(1)}, bf16[64,2048]{1,0:T(8,128)(2,1)S(1)}, u32[]{:S(2)}, u32[]{:S(2)}) %collective-permute-start.24) | collective-permute-done | bytes 262176 | tf_op jit(solution)/shard_map/ppermute | solution.py:334
  195.5 28.0 %feed_forward.2 = (bf16[512,2048]{1,0:T(8,128)(2,1)}, bf16[512,2048]{1,0:T(8,128)(2,1)}, bf16[512,2048]{1,0:T(8,128)(2,1)}, f32[1,2048]{1,0:T(1,128)S(1)}, f32[1...) custom-call(f32[8,128]{1,0:T(8,128)S(1)} %get-tuple-element.261.refs, ...), custom_call_target="tpu_custom_call" | custom-call | flops 17179869184 | bytes 37748736 | tf_op jit(solution)/shard_map/feed_forward/pallas_call | solution.py:361
  229.0 27.3 %feed_forward.3 = (bf16[512,2048]{1,0:T(8,128)(2,1)}, bf16[512,2048]{1,0:T(8,128)(2,1)}, bf16[512,2048]{1,0:T(8,128)(2,1)}, f32[1,2048]{1,0:T(1,128)S(1)}, f32[1...) custom-call(f32[8,128]{1,0:T(8,128)S(1)} %get-tuple-element.264.refs, ...), custom_call_target="tpu_custom_call", output_to_operand_aliasing={{5}: (10, {}), {6}: (11, {}), {7}: (12, {}), {8}: (13, {})} | custom-call | flops 17179869184 | bytes 37748736 | tf_op jit(solution)/shard_map/feed_forward/pallas_call | solution.py:361
  263.3 13.5 %weight_grad.3 = (bf16[2048,2048]{1,0:T(8,128)(2,1)}, f32[8,128]{1,0:T(8,128)S(1)}) custom-call(f32[8,128]{1,0:T(8,128)S(1)} %get-tuple-element.276.refs_0_, bf16[2,512,2048]{2,1,0:T(8,128)(2,1)} %bitcast.85, bf16[2,512,2048]{2,1,0:T(8,128)(2,1)} %bitcast.86, bf16[512,2048]{1,0:T(8,128)(2,1)} %get-tuple-element.277.refs_3_, ...), custom_call_target="tpu_custom_call" | custom-call | flops 8589934592 | bytes 16777216 | tf_op jit(solution)/shard_map/weight_grad/pallas_call | solution.py:361
  284.7 14.0 %weight_grad.4 = (bf16[2048,2048]{1,0:T(8,128)(2,1)}, f32[8,128]{1,0:T(8,128)S(1)}) custom-call(f32[8,128]{1,0:T(8,128)S(1)} %get-tuple-element.282.refs_0_, bf16[512,2048]{1,0:T(8,128)(2,1)} %get-tuple-element.283.refs_1_, bf16[512,2048]{1,0:T(8,128)(2,1)} %get-tuple-element.284.refs_2_, bf16[512,2048]{1,0:T(8,128)(2,1)} %get-tuple-element.285.refs_3_, ...), custom_call_target="tpu_custom_call" | custom-call | flops 8589934592 | bytes 16777216 | tf_op jit(solution)/shard_map/weight_grad/pallas_call | solution.py:361
  298.8 13.7 %collective-permute-done.36.refs_5_ = bf16[2,64,2048]{2,1,0:T(8,128)(2,1)S(1)} collective-permute-done((bf16[2,64,2048]{2,1,0:T(8,128)(2,1)}, bf16[2,64,2048]{2,1,0:T(8,128)(2,1)S(1)}, u32[]{:S(2)}, u32[]{:S(2)}) %collective-permute-start.36) | collective-permute-done | bytes 524320 | tf_op jit(solution)/shard_map/ppermute | solution.py:334
  357.8 6.7 %collective-permute-start.49 = (bf16[2,256,128]{2,1,0:T(8,128)(2,1)S(1)}, bf16[2,256,128]{2,1,0:T(8,128)(2,1)S(1)}, u32[]{:S(2)}, u32[]{:S(2)}) collective-permute-start(bf16[2,256,128]{2,1,0:T(8,128)(2,1)S(1)} %get-tuple-element.313), channel_id=1, source_target_pairs={{0,8},{4,12},{8,0},{12,4},{16,24},{20,28},{24,16},{28,20},{1,9},{5... | collective-permute-start | bytes 393224 | tf_op jit(solution)/shard_map/ppermute | solution.py:334
  366.9 10.3 %attention_back.2 = (bf16[2,256,384]{2,1,0:T(8,128)(2,1)S(1)}, bf16[2,256,384]{2,1,0:T(8,128)(2,1)S(1)}, bf16[2,2,256,384]{3,2,1,0:T(8,128)(2,1)S(1)}, bf16[2,2,...) custom-call(f32[8,128]{1,0:T(8,128)S(1)} %get-tuple-element.307.refs_0_, ...), custom_call_target="tpu_custom_call" | custom-call | flops 2684354560 | bytes 3145728 | tf_op jit(solution)/shard_map/attention_back/pallas_call | solution.py:361
  386.1 10.9 %attention_back.3 = (bf16[2,256,384]{2,1,0:T(8,128)(2,1)}, bf16[2,256,384]{2,1,0:T(8,128)(2,1)}, bf16[2,2,256,384]{3,2,1,0:T(8,128)(2,1)}, bf16[2,2,256,384]{3,2...) custom-call(f32[8,128]{1,0:T(8,128)S(1)} %get-tuple-element.325.refs, ...), custom_call_target="tpu_custom_call", output_to_operand_aliasing={{0}: (15, {}), {1}: (16, {}), {2}: (17, {}), {3}: (18, {}),... | custom-call | flops 2684354560 | bytes 3145728 | tf_op jit(solution)/shard_map/attention_back/pallas_call | solution.py:361
  405.4 10.9 %collective-permute-done.55.refs_3_ = bf16[2,64,2048]{2,1,0:T(8,128)(2,1)S(1)} collective-permute-done((bf16[2,64,2048]{2,1,0:T(8,128)(2,1)S(1)}, bf16[2,64,2048]{2,1,0:T(8,128)(2,1)S(1)}, u32[]{:S(2)}, u32[]{:S(2)}) %collective-permute-start.55) | collective-permute-done | bytes 524320 | tf_op jit(solution)/shard_map/ppermute | solution.py:334
  419.0 14.2 %collective-permute-done.57.refs_2_.refs_4_ = bf16[2,2,256,384]{3,2,1,0:T(8,128)(2,1)S(1)} collective-permute-done((bf16[2,2,256,384]{3,2,1,0:T(8,128)(2,1)}, bf16[2,2,256,384]{3,2,1,0:T(8,128)(2,1)S(1)}, u32[]{:S(2)}, u32[]{:S(2)}) %collective-permute-start.57) | collective-permute-done | bytes 786464 | tf_op jit(solution)/shard_map/ppermute | solution.py:334
  433.2 22.5 %collective-permute-done.58.refs_3_.refs_5_ = bf16[2,2,256,384]{3,2,1,0:T(8,128)(2,1)S(1)} collective-permute-done((bf16[2,2,256,384]{3,2,1,0:T(8,128)(2,1)}, bf16[2,2,256,384]{3,2,1,0:T(8,128)(2,1)S(1)}, u32[]{:S(2)}, u32[]{:S(2)}) %collective-permute-start.58) | collective-permute-done | bytes 786464 | tf_op jit(solution)/shard_map/ppermute | solution.py:334
  468.6 7.7 %project_back.1 = (bf16[512,1536]{1,0:T(8,128)(2,1)S(1)}, bf16[512,1536]{1,0:T(8,128)(2,1)S(1)}, f32[1,1536]{1,0:T(1,128)S(1)}, bf16[2,2,64,2048]{3,2,1,0:T(8,12...) custom-call(f32[8,128]{1,0:T(8,128)S(1)} %get-tuple-element.342.refs, ...), custom_call_target="tpu_custom_call" | custom-call | flops 6442450944 | bytes 17963008 | tf_op jit(solution)/shard_map/project_back/pallas_call | solution.py:361
  478.7 14.6 %weight_grad.5 = (bf16[2048,2048]{1,0:T(8,128)(2,1)}, f32[8,128]{1,0:T(8,128)S(1)}) custom-call(f32[8,128]{1,0:T(8,128)S(1)} %get-tuple-element.345.refs_0_, bf16[512,2048]{1,0:T(8,128)(2,1)} %copy-done.114, bf16[512,2048]{1,0:T(8,128)(2,1)} %copy-done.113, bf16[512,1536]{1,0:T(8,128)(2,1)} %copy-done.125, bf16[512,1536]{1,0:T(8,128)(2,1)} %copy-done.126, ...), custom_call_target="tpu_custom_call" | custom-call | flops 8589934592 | bytes 20971520 | tf_op jit(solution)/shard_map/weight_grad/pallas_call | solution.py:361
  500.3 22.8 %collective-permute-done.63.refs_2_ = bf16[2,2,64,2048]{3,2,1,0:T(8,128)(2,1)S(1)} collective-permute-done((bf16[2,2,64,2048]{3,2,1,0:T(8,128)(2,1)}, bf16[2,2,64,2048]{3,2,1,0:T(8,128)(2,1)S(1)}, u32[]{:S(2)}, u32[]{:S(2)}) %collective-permute-start.63) | collective-permute-done | bytes 1048608 | tf_op jit(solution)/shard_map/ppermute | solution.py:334
  529.7 10.7 %collective-permute-done.65.refs_3_ = bf16[2,64,2048]{2,1,0:T(8,128)(2,1)} collective-permute-done((bf16[2,64,2048]{2,1,0:T(8,128)(2,1)}, bf16[2,64,2048]{2,1,0:T(8,128)(2,1)}, u32[]{:S(2)}, u32[]{:S(2)}) %collective-permute-start.65) | collective-permute-done | bytes 524320 | tf_op jit(solution)/shard_map/ppermute | solution.py:334
  551.8 15.7 %collective-permute-start.73 = (f32[4,8,256]{2,1,0:T(8,128)S(1)}, f32[4,8,256]{2,1,0:T(8,128)S(1)}, u32[]{:S(2)}, u32[]{:S(2)}) collective-permute-start(f32[4,8,256]{2,1,0:T(8,128)S(1)} %dynamic-slice_bitcast_fusion.4), channel_id=1, source_target_pairs={{0,16},{4,20},{8,24},{12,28},{16,0},{20,4},{24,8},{28,12},{1,17},{... | collective-permute-start | bytes 98312 | tf_op jit(solution)/shard_map/ppermute | solution.py:334
  586.6 23.0 %collective-permute-done.76 = f32[4,256]{1,0:T(4,128)S(1)} collective-permute-done((f32[4,256]{1,0:T(4,128)S(1)}, f32[4,256]{1,0:T(4,128)S(1)}, u32[]{:S(2)}, u32[]{:S(2)}) %collective-permute-start.76) | collective-permute-done | bytes 4128 | tf_op jit(solution)/shard_map/ppermute | solution.py:334
  624.0 27.6 %reduce-scatter.8.cloned.1.call-done.refs_1_ = bf16[256,2048]{1,0:T(8,128)(2,1)} async-done(((bf16[2048,2048]{1,0:T(8,128)(2,1)}), bf16[256,2048]{1,0:T(8,128)(2,1)}) %reduce-scatter.8.cloned.1.call-update) | async-done | bytes 1048592 | tf_op jit(solution)/shard_map/reduce_scatter | solution.py:1371
  (489 shorter events, 273.7 us)
Async XLA Ops:
  7.2 611.3 %reduce-scatter.4.cloned.1.call-start = ((), (), s32[]{:S(2)}) async-start(), calls=%async_computation.3 | async-start | bytes 9437184 | tf_op jit(solution)/shard_map/reduce_scatter | solution.py:1371
  32.2 30.7 %collective-permute-start.4 = (bf16[2,256,384]{2,1,0:T(8,128)(2,1)S(1)}, bf16[2,256,384]{2,1,0:T(8,128)(2,1)S(1)}, u32[]{:S(2)}, u32[]{:S(2)}) collective-permute-start(bf16[2,256,384]{2,1,0:T(8,128)(2,1)S(1)} %get-tuple-element.220), channel_id=1, source_target_pairs={{0,8},{4,12},{8,0},{12,4},{16,24},{20,28},{24,16},{28,20},{1,9},{5... | collective-permute-start | bytes 1179656 | tf_op jit(solution)/shard_map/ppermute | solution.py:334
  33.1 53.9 %collective-permute-start.5 = (bf16[2,256,384]{2,1,0:T(8,128)(2,1)S(1)}, bf16[2,256,384]{2,1,0:T(8,128)(2,1)S(1)}, u32[]{:S(2)}, u32[]{:S(2)}) collective-permute-start(bf16[2,256,384]{2,1,0:T(8,128)(2,1)S(1)} %get-tuple-element.221), channel_id=1, source_target_pairs={{0,16},{4,20},{8,24},{12,28},{16,0},{20,4},{24,8},{28,12},{1,17},{... | collective-permute-start | bytes 1179656 | tf_op jit(solution)/shard_map/ppermute | solution.py:334
  41.1 45.9 %collective-permute-start.6 = (bf16[2,256,384]{2,1,0:T(8,128)(2,1)S(1)}, bf16[2,256,384]{2,1,0:T(8,128)(2,1)S(1)}, u32[]{:S(2)}, u32[]{:S(2)}) collective-permute-start(bf16[2,256,384]{2,1,0:T(8,128)(2,1)S(1)} %get-tuple-element.222), channel_id=1, source_target_pairs={{0,24},{4,28},{8,16},{12,20},{16,8},{20,12},{24,0},{28,4},{1,25},{... | collective-permute-start | bytes 1179656 | tf_op jit(solution)/shard_map/ppermute | solution.py:334
  191.1 35.6 %collective-permute-start.30 = (bf16[128,2048]{1,0:T(8,128)(2,1)S(1)}, bf16[128,2048]{1,0:T(8,128)(2,1)S(1)}, u32[]{:S(2)}, u32[]{:S(2)}) collective-permute-start(bf16[128,2048]{1,0:T(8,128)(2,1)S(1)} %get-tuple-element.265.refs_2_), channel_id=1, source_target_pairs={{0,3},{1,2},{2,1},{3,0},{4,7},{5,6},{6,5},{7,4},{8,11},{9,10},{10,... | collective-permute-start | bytes 1572872 | tf_op jit(solution)/shard_map/ppermute | solution.py:334
  192.7 35.4 %collective-permute-start.29 = (bf16[128,2048]{1,0:T(8,128)(2,1)S(1)}, bf16[128,2048]{1,0:T(8,128)(2,1)S(1)}, u32[]{:S(2)}, u32[]{:S(2)}) collective-permute-start(bf16[128,2048]{1,0:T(8,128)(2,1)S(1)} %get-tuple-element.265.refs_2_), channel_id=1, source_target_pairs={{0,2},{1,3},{2,0},{3,1},{4,6},{5,7},{6,4},{7,5},{8,10},{9,11},{10,... | collective-permute-start | bytes 1572872 | tf_op jit(solution)/shard_map/ppermute | solution.py:334
  193.2 34.9 %collective-permute-start.28 = (bf16[128,2048]{1,0:T(8,128)(2,1)S(1)}, bf16[128,2048]{1,0:T(8,128)(2,1)S(1)}, u32[]{:S(2)}, u32[]{:S(2)}) collective-permute-start(bf16[128,2048]{1,0:T(8,128)(2,1)S(1)} %get-tuple-element.265.refs_2_), channel_id=1, source_target_pairs={{0,1},{1,0},{2,3},{3,2},{4,5},{5,4},{6,7},{7,6},{8,9},{9,8},{10,11... | collective-permute-start | bytes 1572872 | tf_op jit(solution)/shard_map/ppermute | solution.py:334
  224.5 34.2 %collective-permute-start.31 = (bf16[128,2048]{1,0:T(8,128)(2,1)S(1)}, bf16[128,2048]{1,0:T(8,128)(2,1)S(1)}, u32[]{:S(2)}, u32[]{:S(2)}) collective-permute-start(bf16[128,2048]{1,0:T(8,128)(2,1)S(1)} %get-tuple-element.272), channel_id=1, source_target_pairs={{0,1},{1,0},{2,3},{3,2},{4,5},{5,4},{6,7},{7,6},{8,9},{9,8},{10,11... | collective-permute-start | bytes 1572872 | tf_op jit(solution)/shard_map/ppermute | solution.py:334
  225.2 33.6 %collective-permute-start.32 = (bf16[128,2048]{1,0:T(8,128)(2,1)S(1)}, bf16[128,2048]{1,0:T(8,128)(2,1)S(1)}, u32[]{:S(2)}, u32[]{:S(2)}) collective-permute-start(bf16[128,2048]{1,0:T(8,128)(2,1)S(1)} %get-tuple-element.273), channel_id=1, source_target_pairs={{0,2},{1,3},{2,0},{3,1},{4,6},{5,7},{6,4},{7,5},{8,10},{9,11},{10,... | collective-permute-start | bytes 1572872 | tf_op jit(solution)/shard_map/ppermute | solution.py:334
  226.7 32.0 %collective-permute-start.33 = (bf16[128,2048]{1,0:T(8,128)(2,1)S(1)}, bf16[128,2048]{1,0:T(8,128)(2,1)S(1)}, u32[]{:S(2)}, u32[]{:S(2)}) collective-permute-start(bf16[128,2048]{1,0:T(8,128)(2,1)S(1)} %get-tuple-element.274), channel_id=1, source_target_pairs={{0,3},{1,2},{2,1},{3,0},{4,7},{5,6},{6,5},{7,4},{8,11},{9,10},{10,... | collective-permute-start | bytes 1572872 | tf_op jit(solution)/shard_map/ppermute | solution.py:334
  279.2 342.1 %reduce-scatter.6.cloned.1.call-start = ((), (), s32[]{:S(2)}) async-start(), calls=%async_computation.4 | async-start | bytes 9437184 | tf_op jit(solution)/shard_map/reduce_scatter | solution.py:1371
  279.3 36.4 %collective-permute-start.38 = (bf16[128,2048]{1,0:T(8,128)(2,1)}, bf16[128,2048]{1,0:T(8,128)(2,1)S(1)}, u32[]{:S(2)}, u32[]{:S(2)}) collective-permute-start(bf16[128,2048]{1,0:T(8,128)(2,1)} %copy-done.101), channel_id=1, source_target_pairs={{0,1},{1,0},{2,3},{3,2},{4,5},{5,4},{6,7},{7,6},{8,9},{9,8},{10,11... | collective-permute-start | bytes 1572872 | tf_op jit(solution)/shard_map/ppermute | solution.py:334
  280.7 34.9 %collective-permute-start.39 = (bf16[128,2048]{1,0:T(8,128)(2,1)}, bf16[128,2048]{1,0:T(8,128)(2,1)S(1)}, u32[]{:S(2)}, u32[]{:S(2)}) collective-permute-start(bf16[128,2048]{1,0:T(8,128)(2,1)} %copy-done.100), channel_id=1, source_target_pairs={{0,2},{1,3},{2,0},{3,1},{4,6},{5,7},{6,4},{7,5},{8,10},{9,11},{10,... | collective-permute-start | bytes 1572872 | tf_op jit(solution)/shard_map/ppermute | solution.py:334
  281.2 34.5 %collective-permute-start.40 = (bf16[128,2048]{1,0:T(8,128)(2,1)}, bf16[128,2048]{1,0:T(8,128)(2,1)S(1)}, u32[]{:S(2)}, u32[]{:S(2)}) collective-permute-start(bf16[128,2048]{1,0:T(8,128)(2,1)} %copy-done.99), channel_id=1, source_target_pairs={{0,3},{1,2},{2,1},{3,0},{4,7},{5,6},{6,5},{7,4},{8,11},{9,10},{10,... | collective-permute-start | bytes 1572872 | tf_op jit(solution)/shard_map/ppermute | solution.py:334
  397.0 36.2 %collective-permute-start.57 = (bf16[2,2,256,384]{3,2,1,0:T(8,128)(2,1)}, bf16[2,2,256,384]{3,2,1,0:T(8,128)(2,1)S(1)}, u32[]{:S(2)}, u32[]{:S(2)}) collective-permute-start(bf16[2,2,256,384]{3,2,1,0:T(8,128)(2,1)} %get-tuple-element.339), channel_id=1, source_target_pairs={{0,8},{4,12},{8,0},{12,4},{16,24},{20,28},{24,16},{28,20},{1,9},{5... | collective-permute-start | bytes 2359304 | tf_op jit(solution)/shard_map/ppermute | solution.py:334
  400.4 55.2 %collective-permute-start.58 = (bf16[2,2,256,384]{3,2,1,0:T(8,128)(2,1)}, bf16[2,2,256,384]{3,2,1,0:T(8,128)(2,1)S(1)}, u32[]{:S(2)}, u32[]{:S(2)}) collective-permute-start(bf16[2,2,256,384]{3,2,1,0:T(8,128)(2,1)} %get-tuple-element.340), channel_id=1, source_target_pairs={{0,16},{4,20},{8,24},{12,28},{16,0},{20,4},{24,8},{28,12},{1,17},{... | collective-permute-start | bytes 2359304 | tf_op jit(solution)/shard_map/ppermute | solution.py:334
  400.4 55.2 %collective-permute-start.59 = (bf16[2,2,256,384]{3,2,1,0:T(8,128)(2,1)}, bf16[2,2,256,384]{3,2,1,0:T(8,128)(2,1)S(1)}, u32[]{:S(2)}, u32[]{:S(2)}) collective-permute-start(bf16[2,2,256,384]{3,2,1,0:T(8,128)(2,1)} %get-tuple-element.341), channel_id=1, source_target_pairs={{0,24},{4,28},{8,16},{12,20},{16,8},{20,12},{24,0},{28,4},{1,25},{... | collective-permute-start | bytes 2359304 | tf_op jit(solution)/shard_map/ppermute | solution.py:334
  457.7 194.0 %reduce-scatter.8.cloned.1.call-start = ((), (), s32[]{:S(2)}) async-start(), calls=%async_computation.5 | async-start | bytes 9437184 | tf_op jit(solution)/shard_map/reduce_scatter | solution.py:1371
  458.1 35.2 %collective-permute-start.61 = (bf16[2,64,2048]{2,1,0:T(8,128)(2,1)}, bf16[2,64,2048]{2,1,0:T(8,128)(2,1)S(1)}, u32[]{:S(2)}, u32[]{:S(2)}) collective-permute-start(bf16[2,64,2048]{2,1,0:T(8,128)(2,1)} %get-tuple-element.355.refs_1_.refs_2_), channel_id=1, source_target_pairs={{0,1},{1,0},{2,3},{3,2},{4,5},{5,4},{6,7},{7,6},{8,9},{9,8},{10,11... | collective-permute-start | bytes 1572872 | tf_op jit(solution)/shard_map/ppermute | solution.py:334
  459.2 34.1 %collective-permute-start.62 = (bf16[2,64,2048]{2,1,0:T(8,128)(2,1)}, bf16[2,64,2048]{2,1,0:T(8,128)(2,1)S(1)}, u32[]{:S(2)}, u32[]{:S(2)}) collective-permute-start(bf16[2,64,2048]{2,1,0:T(8,128)(2,1)} %get-tuple-element.356.refs_3_.refs_5_), channel_id=1, source_target_pairs={{0,2},{1,3},{2,0},{3,1},{4,6},{5,7},{6,4},{7,5},{8,10},{9,11},{10,... | collective-permute-start | bytes 1572872 | tf_op jit(solution)/shard_map/ppermute | solution.py:334
  527.8 48.1 %collective-permute-start.67 = (bf16[2,2,64,2048]{3,2,1,0:T(8,128)(2,1)}, bf16[2,2,64,2048]{3,2,1,0:T(8,128)(2,1)}, u32[]{:S(2)}, u32[]{:S(2)}) collective-permute-start(bf16[2,2,64,2048]{3,2,1,0:T(8,128)(2,1)} %copy-done.89), channel_id=1, source_target_pairs={{0,2},{1,3},{2,0},{3,1},{4,6},{5,7},{6,4},{7,5},{8,10},{9,11},{10,... | collective-permute-start | bytes 3145736 | tf_op jit(solution)/shard_map/ppermute | solution.py:334
  528.3 47.6 %collective-permute-start.68 = (bf16[2,2,64,2048]{3,2,1,0:T(8,128)(2,1)}, bf16[2,2,64,2048]{3,2,1,0:T(8,128)(2,1)}, u32[]{:S(2)}, u32[]{:S(2)}) collective-permute-start(bf16[2,2,64,2048]{3,2,1,0:T(8,128)(2,1)} %copy-done.88), channel_id=1, source_target_pairs={{0,1},{1,0},{2,3},{3,2},{4,5},{5,4},{6,7},{7,6},{8,9},{9,8},{10,11... | collective-permute-start | bytes 3145736 | tf_op jit(solution)/shard_map/ppermute | solution.py:334
  583.1 30.6 %collective-permute-start.71 = (bf16[2,2,64,2048]{3,2,1,0:T(8,128)(2,1)}, bf16[2,2,64,2048]{3,2,1,0:T(8,128)(2,1)S(1)}, u32[]{:S(2)}, u32[]{:S(2)}) collective-permute-start(bf16[2,2,64,2048]{3,2,1,0:T(8,128)(2,1)} %get-tuple-element.375), channel_id=1, source_target_pairs={{0,2},{1,3},{2,0},{3,1},{4,6},{5,7},{6,4},{7,5},{8,10},{9,11},{10,... | collective-permute-start | bytes 3145736 | tf_op jit(solution)/shard_map/ppermute | solution.py:334
  583.9 29.9 %collective-permute-start.72 = (bf16[2,2,64,2048]{3,2,1,0:T(8,128)(2,1)}, bf16[2,2,64,2048]{3,2,1,0:T(8,128)(2,1)}, u32[]{:S(2)}, u32[]{:S(2)}) collective-permute-start(bf16[2,2,64,2048]{3,2,1,0:T(8,128)(2,1)} %get-tuple-element.376), channel_id=1, source_target_pairs={{0,1},{1,0},{2,3},{3,2},{4,5},{5,4},{6,7},{7,6},{8,9},{9,8},{10,11... | collective-permute-start | bytes 3145736 | tf_op jit(solution)/shard_map/ppermute | solution.py:334
  (194 other events, 2185.6 us)
Sparse Core Ops, SparseCore 0:
  279.4 106.0 reduce-scatter.3
  457.8 102.9 reduce-scatter.5
  563.1 88.5 reduce-scatter.7

commit v3 on v2

--- a/solution.py
+++ b/solution.py
@@ -350,26 +350,42 @@
 
 
 def launch(
-    body, args, in_specs, outs, out_specs, scratch, limit, cost, name, after, grid=(), aliases=None
+    body,
+    args,
+    in_specs,
+    outs,
+    out_specs,
+    scratch,
+    limit,
+    cost,
+    name,
+    after,
+    grid=(),
+    aliases=None,
+    scalars=(),
 ):
     first, last = len(after), len(after) + len(args) + len(outs)
 
     def inner(*refs):
-        body(*refs[first:last], *refs[last + 1 :])
+        fixed, refs = refs[: len(scalars)], refs[len(scalars) :]
+        body(*fixed, *refs[first:last], *refs[last + 1 :])
 
     token = pl.BlockSpec(memory_space=HBM)
     *results, done = pl.pallas_call(
         inner,
-        grid=grid,
+        grid_spec=pltpu.PrefetchScalarGridSpec(
+            num_scalar_prefetch=len(scalars),
+            grid=grid,
+            in_specs=[token] * first + list(in_specs),
+            out_specs=(*out_specs, token),
+            scratch_shapes=list(scratch),
+        ),
         out_shape=(*outs, sds((8, 128), F32)),
-        in_specs=[token] * first + list(in_specs),
-        out_specs=(*out_specs, token),
-        scratch_shapes=list(scratch),
         input_output_aliases={first + key: value for key, value in (aliases or {}).items()},
         compiler_params=pltpu.CompilerParams(vmem_limit_bytes=limit),
         cost_estimate=cost,
         name=name,
-    )(*after, *args)
+    )(*scalars, *after, *args)
     return results, (done,)
 
 
@@ -416,7 +432,7 @@
         if arg.dtype == jnp.int32 and math.prod(arg.shape) <= 8:
             specs.append(pl.BlockSpec(memory_space=pltpu.SMEM))
         elif place in in_hbm:
-            specs.append(pl.BlockSpec(memory_space=pl.ANY))
+            specs.append(pl.BlockSpec(memory_space=HBM))
         else:
             specs.append(pl.BlockSpec(memory_space=pltpu.VMEM))
             moved += math.prod(arg.shape) * arg.dtype.itemsize
@@ -443,11 +459,6 @@
 
 def rows_at(start, count):
     return pl.ds(pl.multiple_of(start, count), count)
-
-
-def held_until(items, after):
-    held, _ = lax.optimization_barrier((items, after))
-    return held, after
 
 
 def reduce_first(messages):
@@ -1260,53 +1271,121 @@
     )
 
 
-def weight_grad(groups, step=512, after=()):
+def weight_grad(groups, here=None, after=()):
     count = len(groups[0][0])
     rows, tall = groups[0][0][0].shape
     widths = [rights[0].shape[1] for _, rights in groups]
-    step = min(step, tall)
-
-    def body(*refs):
-        out_ref = refs[-1]
+    total = sum(widths)
+    split = here is not None
+    steps = 8 if split else 4
+    step = tall // steps
+    half = steps // 2
+
+    def block_of(number, *fixed):
+        if not split:
+            return number
+        core = fixed[0][0] & 1
+        mine = number // half
+        return 2 * (number % half) + (core ^ 1 ^ mine)
+
+    def product(refs, store):
         start = 0
         for place, wide in enumerate(widths):
             ours = refs[2 * count * place : 2 * count * (place + 1)]
             value = dot_tn(ours[0][...], ours[count][...])
             for number in range(1, count):
                 value += dot_tn(ours[number][...], ours[count + number][...])
-            out_ref[:, start : start + wide] = value.astype(BF)
+            store(slice(start, start + wide), value.astype(BF))
             start += wide
 
-    in_specs = []
-    args = []
+    def body(*refs):
+        if not split:
+            out_ref = refs[-1]
+
+            def store(place, value):
+                out_ref[:, place] = value
+
+            product(refs, store)
+            return
+        refs, other_ref, own_ref = refs[1:-2], refs[-2], refs[-1]
+        number = pl.program_id(0)
+
+        def into(ref):
+            def store(place, value):
+                ref[0, :, place] = value
+
+            return store
+
+        @pl.when(number < half)
+        def _():
+            product(refs, into(other_ref))
+
+        @pl.when(number >= half)
+        def _():
+            product(refs, into(own_ref))
+
+    args, in_specs = [], []
     for (lefts, rights), wide in zip(groups, widths):
         for item in lefts:
             if isinstance(item, Part):
                 in_specs.append(
-                    pl.BlockSpec((None, rows, step), lambda i, k=item.index: (k, 0, i))
+                    pl.BlockSpec(
+                        (None, rows, step),
+                        lambda i, *fixed, k=item.index: (k, 0, block_of(i, *fixed)),
+                    )
                 )
             else:
-                in_specs.append(pl.BlockSpec((rows, step), lambda i: (0, i)))
-        in_specs += [pl.BlockSpec((rows, wide), lambda i: (0, 0))] * count
+                in_specs.append(
+                    pl.BlockSpec((rows, step), lambda i, *fixed: (0, block_of(i, *fixed)))
+                )
+        in_specs += [pl.BlockSpec((rows, wide), lambda *_: (0, 0))] * count
         args += list(lefts) + list(rights)
-    total = sum(widths)
-    results, done = launch(
+    if split:
+        outs = [HBM((half, step, total), BF)] * 2
+        out_specs = [
+            pl.BlockSpec((1, step, total), lambda i, *_: (jnp.minimum(i, half - 1), 0, 0)),
+            pl.BlockSpec((1, step, total), lambda i, *_: (jnp.maximum(i - half, 0), 0, 0)),
+        ]
+    else:
+        outs = [HBM((tall, total), BF)]
+        out_specs = [pl.BlockSpec((step, total), lambda i: (i, 0))]
+    return launch(
         body,
         operands_of(args),
         in_specs,
-        [HBM((tall, total), BF)],
-        [pl.BlockSpec((step, total), lambda i: (i, 0))],
+        outs,
+        out_specs,
         (),
-        30 << 20,
+        40 << 20,
         cost(
             2 * count * rows * tall * total,
             2 * (count * rows * (tall * len(groups) + total) + tall * total),
         ),
         "weight_grad",
         after,
-        grid=(tall // step,),
-    )
-    return results[0], done
+        grid=(steps,),
+        scalars=(here,) if split else (),
+    )
+
+
+def add_halves(own, got, after=()):
+    def body(own_ref, got_ref, out_ref):
+        out_ref[...] = (own_ref[...].astype(F32) + got_ref[...].astype(F32)).astype(BF)
+
+    block_spec = pl.BlockSpec((1,) + own.shape[1:], lambda i: (i, 0, 0))
+    return launch(
+        body,
+        operands_of([own, got]),
+        [block_spec] * 2,
+        [HBM(own.shape, BF)],
+        [block_spec],
+        (),
+        16 << 20,
+        cost(0, 6 * math.prod(own.shape)),
+        "add_halves",
+        after,
+        grid=(own.shape[0],),
+    )
 
 
 def small_sums(values):
@@ -1367,8 +1446,20 @@
         lax.dynamic_slice(cot_all, (index, start, 0), (1, size, width))[0] for index in micro
     ]
 
+    chips = [[core + 2 * chip for chip in range(ctx_count // 2)] for core in range(2)]
+
     def scattered(part):
         return lax.psum_scatter(part, "ctx", scatter_dimension=0, tiled=True)
+
+    def scattered_chips(part):
+        part = part.reshape(-1, part.shape[2])
+        return lax.psum_scatter(
+            part, "ctx", scatter_dimension=0, axis_index_groups=chips, tiled=True
+        )
+
+    def until(items, *points):
+        held, _ = lax.optimization_barrier((items, points))
+        return held
 
     norm_one, received, lses, heads_low, resids = [], [], [], [], []
 
@@ -1403,7 +1494,7 @@
 
     norm_two, acts, grad_pres, up_sums, cot_sums = [], [], [], [], []
 
-    def feed_micro(index, pieces, feeds, done):
+    def feed_micro(index, pieces, feeds, direct, done):
         (normed, act, grad_pre, up_sum, cot_sum, *messages), done = feed_forward(
             tp_here,
             pieces,
@@ -1414,7 +1505,7 @@
             feeds,
             index,
             micro_count,
-            True,
+            direct,
             after=done,
         )
         norm_two.append(normed)
@@ -1422,7 +1513,8 @@
         grad_pres.append(grad_pre)
         up_sums.append(up_sum)
         cot_sums.append(cot_sum)
-        return messages[:4], reduce_direct(messages[4:]), done
+        messages, ours = messages[:4], messages[4:]
+        return messages, reduce_direct(ours) if direct else ours, done
 
     grad_resids, gain_twos, shift_twos = [], [], []
     grad_mixes, mix_sums, states = [], [], []
@@ -1468,30 +1560,34 @@
     state_b, done = attend_micro(1, got, done)
     got, done = exchange_cores(state_a, done)
     messages, done = mix_micro(got, False, done)
-    sums_a, done = reduce_second(reduce_first(messages), done)
-    state_a, done = norm_micro(0, sums_a, False, done)
+    state_a = reduce_first(messages)
     got, done = exchange_cores(state_b, done)
     messages, done = mix_micro(got, False, done)
     state_b = reduce_first(messages)
+    sums_a, done = reduce_second(state_a, done)
+    state_a, done = norm_micro(0, sums_a, False, done)
+    sums_b, done = reduce_second(state_b, done)
+    pieces_a, done = gather_second(state_a, done)
+    state_b, done = norm_micro(1, sums_b, True, done)
+    pieces_b = gather_direct(state_b[0])
+    feeds, sums_a, done = feed_micro(0, pieces_a, [], True, done)
+    feeds, messages, done = feed_micro(1, pieces_b, feeds, False, done)
+
+    state_b = reduce_first(messages)
+    state_a, done = norm_back_micro(0, sums_a, done)
+    (down_part,), done = weight_grad([(cots, acts)], after=done)
     pieces_a, done = gather_second(state_a, done)
     sums_b, done = reduce_second(state_b, done)
-    state_b, done = norm_micro(1, sums_b, True, done)
-    pieces_b = gather_direct(state_b[0])
-    feeds, sums_a, done = feed_micro(0, pieces_a, [], done)
-    feeds, sums_b, done = feed_micro(1, pieces_b, feeds, done)
-    state_a, done = norm_back_micro(0, sums_a, done)
-    down_part, done = weight_grad([(cots, acts)], after=done)
-    pieces_a, done = gather_second(state_a, done)
-    (down_part,), done = held_until([down_part], done)
-    down_grad = scattered(down_part)
-    up_part, done = weight_grad([(norm_two, grad_pres)], after=done)
+    down_grad = scattered(until(down_part, done))
+    (sent, own), done = weight_grad([(norm_two, grad_pres)], here, after=done)
     done = heads_back_micro(0, pieces_a, done)
     state_b, done = norm_back_micro(1, sums_b, done)
+    got_up = xor_permute(until(sent, done), "ctx", 1)
+    pieces_b, done = gather_second(state_b, done)
     got_a, done = exchange_cores(states[0], done)
-    pieces_b, done = gather_second(state_b, done)
+    (up_part,), done = add_halves(own, got_up, after=done)
     done = heads_back_micro(1, pieces_b, done)
-    feeds, done = held_until(feeds, done)
-    state_feed = reduce_first(feeds)
+    state_feed = reduce_first(until(feeds, done))
     sent, done = attend_back_micro(0, got_a, [], done)
     got_b, done = exchange_cores(states[1], done)
     sums_feed, done = reduce_second(state_feed, done)
@@ -1500,19 +1596,18 @@
     halves, done = finish_outputs(sums_feed, resids, low_bias, after=done)
     state_out = gather_first(halves)
     got, done = exchange_cores(state_back, done)
-    (up_part,), done = held_until([up_part], done)
-    up_grad = scattered(up_part)
+    up_grad = scattered_chips(until(up_part, done))
     (*grad_projs, proj_sum, first, second, third, fourth), done = project_back(
         here, tp_here, got, weight_three, after=done
     )
     state_one = reduce_first((first, second, third, fourth))
-    last_part, done = weight_grad(
-        [(norm_one, grad_projs), (grad_mixes, heads_low)], after=done
-    )
+    last = [(norm_one, grad_projs), (grad_mixes, heads_low)]
+    (sent, own), done = weight_grad(last, here, after=done)
     pieces_out, done = gather_second(state_out, done)
-    (last_part,), done = held_until([last_part], done)
-    last_grad = scattered(last_part)
+    got_last = xor_permute(until(sent, done), "ctx", 1)
     sums_one, done = reduce_second(state_one, done)
+    (last_part,), done = add_halves(own, got_last, after=done)
+    last_grad = scattered_chips(last_part)
     (gain_sum, shift_sum, *halves), done = first_norm_back(
         sums_one, x_mine, grad_resids, gain_one, after=done
     )

time: 666 us -> 639 us (0.959)
  waiting for transfers between devices: 277 us -> 234 us
  Pallas kernels: 186 us -> 202 us
    reduce_scatter x3 -> x1, waiting for transfers between devices: 27.7 us -> 0.01 us  [scattered(): return lax.psum_scatter(part, 'ctx', scatter_dimension=0, tiled=True)]
    pallas_call x43 -> x46, Pallas kernels: 186 us -> 202 us  [launch(): pl.pallas_call(inner, grid_spec=pltpu.PrefetchScalarGridSpec(num_scalar_p...]
    ppermute x78 -> x81, waiting for transfers between devices: 249 us -> 234 us  [xor_permute(): return lax.ppermute(values, axis, [(i, i ^ step) for i in range(count)])]
    ppermute x78 -> x81, starting transfers between devices: 121 us -> 115 us  [xor_permute(): return lax.ppermute(values, axis, [(i, i ^ step) for i in range(count)])]
    unnamed x274 -> x278, local copies, waits for them, and re-layouts: 55.2 us -> 59.6 us
  transfers between devices with their start and end apart: 81 -> 84, of which waited for: 37 -> 33; matrix products, arithmetic and copies ran while one was open for 1% -> 1% of each run, Pallas kernels for 26% -> 30%
where the time goes in v3:
time: 639 us; the launch traced here: 633 us
  waiting for transfers between devices  234 us (37%)
  Pallas kernels  202 us (32%)
  starting transfers between devices  115 us (18%)
  local copies, waits for them, and re-layouts  66 us (10%)
  between operations  15.5 us (2%)
    ppermute x81, waiting for transfers between devices, xor_permute(): return lax.ppermute(values, axis, [(i, i ^ step) for i in range(count)])  234 us
    pallas_call x46, Pallas kernels, launch(): pl.pallas_call(inner, grid_spec=pltpu.PrefetchScalarGridSpec(num_scalar_p...  202 us
    ppermute x81, starting transfers between devices, xor_permute(): return lax.ppermute(values, axis, [(i, i ^ step) for i in range(count)])  115 us
    unnamed x278, local copies, waits for them, and re-layouts  59.6 us
  transfers between devices with their start and end apart: 84, of which 33 were waited for; matrix products, arithmetic and copies ran while one was open for 1% of the time, Pallas kernels for 30%

profile of v3, /device:TPU:0, one launch (start us, length us, event | category | flops | bytes accessed | tf_op | source)
XLA Modules:
  0.0 633.4 jit_solution(5286067988383901900)
XLA Ops:
  45.7 7.6 %collective-permute-done.1.refs_3_.refs_4_ = bf16[2,256,384]{2,1,0:T(8,128)(2,1)S(1)} collective-permute-done((bf16[2,256,384]{2,1,0:T(8,128)(2,1)S(1)}, bf16[2,256,384]{2,1,0:T(8,128)(2,1)S(1)}, u32[]{:S(2)}, u32[]{:S(2)}) %collective-permute-start.1) | collective-permute-done | bytes 393248 | tf_op jit(solution)/shard_map/ppermute | solution.py:334
  61.9 25.2 %collective-permute-done.5.refs_3_.refs_4_ = bf16[2,256,384]{2,1,0:T(8,128)(2,1)S(1)} collective-permute-done((bf16[2,256,384]{2,1,0:T(8,128)(2,1)S(1)}, bf16[2,256,384]{2,1,0:T(8,128)(2,1)S(1)}, u32[]{:S(2)}, u32[]{:S(2)}) %collective-permute-start.5) | collective-permute-done | bytes 393248 | tf_op jit(solution)/shard_map/ppermute | solution.py:334
  87.2 7.6 %collective-permute-start.8 = (bf16[2,256,128]{2,1,0:T(8,128)(2,1)S(1)}, bf16[2,256,128]{2,1,0:T(8,128)(2,1)S(1)}, u32[]{:S(2)}, u32[]{:S(2)}) collective-permute-start(bf16[2,256,128]{2,1,0:T(8,128)(2,1)S(1)} %get-tuple-element.238), channel_id=1, source_target_pairs={{0,8},{4,12},{8,0},{12,4},{16,24},{20,28},{24,16},{28,20},{1,9},{5... | collective-permute-start | bytes 393224 | tf_op jit(solution)/shard_map/ppermute | solution.py:334
  97.3 6.4 %attention.3 = (bf16[256,128]{1,0:T(8,128)(2,1)S(1)}, bf16[256,128]{1,0:T(8,128)(2,1)S(1)}, bf16[2,256,128]{2,1,0:T(8,128)(2,1)S(1)}, bf16[2,256,128]{2,1,0:T(8,...) custom-call(f32[8,128]{1,0:T(8,128)S(1)} %get-tuple-element.233.refs_0_, ...), custom_call_target="tpu_custom_call" | custom-call | flops 2147483648 | bytes 2727936 | tf_op jit(solution)/shard_map/attention/pallas_call | solution.py:374
  123.0 8.0 %collective-permute-done.13.refs_3_.refs_5_ = bf16[2,256,128]{2,1,0:T(8,128)(2,1)S(1)} collective-permute-done((bf16[2,256,128]{2,1,0:T(8,128)(2,1)}, bf16[2,256,128]{2,1,0:T(8,128)(2,1)S(1)}, u32[]{:S(2)}, u32[]{:S(2)}) %collective-permute-start.13) | collective-permute-done | bytes 131104 | tf_op jit(solution)/shard_map/ppermute | solution.py:334
  169.8 12.4 %collective-permute-done.24.refs_3_ = bf16[64,2048]{1,0:T(8,128)(2,1)S(1)} collective-permute-done((bf16[64,2048]{1,0:T(8,128)(2,1)S(1)}, bf16[64,2048]{1,0:T(8,128)(2,1)S(1)}, u32[]{:S(2)}, u32[]{:S(2)}) %collective-permute-start.24) | collective-permute-done | bytes 262176 | tf_op jit(solution)/shard_map/ppermute | solution.py:334
  190.5 27.7 %feed_forward.2 = (bf16[512,2048]{1,0:T(8,128)(2,1)}, bf16[512,2048]{1,0:T(8,128)(2,1)}, bf16[512,2048]{1,0:T(8,128)(2,1)}, f32[1,2048]{1,0:T(1,128)S(1)}, f32[1...) custom-call(f32[8,128]{1,0:T(8,128)S(1)} %get-tuple-element.271.refs, ...), custom_call_target="tpu_custom_call" | custom-call | flops 17179869184 | bytes 37748736 | tf_op jit(solution)/shard_map/feed_forward/pallas_call | solution.py:374
  223.7 27.3 %feed_forward.3 = (bf16[512,2048]{1,0:T(8,128)(2,1)}, bf16[512,2048]{1,0:T(8,128)(2,1)}, bf16[512,2048]{1,0:T(8,128)(2,1)}, f32[1,2048]{1,0:T(1,128)S(1)}, f32[1...) custom-call(f32[8,128]{1,0:T(8,128)S(1)} %get-tuple-element.274.refs, ...), custom_call_target="tpu_custom_call", output_to_operand_aliasing={{5}: (10, {}), {6}: (11, {}), {7}: (12, {}), {8}: (13, {})} | custom-call | flops 17179869184 | bytes 37748736 | tf_op jit(solution)/shard_map/feed_forward/pallas_call | solution.py:374
  257.5 13.5 %weight_grad.3 = (bf16[2048,2048]{1,0:T(8,128)(2,1)}, f32[8,128]{1,0:T(8,128)S(1)}) custom-call(f32[8,128]{1,0:T(8,128)S(1)} %get-tuple-element.286.refs_0_, bf16[2,512,2048]{2,1,0:T(8,128)(2,1)} %bitcast.89, bf16[2,512,2048]{2,1,0:T(8,128)(2,1)} %bitcast.90, bf16[512,2048]{1,0:T(8,128)(2,1)} %get-tuple-element.287.refs_3_, ...), custom_call_target="tpu_custom_call" | custom-call | flops 8589934592 | bytes 16777216 | tf_op jit(solution)/shard_map/weight_grad/pallas_call | solution.py:374
  279.4 15.2 %weight_grad.4 = (bf16[4,256,2048]{2,1,0:T(8,128)(2,1)}, bf16[4,256,2048]{2,1,0:T(8,128)(2,1)}, f32[8,128]{1,0:T(8,128)S(1)}) custom-call(s32[1]{0:T(128)} %bitcast.refs_0_.refs_1_, f32[8,128]{1,0:T(8,128)S(1)} %get-tuple-element.297.refs_1_, bf16[512,2048]{1,0:T(8,128)(2,1)} %get-tuple-element.298.refs_2_, bf16[512,2048]{1,0:T(8,128)(2,1)} %get-tuple-element.299.refs_3_, ...), custom_call_target="tpu_custom_call" | custom-call | flops 8589934592 | bytes 16777216 | tf_op jit(solution)/shard_map/weight_grad/pallas_call | solution.py:374
  299.6 8.2 %collective-permute-done.42.refs_2_.refs_4_ = bf16[64,2048]{1,0:T(8,128)(2,1)S(1)} collective-permute-done((bf16[64,2048]{1,0:T(8,128)(2,1)S(1)}, bf16[64,2048]{1,0:T(8,128)(2,1)S(1)}, u32[]{:S(2)}, u32[]{:S(2)}) %collective-permute-start.42) | collective-permute-done | bytes 262176 | tf_op jit(solution)/shard_map/ppermute | solution.py:334
  313.4 9.9 %collective-permute-done.44.refs_2_.refs_8_ = bf16[2,256,128]{2,1,0:T(8,128)(2,1)S(1)} collective-permute-done((bf16[2,256,128]{2,1,0:T(8,128)(2,1)S(1)}, bf16[2,256,128]{2,1,0:T(8,128)(2,1)S(1)}, u32[]{:S(2)}, u32[]{:S(2)}) %collective-permute-start.44) | collective-permute-done | bytes 131104 | tf_op jit(solution)/shard_map/ppermute | solution.py:334
  325.0 8.8 %collective-permute-done.46.refs_4_.refs_10_ = bf16[2,256,128]{2,1,0:T(8,128)(2,1)S(1)} collective-permute-done((bf16[2,256,128]{2,1,0:T(8,128)(2,1)S(1)}, bf16[2,256,128]{2,1,0:T(8,128)(2,1)S(1)}, u32[]{:S(2)}, u32[]{:S(2)}) %collective-permute-start.46) | collective-permute-done | bytes 131104 | tf_op jit(solution)/shard_map/ppermute | solution.py:334
  353.2 10.0 %attention_back.2 = (bf16[2,256,384]{2,1,0:T(8,128)(2,1)S(1)}, bf16[2,256,384]{2,1,0:T(8,128)(2,1)S(1)}, bf16[2,2,256,384]{3,2,1,0:T(8,128)(2,1)S(1)}, bf16[2,2,...) custom-call(f32[8,128]{1,0:T(8,128)S(1)} %get-tuple-element.324.refs_0_, ...), custom_call_target="tpu_custom_call" | custom-call | flops 2684354560 | bytes 3145728 | tf_op jit(solution)/shard_map/attention_back/pallas_call | solution.py:374
  373.7 11.2 %attention_back.3 = (bf16[2,256,384]{2,1,0:T(8,128)(2,1)}, bf16[2,256,384]{2,1,0:T(8,128)(2,1)}, bf16[2,2,256,384]{3,2,1,0:T(8,128)(2,1)}, bf16[2,2,256,384]{3,2...) custom-call(f32[8,128]{1,0:T(8,128)S(1)} %get-tuple-element.342.refs, ...), custom_call_target="tpu_custom_call", output_to_operand_aliasing={{0}: (15, {}), {1}: (16, {}), {2}: (17, {}), {3}: (18, {}),... | custom-call | flops 2684354560 | bytes 3145728 | tf_op jit(solution)/shard_map/attention_back/pallas_call | solution.py:374
  393.7 11.3 %collective-permute-done.57.refs_3_ = bf16[2,64,2048]{2,1,0:T(8,128)(2,1)S(1)} collective-permute-done((bf16[2,64,2048]{2,1,0:T(8,128)(2,1)S(1)}, bf16[2,64,2048]{2,1,0:T(8,128)(2,1)S(1)}, u32[]{:S(2)}, u32[]{:S(2)}) %collective-permute-start.57) | collective-permute-done | bytes 524320 | tf_op jit(solution)/shard_map/ppermute | solution.py:334
  406.6 16.6 %collective-permute-done.59.refs_2_.refs_4_ = bf16[2,2,256,384]{3,2,1,0:T(8,128)(2,1)S(1)} collective-permute-done((bf16[2,2,256,384]{3,2,1,0:T(8,128)(2,1)}, bf16[2,2,256,384]{3,2,1,0:T(8,128)(2,1)S(1)}, u32[]{:S(2)}, u32[]{:S(2)}) %collective-permute-start.59) | collective-permute-done | bytes 786464 | tf_op jit(solution)/shard_map/ppermute | solution.py:334
  423.2 20.8 %collective-permute-done.60.refs_3_.refs_5_ = bf16[2,2,256,384]{3,2,1,0:T(8,128)(2,1)S(1)} collective-permute-done((bf16[2,2,256,384]{3,2,1,0:T(8,128)(2,1)}, bf16[2,2,256,384]{3,2,1,0:T(8,128)(2,1)S(1)}, u32[]{:S(2)}, u32[]{:S(2)}) %collective-permute-start.60) | collective-permute-done | bytes 786464 | tf_op jit(solution)/shard_map/ppermute | solution.py:334
  456.5 7.7 %project_back.1 = (bf16[512,1536]{1,0:T(8,128)(2,1)S(1)}, bf16[512,1536]{1,0:T(8,128)(2,1)S(1)}, f32[1,1536]{1,0:T(1,128)S(1)}, bf16[2,2,64,2048]{3,2,1,0:T(8,12...) custom-call(f32[8,128]{1,0:T(8,128)S(1)} %get-tuple-element.359.refs, ...), custom_call_target="tpu_custom_call" | custom-call | flops 6442450944 | bytes 17963008 | tf_op jit(solution)/shard_map/project_back/pallas_call | solution.py:374
  466.6 15.4 %weight_grad.5 = (bf16[4,256,2048]{2,1,0:T(8,128)(2,1)}, bf16[4,256,2048]{2,1,0:T(8,128)(2,1)}, f32[8,128]{1,0:T(8,128)S(1)}) custom-call(s32[1]{0:T(128)} %bitcast.refs_0_.refs_1_, f32[8,128]{1,0:T(8,128)S(1)} %get-tuple-element.362.refs_1_, bf16[512,2048]{1,0:T(8,128)(2,1)} %copy-done.113, bf16[512,2048]{1,0:T(8,128)(2,1)} %copy-done.112, ...), custom_call_target="tpu_custom_call" | custom-call | flops 8589934592 | bytes 20971520 | tf_op jit(solution)/shard_map/weight_grad/pallas_call | solution.py:374
  487.3 22.7 %collective-permute-done.65.refs_2_ = bf16[2,2,64,2048]{3,2,1,0:T(8,128)(2,1)S(1)} collective-permute-done((bf16[2,2,64,2048]{3,2,1,0:T(8,128)(2,1)S(1)}, bf16[2,2,64,2048]{3,2,1,0:T(8,128)(2,1)S(1)}, u32[]{:S(2)}, u32[]{:S(2)}) %collective-permute-start.65) | collective-permute-done | bytes 1048608 | tf_op jit(solution)/shard_map/ppermute | solution.py:334
  525.8 10.7 %collective-permute-done.68.refs_3_ = bf16[2,64,2048]{2,1,0:T(8,128)(2,1)} collective-permute-done((bf16[2,64,2048]{2,1,0:T(8,128)(2,1)}, bf16[2,64,2048]{2,1,0:T(8,128)(2,1)}, u32[]{:S(2)}, u32[]{:S(2)}) %collective-permute-start.68) | collective-permute-done | bytes 524320 | tf_op jit(solution)/shard_map/ppermute | solution.py:334
  547.5 16.8 %collective-permute-start.76 = (f32[4,8,256]{2,1,0:T(8,128)S(1)}, f32[4,8,256]{2,1,0:T(8,128)S(1)}, u32[]{:S(2)}, u32[]{:S(2)}) collective-permute-start(f32[4,8,256]{2,1,0:T(8,128)S(1)} %dynamic-slice_bitcast_fusion.4), channel_id=1, source_target_pairs={{0,16},{4,20},{8,24},{12,28},{16,0},{20,4},{24,8},{28,12},{1,17},{... | collective-permute-start | bytes 98312 | tf_op jit(solution)/shard_map/ppermute | solution.py:334
  586.2 23.2 %collective-permute-done.79 = f32[4,256]{1,0:T(4,128)S(1)} collective-permute-done((f32[4,256]{1,0:T(4,128)S(1)}, f32[4,256]{1,0:T(4,128)S(1)}, u32[]{:S(2)}, u32[]{:S(2)}) %collective-permute-start.79) | collective-permute-done | bytes 4128 | tf_op jit(solution)/shard_map/ppermute | solution.py:334
  (502 shorter events, 273.6 us)
Async XLA Ops:
  7.2 611.2 %reduce-scatter.4.cloned.1.call-start = ((), (), s32[]{:S(2)}) async-start(), calls=%async_computation.3 | async-start | bytes 9437184 | tf_op jit(solution)/shard_map/reduce_scatter | solution.py:1452
  23.5 29.8 %collective-permute-start.1 = (bf16[2,256,384]{2,1,0:T(8,128)(2,1)S(1)}, bf16[2,256,384]{2,1,0:T(8,128)(2,1)S(1)}, u32[]{:S(2)}, u32[]{:S(2)}) collective-permute-start(bf16[2,256,384]{2,1,0:T(8,128)(2,1)S(1)} %get-tuple-element.223), channel_id=1, source_target_pairs={{0,16},{4,20},{8,24},{12,28},{16,0},{20,4},{24,8},{28,12},{1,17},{... | collective-permute-start | bytes 1179656 | tf_op jit(solution)/shard_map/ppermute | solution.py:334
  33.2 53.9 %collective-permute-start.5 = (bf16[2,256,384]{2,1,0:T(8,128)(2,1)S(1)}, bf16[2,256,384]{2,1,0:T(8,128)(2,1)S(1)}, u32[]{:S(2)}, u32[]{:S(2)}) collective-permute-start(bf16[2,256,384]{2,1,0:T(8,128)(2,1)S(1)} %get-tuple-element.231), channel_id=1, source_target_pairs={{0,16},{4,20},{8,24},{12,28},{16,0},{20,4},{24,8},{28,12},{1,17},{... | collective-permute-start | bytes 1179656 | tf_op jit(solution)/shard_map/ppermute | solution.py:334
  41.1 45.9 %collective-permute-start.6 = (bf16[2,256,384]{2,1,0:T(8,128)(2,1)S(1)}, bf16[2,256,384]{2,1,0:T(8,128)(2,1)S(1)}, u32[]{:S(2)}, u32[]{:S(2)}) collective-permute-start(bf16[2,256,384]{2,1,0:T(8,128)(2,1)S(1)} %get-tuple-element.232), channel_id=1, source_target_pairs={{0,24},{4,28},{8,16},{12,20},{16,8},{20,12},{24,0},{28,4},{1,25},{... | collective-permute-start | bytes 1179656 | tf_op jit(solution)/shard_map/ppermute | solution.py:334
  186.1 34.5 %collective-permute-start.30 = (bf16[128,2048]{1,0:T(8,128)(2,1)S(1)}, bf16[128,2048]{1,0:T(8,128)(2,1)S(1)}, u32[]{:S(2)}, u32[]{:S(2)}) collective-permute-start(bf16[128,2048]{1,0:T(8,128)(2,1)S(1)} %get-tuple-element.275.refs_2_), channel_id=1, source_target_pairs={{0,3},{1,2},{2,1},{3,0},{4,7},{5,6},{6,5},{7,4},{8,11},{9,10},{10,... | collective-permute-start | bytes 1572872 | tf_op jit(solution)/shard_map/ppermute | solution.py:334
  186.8 36.0 %collective-permute-start.29 = (bf16[128,2048]{1,0:T(8,128)(2,1)S(1)}, bf16[128,2048]{1,0:T(8,128)(2,1)S(1)}, u32[]{:S(2)}, u32[]{:S(2)}) collective-permute-start(bf16[128,2048]{1,0:T(8,128)(2,1)S(1)} %get-tuple-element.275.refs_2_), channel_id=1, source_target_pairs={{0,2},{1,3},{2,0},{3,1},{4,6},{5,7},{6,4},{7,5},{8,10},{9,11},{10,... | collective-permute-start | bytes 1572872 | tf_op jit(solution)/shard_map/ppermute | solution.py:334
  188.1 34.7 %collective-permute-start.28 = (bf16[128,2048]{1,0:T(8,128)(2,1)S(1)}, bf16[128,2048]{1,0:T(8,128)(2,1)S(1)}, u32[]{:S(2)}, u32[]{:S(2)}) collective-permute-start(bf16[128,2048]{1,0:T(8,128)(2,1)S(1)} %get-tuple-element.275.refs_2_), channel_id=1, source_target_pairs={{0,1},{1,0},{2,3},{3,2},{4,5},{5,4},{6,7},{7,6},{8,9},{9,8},{10,11... | collective-permute-start | bytes 1572872 | tf_op jit(solution)/shard_map/ppermute | solution.py:334
  219.3 33.1 %collective-permute-start.31 = (bf16[128,2048]{1,0:T(8,128)(2,1)S(1)}, bf16[128,2048]{1,0:T(8,128)(2,1)S(1)}, u32[]{:S(2)}, u32[]{:S(2)}) collective-permute-start(bf16[128,2048]{1,0:T(8,128)(2,1)S(1)} %get-tuple-element.282), channel_id=1, source_target_pairs={{0,1},{1,0},{2,3},{3,2},{4,5},{5,4},{6,7},{7,6},{8,9},{9,8},{10,11... | collective-permute-start | bytes 1572872 | tf_op jit(solution)/shard_map/ppermute | solution.py:334
  219.8 32.6 %collective-permute-start.32 = (bf16[128,2048]{1,0:T(8,128)(2,1)S(1)}, bf16[128,2048]{1,0:T(8,128)(2,1)S(1)}, u32[]{:S(2)}, u32[]{:S(2)}) collective-permute-start(bf16[128,2048]{1,0:T(8,128)(2,1)S(1)} %get-tuple-element.283), channel_id=1, source_target_pairs={{0,2},{1,3},{2,0},{3,1},{4,6},{5,7},{6,4},{7,5},{8,10},{9,11},{10,... | collective-permute-start | bytes 1572872 | tf_op jit(solution)/shard_map/ppermute | solution.py:334
  220.6 31.8 %collective-permute-start.33 = (bf16[128,2048]{1,0:T(8,128)(2,1)S(1)}, bf16[128,2048]{1,0:T(8,128)(2,1)S(1)}, u32[]{:S(2)}, u32[]{:S(2)}) collective-permute-start(bf16[128,2048]{1,0:T(8,128)(2,1)S(1)} %get-tuple-element.284), channel_id=1, source_target_pairs={{0,3},{1,2},{2,1},{3,0},{4,7},{5,6},{6,5},{7,4},{8,11},{9,10},{10,... | collective-permute-start | bytes 1572872 | tf_op jit(solution)/shard_map/ppermute | solution.py:334
  275.2 346.1 %reduce-scatter.6.cloned.1.call-start = ((), (), s32[]{:S(2)}) async-start(), calls=%async_computation.4 | async-start | bytes 5242880 | tf_op jit(solution)/shard_map/reduce_scatter | solution.py:1456
  299.1 34.7 %collective-permute-start.47 = (bf16[4,256,2048]{2,1,0:T(8,128)(2,1)S(1)}, bf16[4,256,2048]{2,1,0:T(8,128)(2,1)S(1)}, u32[]{:S(2)}, u32[]{:S(2)}) collective-permute-start(bf16[4,256,2048]{2,1,0:T(8,128)(2,1)S(1)} %copy-done.130), channel_id=1, source_target_pairs={{0,4},{4,0},{8,12},{12,8},{16,20},{20,16},{24,28},{28,24},{1,5},{5... | collective-permute-start | bytes 12582920 | tf_op jit(solution)/shard_map/ppermute | solution.py:334
  307.9 34.4 %collective-permute-start.48 = (bf16[2,64,2048]{2,1,0:T(8,128)(2,1)S(1)}, bf16[2,64,2048]{2,1,0:T(8,128)(2,1)S(1)}, u32[]{:S(2)}, u32[]{:S(2)}) collective-permute-start(bf16[2,64,2048]{2,1,0:T(8,128)(2,1)S(1)} %get-tuple-element.322), channel_id=1, source_target_pairs={{0,2},{1,3},{2,0},{3,1},{4,6},{5,7},{6,4},{7,5},{8,10},{9,11},{10,... | collective-permute-start | bytes 1572872 | tf_op jit(solution)/shard_map/ppermute | solution.py:334
  308.5 33.8 %collective-permute-start.49 = (bf16[2,64,2048]{2,1,0:T(8,128)(2,1)S(1)}, bf16[2,64,2048]{2,1,0:T(8,128)(2,1)S(1)}, u32[]{:S(2)}, u32[]{:S(2)}) collective-permute-start(bf16[2,64,2048]{2,1,0:T(8,128)(2,1)S(1)} %get-tuple-element.323), channel_id=1, source_target_pairs={{0,1},{1,0},{2,3},{3,2},{4,5},{5,4},{6,7},{7,6},{8,9},{9,8},{10,11... | collective-permute-start | bytes 1572872 | tf_op jit(solution)/shard_map/ppermute | solution.py:334
  384.9 38.3 %collective-permute-start.59 = (bf16[2,2,256,384]{3,2,1,0:T(8,128)(2,1)}, bf16[2,2,256,384]{3,2,1,0:T(8,128)(2,1)S(1)}, u32[]{:S(2)}, u32[]{:S(2)}) collective-permute-start(bf16[2,2,256,384]{3,2,1,0:T(8,128)(2,1)} %get-tuple-element.356), channel_id=1, source_target_pairs={{0,8},{4,12},{8,0},{12,4},{16,24},{20,28},{24,16},{28,20},{1,9},{5... | collective-permute-start | bytes 2359304 | tf_op jit(solution)/shard_map/ppermute | solution.py:334
  388.8 55.2 %collective-permute-start.60 = (bf16[2,2,256,384]{3,2,1,0:T(8,128)(2,1)}, bf16[2,2,256,384]{3,2,1,0:T(8,128)(2,1)S(1)}, u32[]{:S(2)}, u32[]{:S(2)}) collective-permute-start(bf16[2,2,256,384]{3,2,1,0:T(8,128)(2,1)} %get-tuple-element.357), channel_id=1, source_target_pairs={{0,16},{4,20},{8,24},{12,28},{16,0},{20,4},{24,8},{28,12},{1,17},{... | collective-permute-start | bytes 2359304 | tf_op jit(solution)/shard_map/ppermute | solution.py:334
  390.2 53.9 %collective-permute-start.61 = (bf16[2,2,256,384]{3,2,1,0:T(8,128)(2,1)}, bf16[2,2,256,384]{3,2,1,0:T(8,128)(2,1)S(1)}, u32[]{:S(2)}, u32[]{:S(2)}) collective-permute-start(bf16[2,2,256,384]{3,2,1,0:T(8,128)(2,1)} %get-tuple-element.358), channel_id=1, source_target_pairs={{0,24},{4,28},{8,16},{12,20},{16,8},{20,12},{24,0},{28,4},{1,25},{... | collective-permute-start | bytes 2359304 | tf_op jit(solution)/shard_map/ppermute | solution.py:334
  445.8 178.1 %reduce-scatter.8.cloned.1.call-start = ((), (), s32[]{:S(2)}) async-start(), calls=%async_computation.5 | async-start | bytes 5242880 | tf_op jit(solution)/shard_map/reduce_scatter | solution.py:1456
  446.0 36.1 %collective-permute-start.63 = (bf16[2,64,2048]{2,1,0:T(8,128)(2,1)}, bf16[2,64,2048]{2,1,0:T(8,128)(2,1)S(1)}, u32[]{:S(2)}, u32[]{:S(2)}) collective-permute-start(bf16[2,64,2048]{2,1,0:T(8,128)(2,1)} %get-tuple-element.372.refs_1_.refs_2_), channel_id=1, source_target_pairs={{0,1},{1,0},{2,3},{3,2},{4,5},{5,4},{6,7},{7,6},{8,9},{9,8},{10,11... | collective-permute-start | bytes 1572872 | tf_op jit(solution)/shard_map/ppermute | solution.py:334
  447.4 34.7 %collective-permute-start.64 = (bf16[2,64,2048]{2,1,0:T(8,128)(2,1)}, bf16[2,64,2048]{2,1,0:T(8,128)(2,1)S(1)}, u32[]{:S(2)}, u32[]{:S(2)}) collective-permute-start(bf16[2,64,2048]{2,1,0:T(8,128)(2,1)} %get-tuple-element.373.refs_3_.refs_5_), channel_id=1, source_target_pairs={{0,2},{1,3},{2,0},{3,1},{4,6},{5,7},{6,4},{7,5},{8,10},{9,11},{10,... | collective-permute-start | bytes 1572872 | tf_op jit(solution)/shard_map/ppermute | solution.py:334
  523.2 53.2 %collective-permute-start.70 = (bf16[2,2,64,2048]{3,2,1,0:T(8,128)(2,1)}, bf16[2,2,64,2048]{3,2,1,0:T(8,128)(2,1)}, u32[]{:S(2)}, u32[]{:S(2)}) collective-permute-start(bf16[2,2,64,2048]{3,2,1,0:T(8,128)(2,1)} %copy-done.91), channel_id=1, source_target_pairs={{0,2},{1,3},{2,0},{3,1},{4,6},{5,7},{6,4},{7,5},{8,10},{9,11},{10,... | collective-permute-start | bytes 3145736 | tf_op jit(solution)/shard_map/ppermute | solution.py:334
  524.1 52.3 %collective-permute-start.71 = (bf16[2,2,64,2048]{3,2,1,0:T(8,128)(2,1)}, bf16[2,2,64,2048]{3,2,1,0:T(8,128)(2,1)}, u32[]{:S(2)}, u32[]{:S(2)}) collective-permute-start(bf16[2,2,64,2048]{3,2,1,0:T(8,128)(2,1)} %copy-done.90), channel_id=1, source_target_pairs={{0,1},{1,0},{2,3},{3,2},{4,5},{5,4},{6,7},{7,6},{8,9},{9,8},{10,11... | collective-permute-start | bytes 3145736 | tf_op jit(solution)/shard_map/ppermute | solution.py:334
  583.6 30.1 %collective-permute-start.74 = (bf16[2,2,64,2048]{3,2,1,0:T(8,128)(2,1)}, bf16[2,2,64,2048]{3,2,1,0:T(8,128)(2,1)S(1)}, u32[]{:S(2)}, u32[]{:S(2)}) collective-permute-start(bf16[2,2,64,2048]{3,2,1,0:T(8,128)(2,1)} %get-tuple-element.396), channel_id=1, source_target_pairs={{0,2},{1,3},{2,0},{3,1},{4,6},{5,7},{6,4},{7,5},{8,10},{9,11},{10,... | collective-permute-start | bytes 3145736 | tf_op jit(solution)/shard_map/ppermute | solution.py:334
  583.6 30.1 %collective-permute-start.75 = (bf16[2,2,64,2048]{3,2,1,0:T(8,128)(2,1)}, bf16[2,2,64,2048]{3,2,1,0:T(8,128)(2,1)}, u32[]{:S(2)}, u32[]{:S(2)}) collective-permute-start(bf16[2,2,64,2048]{3,2,1,0:T(8,128)(2,1)} %get-tuple-element.397), channel_id=1, source_target_pairs={{0,1},{1,0},{2,3},{3,2},{4,5},{5,4},{6,7},{7,6},{8,9},{9,8},{10,11... | collective-permute-start | bytes 3145736 | tf_op jit(solution)/shard_map/ppermute | solution.py:334
  (199 other events, 2465.2 us)
Sparse Core Ops, SparseCore 0:
  275.3 105.4 reduce-scatter.3
  446.0 90.4 reduce-scatter.5
  538.8 78.3 reduce-scatter.7

commit v4 on v3

--- a/solution.py
+++ b/solution.py
@@ -401,28 +401,11 @@
 
 def operands_of(args):
     arrays = [arg.array if isinstance(arg, Part) else arg for arg in args]
-    return [
-        array if array.dtype == jnp.int32 else pltpu.with_memory_space_constraint(array, HBM)
-        for array in arrays
-    ]
-
-
-class Part:
-    def __init__(self, array, index):
-        self.array, self.index = array, index
-        self.shape, self.dtype = array.shape[1:], array.dtype
-
-    def spec(self):
-        index, rest = self.index, (0,) * len(self.shape)
-        return pl.BlockSpec((None,) + self.shape, lambda *_: (index,) + rest)
-
-
-def operands_of(args):
-    arrays = [arg.array if isinstance(arg, Part) else arg for arg in args]
-    return [
-        array if array.dtype == jnp.int32 else pltpu.with_memory_space_constraint(array, HBM)
-        for array in arrays
-    ]
+    return [array if array.dtype == jnp.int32 else pinned(array) for array in arrays]
+
+
+def pinned(array):
+    return pltpu.with_memory_space_constraint(array, HBM)
 
 
 def run_kernel(body, outs, args, flops=0, exps=0, scratch=(), limit=8, name=None, after=(), in_hbm=()):
@@ -441,7 +424,7 @@
     held = moved + sum(math.prod(item.shape) * item.dtype.itemsize for item in kept)
     return launch(
         body,
-        args,
+        [pinned(arg) if place in in_hbm else arg for place, arg in enumerate(args)],
         specs,
         outs,
         [pl.BlockSpec(memory_space=pltpu.VMEM) for _ in outs],
@@ -469,25 +452,26 @@
 
 
 def reduce_second(state, after=()):
-    middle_shape = state[0][0].shape[:-3] + state[0][0].shape[-2:]
+    shape = state[0][0].shape[:-3] + state[0][0].shape[-2:]
 
     def body(*refs):
         for part in range(2):
             keep, got = refs[2 * part : 2 * part + 2]
+            refs[4 + part][...] = keep[..., 0, :, :].astype(F32) + got[..., 0, :, :].astype(F32)
             value = keep[..., 1, :, :].astype(F32) + got[..., 1, :, :].astype(F32)
-            refs[4 + part][...] = value.astype(BF)
-
-    middles, done = run_kernel(
-        body,
-        [sds(middle_shape)] * 2,
+            refs[6 + part][...] = value.astype(BF)
+
+    (*rest, low, high), done = run_kernel(
+        body,
+        [sds(shape, F32)] * 2 + [sds(shape)] * 2,
         [item for pair in state for item in pair],
         after=after,
         name="reduce_middle",
-        limit=3,
+        limit=4,
     )
     sums = []
     for part, (_, second) in enumerate(ORDERS):
-        sums += [*state[part], xor_permute(middles[part], "tp", second)]
+        sums += [rest[part], xor_permute((low, high)[part], "tp", second)]
     return sums, done
 
 
@@ -531,14 +515,9 @@
 
 
 def total_of(refs):
-    if len(refs) == 4:
+    if refs[0].dtype == BF:
         return sum([ref[...].astype(F32) for ref in refs[1:]], refs[0][...].astype(F32))
-    halves = []
-    for part in range(2):
-        keep, got, late = refs[3 * part : 3 * part + 3]
-        halves.append(
-            keep[0].astype(F32) + got[0].astype(F32) + late[...].astype(F32)
-        )
+    halves = [refs[2 * part][...] + refs[2 * part + 1][...].astype(F32) for part in range(2)]
     return jnp.concatenate(halves, axis=0)
 
 
@@ -1078,7 +1057,7 @@
     size, width = grad_resids[0].shape
 
     def body(*rest):
-        refs, rest = rest[:6], rest[6:]
+        refs, rest = rest[:4], rest[4:]
         x_refs, grad_refs, gain_ref = rest[:count], rest[count : 2 * count], rest[2 * count]
         gain_out, shift_out, *outs = rest[2 * count + 1 :]
         for index in range(count):
@@ -1110,8 +1089,8 @@
     count = len(resids)
 
     def body(*rest):
-        refs, resid_refs, bias_ref = rest[:6], rest[6 : 6 + count], rest[6 + count]
-        low_ref, high_ref = rest[7 + count :]
+        refs, resid_refs, bias_ref = rest[:4], rest[4 : 4 + count], rest[4 + count]
+        low_ref, high_ref = rest[5 + count :]
         for index in range(count):
             ours = [ref.at[index] for ref in refs]
             value = (resid_refs[index][...] + total_of(ours) + bias_ref[...]).astype(BF)
@@ -1560,14 +1539,13 @@
     state_b, done = attend_micro(1, got, done)
     got, done = exchange_cores(state_a, done)
     messages, done = mix_micro(got, False, done)
-    state_a = reduce_first(messages)
+    sums_a, done = reduce_second(reduce_first(messages), done)
     got, done = exchange_cores(state_b, done)
     messages, done = mix_micro(got, False, done)
     state_b = reduce_first(messages)
-    sums_a, done = reduce_second(state_a, done)
     state_a, done = norm_micro(0, sums_a, False, done)
+    pieces_a, done = gather_second(state_a, done)
     sums_b, done = reduce_second(state_b, done)
-    pieces_a, done = gather_second(state_a, done)
     state_b, done = norm_micro(1, sums_b, True, done)
     pieces_b = gather_direct(state_b[0])
     feeds, sums_a, done = feed_micro(0, pieces_a, [], True, done)
@@ -1579,23 +1557,24 @@
     pieces_a, done = gather_second(state_a, done)
     sums_b, done = reduce_second(state_b, done)
     down_grad = scattered(until(down_part, done))
-    (sent, own), done = weight_grad([(norm_two, grad_pres)], here, after=done)
     done = heads_back_micro(0, pieces_a, done)
     state_b, done = norm_back_micro(1, sums_b, done)
-    got_up = xor_permute(until(sent, done), "ctx", 1)
     pieces_b, done = gather_second(state_b, done)
+    (sent, own), done = weight_grad([(norm_two, grad_pres)], here, after=done)
     got_a, done = exchange_cores(states[0], done)
-    (up_part,), done = add_halves(own, got_up, after=done)
     done = heads_back_micro(1, pieces_b, done)
     state_feed = reduce_first(until(feeds, done))
-    sent, done = attend_back_micro(0, got_a, [], done)
+    sent_back, done = attend_back_micro(0, got_a, [], done)
     got_b, done = exchange_cores(states[1], done)
     sums_feed, done = reduce_second(state_feed, done)
-    sent, done = attend_back_micro(1, got_b, sent, done)
-    state_back = exchange_chips(*sent)
+    got_up = xor_permute(until(sent, done), "ctx", 1)
+    sent_back, done = attend_back_micro(1, got_b, sent_back, done)
+    state_back = exchange_chips(*sent_back)
     halves, done = finish_outputs(sums_feed, resids, low_bias, after=done)
-    state_out = gather_first(halves)
+    (up_part,), done = add_halves(own, got_up, after=done)
+    pieces_out, done = gather_second(gather_first(halves), done)
     got, done = exchange_cores(state_back, done)
+    outputs, done = assemble_outputs(tp_here, pieces_out, BF, after=done)
     up_grad = scattered_chips(until(up_part, done))
     (*grad_projs, proj_sum, first, second, third, fourth), done = project_back(
         here, tp_here, got, weight_three, after=done
@@ -1603,19 +1582,17 @@
     state_one = reduce_first((first, second, third, fourth))
     last = [(norm_one, grad_projs), (grad_mixes, heads_low)]
     (sent, own), done = weight_grad(last, here, after=done)
-    pieces_out, done = gather_second(state_out, done)
+    sums_one, done = reduce_second(state_one, done)
     got_last = xor_permute(until(sent, done), "ctx", 1)
-    sums_one, done = reduce_second(state_one, done)
     (last_part,), done = add_halves(own, got_last, after=done)
-    last_grad = scattered_chips(last_part)
     (gain_sum, shift_sum, *halves), done = first_norm_back(
         sums_one, x_mine, grad_resids, gain_one, after=done
     )
-    outputs, done = assemble_outputs(tp_here, pieces_out, BF, after=done)
+    last_grad = scattered_chips(until(last_part, done))
+    pieces_in, done = gather_second(gather_first(halves), done)
     gain_ones, shift_ones, proj_sums = [gain_sum], [shift_sum], [proj_sum]
-    pieces_in, done = gather_second(gather_first(halves), done)
+    (down_grad,), done = widen(down_grad, True, after=done)
     input_grad, done = assemble_outputs(tp_here, pieces_in, F32, after=done)
-    (down_grad,), done = widen(down_grad, True, after=done)
     (up_grad,), done = widen(up_grad, False, after=done)
     (proj_grad, mixer_grad), done = widen_last(last_grad, inner, after=done)
     proj_grad = jnp.transpose(proj_grad, (1, 0, 2))

time: 639 us -> 631 us (0.987)
  local copies, waits for them, and re-layouts: 66 us -> 49 us
  waiting for transfers between devices: 234 us -> 245 us
    reduce_scatter x2, waiting for transfers between devices: 0.01 us -> 36 us  [scattered_chips(): lax.psum_scatter(part, 'ctx', scatter_dimension=0, axis_index_groups=chip...]
    ppermute x81, waiting for transfers between devices: 234 us -> 209 us  [xor_permute(): return lax.ppermute(values, axis, [(i, i ^ step) for i in range(count)])]
    unnamed x278 -> x232, local copies, waits for them, and re-layouts: 59.6 us -> 42.6 us
  transfers between devices with their start and end apart: 84 -> 84, of which waited for: 33 -> 34; matrix products, arithmetic and copies ran while one was open for 1% -> 1% of each run, Pallas kernels for 30% -> 30%
where the time goes in v4:
time: 631 us; the launch traced here: 621 us
  waiting for transfers between devices  245 us (39%)
  Pallas kernels  197 us (31%)
  starting transfers between devices  115 us (18%)
  local copies, waits for them, and re-layouts  49 us (8%)
  between operations  15.4 us (2%)
    ppermute x81, waiting for transfers between devices, xor_permute(): return lax.ppermute(values, axis, [(i, i ^ step) for i in range(count)])  209 us
    pallas_call x46, Pallas kernels, launch(): pl.pallas_call(inner, grid_spec=pltpu.PrefetchScalarGridSpec(num_scalar_p...  197 us
    ppermute x81, starting transfers between devices, xor_permute(): return lax.ppermute(values, axis, [(i, i ^ step) for i in range(count)])  114 us
    unnamed x232, local copies, waits for them, and re-layouts  42.6 us
    reduce_scatter x2, waiting for transfers between devices, scattered_chips(): lax.psum_scatter(part, 'ctx', scatter_dimension=0, axis_index_groups=chip...  36 us
  transfers between devices with their start and end apart: 84, of which 34 were waited for; matrix products, arithmetic and copies ran while one was open for 1% of the time, Pallas kernels for 30%

profile of v4, /device:TPU:0, one launch (start us, length us, event | category | flops | bytes accessed | tf_op | source)
XLA Modules:
  0.0 621.2 jit_solution(5844904825907129087)
XLA Ops:
  9.5 6.9 %project.2 = (bf16[512,2048]{1,0:T(8,128)(2,1)S(1)}, bf16[256,384]{1,0:T(8,128)(2,1)S(1)}, bf16[256,384]{1,0:T(8,128)(2,1)S(1)}, bf16[2,256,384]{2,1,0:T(8,128)(...) custom-call(s32[1]{0:T(128)} %bitcast.refs_0_.refs_1_, ...), custom_call_target="tpu_custom_call" | custom-call | flops 3221225472 | bytes 3692544 | tf_op jit(solution)/shard_map/project/pallas_call | solution.py:374
  23.4 6.9 %project.3 = (bf16[512,2048]{1,0:T(8,128)(2,1)S(1)}, bf16[256,384]{1,0:T(8,128)(2,1)S(1)}, bf16[256,384]{1,0:T(8,128)(2,1)S(1)}, bf16[2,256,384]{2,1,0:T(8,128)(...) custom-call(f32[8,128]{1,0:T(8,128)S(1)} %get-tuple-element.230.refs_0_, ...), custom_call_target="tpu_custom_call" | custom-call | flops 3221225472 | bytes 3692544 | tf_op jit(solution)/shard_map/project/pallas_call | solution.py:374
  43.0 7.7 %collective-permute-done.1.refs_3_.refs_4_ = bf16[2,256,384]{2,1,0:T(8,128)(2,1)S(1)} collective-permute-done((bf16[2,256,384]{2,1,0:T(8,128)(2,1)S(1)}, bf16[2,256,384]{2,1,0:T(8,128)(2,1)S(1)}, u32[]{:S(2)}, u32[]{:S(2)}) %collective-permute-start.1) | collective-permute-done | bytes 393248 | tf_op jit(solution)/shard_map/ppermute | solution.py:334
  53.1 6.5 %attention.2 = (bf16[256,128]{1,0:T(8,128)(2,1)S(1)}, bf16[256,128]{1,0:T(8,128)(2,1)S(1)}, bf16[2,256,128]{2,1,0:T(8,128)(2,1)S(1)}, bf16[2,256,128]{2,1,0:T(8,...) custom-call(f32[8,128]{1,0:T(8,128)S(1)} %get-tuple-element.236.refs_0_, ...), custom_call_target="tpu_custom_call" | custom-call | flops 2147483648 | bytes 2727936 | tf_op jit(solution)/shard_map/attention/pallas_call | solution.py:374
  59.6 24.7 %collective-permute-done.5.refs_3_.refs_4_ = bf16[2,256,384]{2,1,0:T(8,128)(2,1)S(1)} collective-permute-done((bf16[2,256,384]{2,1,0:T(8,128)(2,1)S(1)}, bf16[2,256,384]{2,1,0:T(8,128)(2,1)S(1)}, u32[]{:S(2)}, u32[]{:S(2)}) %collective-permute-start.5) | collective-permute-done | bytes 393248 | tf_op jit(solution)/shard_map/ppermute | solution.py:334
  84.6 7.6 %collective-permute-start.8 = (bf16[2,256,128]{2,1,0:T(8,128)(2,1)S(1)}, bf16[2,256,128]{2,1,0:T(8,128)(2,1)S(1)}, u32[]{:S(2)}, u32[]{:S(2)}) collective-permute-start(bf16[2,256,128]{2,1,0:T(8,128)(2,1)S(1)} %get-tuple-element.249), channel_id=1, source_target_pairs={{0,8},{4,12},{8,0},{12,4},{16,24},{20,28},{24,16},{28,20},{1,9},{5... | collective-permute-start | bytes 393224 | tf_op jit(solution)/shard_map/ppermute | solution.py:334
  94.7 6.7 %attention.3 = (bf16[256,128]{1,0:T(8,128)(2,1)S(1)}, bf16[256,128]{1,0:T(8,128)(2,1)S(1)}, bf16[2,256,128]{2,1,0:T(8,128)(2,1)}, bf16[2,256,128]{2,1,0:T(8,128)...) custom-call(f32[8,128]{1,0:T(8,128)S(1)} %get-tuple-element.244.refs_0_, ...), custom_call_target="tpu_custom_call" | custom-call | flops 2147483648 | bytes 2727936 | tf_op jit(solution)/shard_map/attention/pallas_call | solution.py:374
  141.2 13.8 %collective-permute-done.20.refs_2_.refs_3_ = bf16[64,2048]{1,0:T(8,128)(2,1)S(1)} collective-permute-done((bf16[64,2048]{1,0:T(8,128)(2,1)S(1)}, bf16[64,2048]{1,0:T(8,128)(2,1)S(1)}, u32[]{:S(2)}, u32[]{:S(2)}) %collective-permute-start.20) | collective-permute-done | bytes 262176 | tf_op jit(solution)/shard_map/ppermute | solution.py:334
  163.1 11.5 %collective-permute-done.24.refs_2_ = bf16[64,2048]{1,0:T(8,128)(2,1)S(1)} collective-permute-done((bf16[64,2048]{1,0:T(8,128)(2,1)S(1)}, bf16[64,2048]{1,0:T(8,128)(2,1)S(1)}, u32[]{:S(2)}, u32[]{:S(2)}) %collective-permute-start.24) | collective-permute-done | bytes 262176 | tf_op jit(solution)/shard_map/ppermute | solution.py:334
  181.8 27.6 %feed_forward.2 = (bf16[512,2048]{1,0:T(8,128)(2,1)}, bf16[512,2048]{1,0:T(8,128)(2,1)}, bf16[512,2048]{1,0:T(8,128)(2,1)}, f32[1,2048]{1,0:T(1,128)S(1)}, f32[1...) custom-call(f32[8,128]{1,0:T(8,128)S(1)} %get-tuple-element.286.refs, ...), custom_call_target="tpu_custom_call" | custom-call | flops 17179869184 | bytes 37748736 | tf_op jit(solution)/shard_map/feed_forward/pallas_call | solution.py:374
  214.8 27.3 %feed_forward.3 = (bf16[512,2048]{1,0:T(8,128)(2,1)}, bf16[512,2048]{1,0:T(8,128)(2,1)}, bf16[512,2048]{1,0:T(8,128)(2,1)}, f32[1,2048]{1,0:T(1,128)S(1)}, f32[1...) custom-call(f32[8,128]{1,0:T(8,128)S(1)} %get-tuple-element.289.refs, ...), custom_call_target="tpu_custom_call", output_to_operand_aliasing={{5}: (10, {}), {6}: (11, {}), {7}: (12, {}), {8}: (13, {})} | custom-call | flops 17179869184 | bytes 37748736 | tf_op jit(solution)/shard_map/feed_forward/pallas_call | solution.py:374
  248.6 13.4 %weight_grad.3 = (bf16[2048,2048]{1,0:T(8,128)(2,1)}, f32[8,128]{1,0:T(8,128)S(1)}) custom-call(f32[8,128]{1,0:T(8,128)S(1)} %get-tuple-element.301.refs_0_, bf16[2,512,2048]{2,1,0:T(8,128)(2,1)} %bitcast.89, bf16[2,512,2048]{2,1,0:T(8,128)(2,1)} %bitcast.90, bf16[512,2048]{1,0:T(8,128)(2,1)} %get-tuple-element.302.refs_3_, ...), custom_call_target="tpu_custom_call" | custom-call | flops 8589934592 | bytes 16777216 | tf_op jit(solution)/shard_map/weight_grad/pallas_call | solution.py:374
  271.3 7.5 %collective-permute-done.38.refs_5_ = bf16[2,64,2048]{2,1,0:T(8,128)(2,1)S(1)} collective-permute-done((bf16[2,64,2048]{2,1,0:T(8,128)(2,1)}, bf16[2,64,2048]{2,1,0:T(8,128)(2,1)S(1)}, u32[]{:S(2)}, u32[]{:S(2)}) %collective-permute-start.38) | collective-permute-done | bytes 524320 | tf_op jit(solution)/shard_map/ppermute | solution.py:334
  298.9 14.5 %weight_grad.4 = (bf16[4,256,2048]{2,1,0:T(8,128)(2,1)}, bf16[4,256,2048]{2,1,0:T(8,128)(2,1)}, f32[8,128]{1,0:T(8,128)S(1)}) custom-call(s32[1]{0:T(128)} %bitcast.refs_0_.refs_1_, f32[8,128]{1,0:T(8,128)S(1)} %get-tuple-element.324.refs_1_, bf16[512,2048]{1,0:T(8,128)(2,1)} %get-tuple-element.325.refs_2_, bf16[512,2048]{1,0:T(8,128)(2,1)} %get-tuple-element.326.refs_3_, ...), custom_call_target="tpu_custom_call" | custom-call | flops 8589934592 | bytes 16777216 | tf_op jit(solution)/shard_map/weight_grad/pallas_call | solution.py:374
  323.6 10.1 %attention_back.2 = (bf16[2,256,384]{2,1,0:T(8,128)(2,1)S(1)}, bf16[2,256,384]{2,1,0:T(8,128)(2,1)S(1)}, bf16[2,2,256,384]{3,2,1,0:T(8,128)(2,1)S(1)}, bf16[2,2,...) custom-call(f32[8,128]{1,0:T(8,128)S(1)} %get-tuple-element.337.refs_0_, ...), custom_call_target="tpu_custom_call" | custom-call | flops 2684354560 | bytes 3145728 | tf_op jit(solution)/shard_map/attention_back/pallas_call | solution.py:374
  351.0 11.1 %attention_back.3 = (bf16[2,256,384]{2,1,0:T(8,128)(2,1)}, bf16[2,256,384]{2,1,0:T(8,128)(2,1)}, bf16[2,2,256,384]{3,2,1,0:T(8,128)(2,1)}, bf16[2,2,256,384]{3,2...) custom-call(f32[8,128]{1,0:T(8,128)S(1)} %get-tuple-element.355.refs, ...), custom_call_target="tpu_custom_call", output_to_operand_aliasing={{0}: (15, {}), {1}: (16, {}), {2}: (17, {}), {3}: (18, {}),... | custom-call | flops 2684354560 | bytes 3145728 | tf_op jit(solution)/shard_map/attention_back/pallas_call | solution.py:374
  385.8 28.8 %collective-permute-done.61.refs_2_.refs_4_ = bf16[2,2,256,384]{3,2,1,0:T(8,128)(2,1)S(1)} collective-permute-done((bf16[2,2,256,384]{3,2,1,0:T(8,128)(2,1)S(1)}, bf16[2,2,256,384]{3,2,1,0:T(8,128)(2,1)S(1)}, u32[]{:S(2)}, u32[]{:S(2)}) %collective-permute-start.61) | collective-permute-done | bytes 786464 | tf_op jit(solution)/shard_map/ppermute | solution.py:334
  414.6 23.5 %collective-permute-done.62.refs_3_.refs_5_ = bf16[2,2,256,384]{3,2,1,0:T(8,128)(2,1)S(1)} collective-permute-done((bf16[2,2,256,384]{3,2,1,0:T(8,128)(2,1)S(1)}, bf16[2,2,256,384]{3,2,1,0:T(8,128)(2,1)S(1)}, u32[]{:S(2)}, u32[]{:S(2)}) %collective-permute-start.62) | collective-permute-done | bytes 786464 | tf_op jit(solution)/shard_map/ppermute | solution.py:334
  448.6 7.8 %project_back.1 = (bf16[512,1536]{1,0:T(8,128)(2,1)S(1)}, bf16[512,1536]{1,0:T(8,128)(2,1)S(1)}, f32[1,1536]{1,0:T(1,128)S(1)}, bf16[2,2,64,2048]{3,2,1,0:T(8,12...) custom-call(f32[8,128]{1,0:T(8,128)S(1)} %get-tuple-element.385.refs, ...), custom_call_target="tpu_custom_call" | custom-call | flops 6442450944 | bytes 17963008 | tf_op jit(solution)/shard_map/project_back/pallas_call | solution.py:374
  461.3 15.5 %weight_grad.5 = (bf16[4,256,2048]{2,1,0:T(8,128)(2,1)}, bf16[4,256,2048]{2,1,0:T(8,128)(2,1)}, f32[8,128]{1,0:T(8,128)S(1)}) custom-call(s32[1]{0:T(128)} %bitcast.refs_0_.refs_1_, f32[8,128]{1,0:T(8,128)S(1)} %get-tuple-element.388.refs_1_, bf16[512,2048]{1,0:T(8,128)(2,1)} %copy-done.89, bf16[512,2048]{1,0:T(8,128)(2,1)} %copy-done.88, ...), custom_call_target="tpu_custom_call" | custom-call | flops 8589934592 | bytes 20971520 | tf_op jit(solution)/shard_map/weight_grad/pallas_call | solution.py:374
  476.8 7.1 %collective-permute-done.67.refs_2_ = bf16[2,2,64,2048]{3,2,1,0:T(8,128)(2,1)S(1)} collective-permute-done((bf16[2,2,64,2048]{3,2,1,0:T(8,128)(2,1)S(1)}, bf16[2,2,64,2048]{3,2,1,0:T(8,128)(2,1)S(1)}, u32[]{:S(2)}, u32[]{:S(2)}) %collective-permute-start.67) | collective-permute-done | bytes 1048608 | tf_op jit(solution)/shard_map/ppermute | solution.py:334
  503.3 16.8 %collective-permute-start.76 = (f32[4,8,256]{2,1,0:T(8,128)S(1)}, f32[4,8,256]{2,1,0:T(8,128)S(1)}, u32[]{:S(2)}, u32[]{:S(2)}) collective-permute-start(f32[4,8,256]{2,1,0:T(8,128)S(1)} %dynamic-slice_bitcast_fusion.4), channel_id=1, source_target_pairs={{0,16},{4,20},{8,24},{12,28},{16,0},{20,4},{24,8},{28,12},{1,17},{... | collective-permute-start | bytes 98312 | tf_op jit(solution)/shard_map/ppermute | solution.py:334
  540.1 21.1 %collective-permute-done.79 = f32[4,256]{1,0:T(4,128)S(1)} collective-permute-done((f32[4,256]{1,0:T(4,128)S(1)}, f32[4,256]{1,0:T(4,128)S(1)}, u32[]{:S(2)}, u32[]{:S(2)}) %collective-permute-start.79) | collective-permute-done | bytes 4128 | tf_op jit(solution)/shard_map/ppermute | solution.py:334
  575.8 36.0 %reduce-scatter.8.cloned.1.call-done.refs_1_ = bf16[256,2048]{1,0:T(8,128)(2,1)} async-done(((bf16[1024,2048]{1,0:T(8,128)(2,1)}), bf16[256,2048]{1,0:T(8,128)(2,1)}) %reduce-scatter.8.cloned.1.call-update) | async-done | bytes 1048592 | tf_op jit(solution)/shard_map/reduce_scatter | solution.py:1435
  (456 shorter events, 245.4 us)
Async XLA Ops:
  7.2 558.3 %reduce-scatter.4.cloned.1.call-start = ((), (), s32[]{:S(2)}) async-start(), calls=%async_computation.3 | async-start | bytes 9437184 | tf_op jit(solution)/shard_map/reduce_scatter | solution.py:1431
  20.8 29.8 %collective-permute-start.1 = (bf16[2,256,384]{2,1,0:T(8,128)(2,1)S(1)}, bf16[2,256,384]{2,1,0:T(8,128)(2,1)S(1)}, u32[]{:S(2)}, u32[]{:S(2)}) collective-permute-start(bf16[2,256,384]{2,1,0:T(8,128)(2,1)S(1)} %get-tuple-element.234), channel_id=1, source_target_pairs={{0,16},{4,20},{8,24},{12,28},{16,0},{20,4},{24,8},{28,12},{1,17},{... | collective-permute-start | bytes 1179656 | tf_op jit(solution)/shard_map/ppermute | solution.py:334
  23.4 27.3 %collective-permute-start.2 = (bf16[2,256,384]{2,1,0:T(8,128)(2,1)S(1)}, bf16[2,256,384]{2,1,0:T(8,128)(2,1)S(1)}, u32[]{:S(2)}, u32[]{:S(2)}) collective-permute-start(bf16[2,256,384]{2,1,0:T(8,128)(2,1)S(1)} %get-tuple-element.235), channel_id=1, source_target_pairs={{0,24},{4,28},{8,16},{12,20},{16,8},{20,12},{24,0},{28,4},{1,25},{... | collective-permute-start | bytes 1179656 | tf_op jit(solution)/shard_map/ppermute | solution.py:334
  30.3 29.3 %collective-permute-start.4 = (bf16[2,256,384]{2,1,0:T(8,128)(2,1)S(1)}, bf16[2,256,384]{2,1,0:T(8,128)(2,1)S(1)}, u32[]{:S(2)}, u32[]{:S(2)}) collective-permute-start(bf16[2,256,384]{2,1,0:T(8,128)(2,1)S(1)} %get-tuple-element.241), channel_id=1, source_target_pairs={{0,8},{4,12},{8,0},{12,4},{16,24},{20,28},{24,16},{28,20},{1,9},{5... | collective-permute-start | bytes 1179656 | tf_op jit(solution)/shard_map/ppermute | solution.py:334
  31.3 53.1 %collective-permute-start.5 = (bf16[2,256,384]{2,1,0:T(8,128)(2,1)S(1)}, bf16[2,256,384]{2,1,0:T(8,128)(2,1)S(1)}, u32[]{:S(2)}, u32[]{:S(2)}) collective-permute-start(bf16[2,256,384]{2,1,0:T(8,128)(2,1)S(1)} %get-tuple-element.242), channel_id=1, source_target_pairs={{0,16},{4,20},{8,24},{12,28},{16,0},{20,4},{24,8},{28,12},{1,17},{... | collective-permute-start | bytes 1179656 | tf_op jit(solution)/shard_map/ppermute | solution.py:334
  38.4 45.9 %collective-permute-start.6 = (bf16[2,256,384]{2,1,0:T(8,128)(2,1)S(1)}, bf16[2,256,384]{2,1,0:T(8,128)(2,1)S(1)}, u32[]{:S(2)}, u32[]{:S(2)}) collective-permute-start(bf16[2,256,384]{2,1,0:T(8,128)(2,1)S(1)} %get-tuple-element.243), channel_id=1, source_target_pairs={{0,24},{4,28},{8,16},{12,20},{16,8},{20,12},{24,0},{28,4},{1,25},{... | collective-permute-start | bytes 1179656 | tf_op jit(solution)/shard_map/ppermute | solution.py:334
  177.4 34.3 %collective-permute-start.30 = (bf16[128,2048]{1,0:T(8,128)(2,1)S(1)}, bf16[128,2048]{1,0:T(8,128)(2,1)S(1)}, u32[]{:S(2)}, u32[]{:S(2)}) collective-permute-start(bf16[128,2048]{1,0:T(8,128)(2,1)S(1)} %get-tuple-element.290.refs_2_), channel_id=1, source_target_pairs={{0,3},{1,2},{2,1},{3,0},{4,7},{5,6},{6,5},{7,4},{8,11},{9,10},{10,... | collective-permute-start | bytes 1572872 | tf_op jit(solution)/shard_map/ppermute | solution.py:334
  178.1 35.7 %collective-permute-start.29 = (bf16[128,2048]{1,0:T(8,128)(2,1)S(1)}, bf16[128,2048]{1,0:T(8,128)(2,1)S(1)}, u32[]{:S(2)}, u32[]{:S(2)}) collective-permute-start(bf16[128,2048]{1,0:T(8,128)(2,1)S(1)} %get-tuple-element.290.refs_2_), channel_id=1, source_target_pairs={{0,2},{1,3},{2,0},{3,1},{4,6},{5,7},{6,4},{7,5},{8,10},{9,11},{10,... | collective-permute-start | bytes 1572872 | tf_op jit(solution)/shard_map/ppermute | solution.py:334
  179.4 34.4 %collective-permute-start.28 = (bf16[128,2048]{1,0:T(8,128)(2,1)S(1)}, bf16[128,2048]{1,0:T(8,128)(2,1)S(1)}, u32[]{:S(2)}, u32[]{:S(2)}) collective-permute-start(bf16[128,2048]{1,0:T(8,128)(2,1)S(1)} %get-tuple-element.290.refs_2_), channel_id=1, source_target_pairs={{0,1},{1,0},{2,3},{3,2},{4,5},{5,4},{6,7},{7,6},{8,9},{9,8},{10,11... | collective-permute-start | bytes 1572872 | tf_op jit(solution)/shard_map/ppermute | solution.py:334
  210.4 31.7 %collective-permute-start.31 = (bf16[128,2048]{1,0:T(8,128)(2,1)S(1)}, bf16[128,2048]{1,0:T(8,128)(2,1)S(1)}, u32[]{:S(2)}, u32[]{:S(2)}) collective-permute-start(bf16[128,2048]{1,0:T(8,128)(2,1)S(1)} %get-tuple-element.297), channel_id=1, source_target_pairs={{0,1},{1,0},{2,3},{3,2},{4,5},{5,4},{6,7},{7,6},{8,9},{9,8},{10,11... | collective-permute-start | bytes 1572872 | tf_op jit(solution)/shard_map/ppermute | solution.py:334
  211.0 31.1 %collective-permute-start.32 = (bf16[128,2048]{1,0:T(8,128)(2,1)S(1)}, bf16[128,2048]{1,0:T(8,128)(2,1)S(1)}, u32[]{:S(2)}, u32[]{:S(2)}) collective-permute-start(bf16[128,2048]{1,0:T(8,128)(2,1)S(1)} %get-tuple-element.298), channel_id=1, source_target_pairs={{0,2},{1,3},{2,0},{3,1},{4,6},{5,7},{6,4},{7,5},{8,10},{9,11},{10,... | collective-permute-start | bytes 1572872 | tf_op jit(solution)/shard_map/ppermute | solution.py:334
  211.7 30.4 %collective-permute-start.33 = (bf16[128,2048]{1,0:T(8,128)(2,1)S(1)}, bf16[128,2048]{1,0:T(8,128)(2,1)S(1)}, u32[]{:S(2)}, u32[]{:S(2)}) collective-permute-start(bf16[128,2048]{1,0:T(8,128)(2,1)S(1)} %get-tuple-element.299), channel_id=1, source_target_pairs={{0,3},{1,2},{2,1},{3,0},{4,7},{5,6},{6,5},{7,4},{8,11},{9,10},{10,... | collective-permute-start | bytes 1572872 | tf_op jit(solution)/shard_map/ppermute | solution.py:334
  266.8 306.3 %reduce-scatter.6.cloned.1.call-start = ((), (), s32[]{:S(2)}) async-start(), calls=%async_computation.4 | async-start | bytes 5242880 | tf_op jit(solution)/shard_map/reduce_scatter | solution.py:1435
  316.7 25.1 %collective-permute-start.53 = (bf16[2,2,64,2048]{3,2,1,0:T(8,128)(2,1)S(1)}, bf16[2,2,64,2048]{3,2,1,0:T(8,128)(2,1)S(1)}, u32[]{:S(2)}, u32[]{:S(2)}) collective-permute-start(bf16[2,2,64,2048]{3,2,1,0:T(8,128)(2,1)S(1)} %copy-done.68), channel_id=1, source_target_pairs={{0,1},{1,0},{2,3},{3,2},{4,5},{5,4},{6,7},{7,6},{8,9},{9,8},{10,11... | collective-permute-start | bytes 3145736 | tf_op jit(solution)/shard_map/ppermute | solution.py:334
  377.5 60.8 %collective-permute-start.64 = (bf16[2,2,64,2048]{3,2,1,0:T(8,128)(2,1)S(1)}, bf16[2,2,64,2048]{3,2,1,0:T(8,128)(2,1)S(1)}, u32[]{:S(2)}, u32[]{:S(2)}) collective-permute-start(bf16[2,2,64,2048]{3,2,1,0:T(8,128)(2,1)S(1)} %get-tuple-element.382), channel_id=1, source_target_pairs={{0,2},{1,3},{2,0},{3,1},{4,6},{5,7},{6,4},{7,5},{8,10},{9,11},{10,... | collective-permute-start | bytes 3145736 | tf_op jit(solution)/shard_map/ppermute | solution.py:334
  378.0 60.4 %collective-permute-start.65 = (bf16[2,2,64,2048]{3,2,1,0:T(8,128)(2,1)S(1)}, bf16[2,2,64,2048]{3,2,1,0:T(8,128)(2,1)S(1)}, u32[]{:S(2)}, u32[]{:S(2)}) collective-permute-start(bf16[2,2,64,2048]{3,2,1,0:T(8,128)(2,1)S(1)} %get-tuple-element.383), channel_id=1, source_target_pairs={{0,1},{1,0},{2,3},{3,2},{4,5},{5,4},{6,7},{7,6},{8,9},{9,8},{10,11... | collective-permute-start | bytes 3145736 | tf_op jit(solution)/shard_map/ppermute | solution.py:334
  379.1 35.5 %collective-permute-start.61 = (bf16[2,2,256,384]{3,2,1,0:T(8,128)(2,1)S(1)}, bf16[2,2,256,384]{3,2,1,0:T(8,128)(2,1)S(1)}, u32[]{:S(2)}, u32[]{:S(2)}) collective-permute-start(bf16[2,2,256,384]{3,2,1,0:T(8,128)(2,1)S(1)} %copy-done.72), channel_id=1, source_target_pairs={{0,8},{4,12},{8,0},{12,4},{16,24},{20,28},{24,16},{28,20},{1,9},{5... | collective-permute-start | bytes 2359304 | tf_op jit(solution)/shard_map/ppermute | solution.py:334
  383.1 55.1 %collective-permute-start.62 = (bf16[2,2,256,384]{3,2,1,0:T(8,128)(2,1)S(1)}, bf16[2,2,256,384]{3,2,1,0:T(8,128)(2,1)S(1)}, u32[]{:S(2)}, u32[]{:S(2)}) collective-permute-start(bf16[2,2,256,384]{3,2,1,0:T(8,128)(2,1)S(1)} %copy-done.74), channel_id=1, source_target_pairs={{0,16},{4,20},{8,24},{12,28},{16,0},{20,4},{24,8},{28,12},{1,17},{... | collective-permute-start | bytes 2359304 | tf_op jit(solution)/shard_map/ppermute | solution.py:334
  384.4 53.8 %collective-permute-start.63 = (bf16[2,2,256,384]{3,2,1,0:T(8,128)(2,1)S(1)}, bf16[2,2,256,384]{3,2,1,0:T(8,128)(2,1)S(1)}, u32[]{:S(2)}, u32[]{:S(2)}) collective-permute-start(bf16[2,2,256,384]{3,2,1,0:T(8,128)(2,1)S(1)} %copy-done.76), channel_id=1, source_target_pairs={{0,24},{4,28},{8,16},{12,20},{16,8},{20,12},{24,0},{28,4},{1,25},{... | collective-permute-start | bytes 2359304 | tf_op jit(solution)/shard_map/ppermute | solution.py:334
  440.9 170.8 %reduce-scatter.8.cloned.1.call-start = ((), (), s32[]{:S(2)}) async-start(), calls=%async_computation.5 | async-start | bytes 5242880 | tf_op jit(solution)/shard_map/reduce_scatter | solution.py:1435
  458.7 25.2 %collective-permute-start.67 = (bf16[2,2,64,2048]{3,2,1,0:T(8,128)(2,1)S(1)}, bf16[2,2,64,2048]{3,2,1,0:T(8,128)(2,1)S(1)}, u32[]{:S(2)}, u32[]{:S(2)}) collective-permute-start(bf16[2,2,64,2048]{3,2,1,0:T(8,128)(2,1)S(1)} %get-tuple-element.399), channel_id=1, source_target_pairs={{0,1},{1,0},{2,3},{3,2},{4,5},{5,4},{6,7},{7,6},{8,9},{9,8},{10,11... | collective-permute-start | bytes 3145736 | tf_op jit(solution)/shard_map/ppermute | solution.py:334
  459.6 24.9 %collective-permute-start.68 = (bf16[2,2,64,2048]{3,2,1,0:T(8,128)(2,1)S(1)}, bf16[2,2,64,2048]{3,2,1,0:T(8,128)(2,1)S(1)}, u32[]{:S(2)}, u32[]{:S(2)}) collective-permute-start(bf16[2,2,64,2048]{3,2,1,0:T(8,128)(2,1)S(1)} %get-tuple-element.401), channel_id=1, source_target_pairs={{0,2},{1,3},{2,0},{3,1},{4,6},{5,7},{6,4},{7,5},{8,10},{9,11},{10,... | collective-permute-start | bytes 3145736 | tf_op jit(solution)/shard_map/ppermute | solution.py:334
  535.8 32.6 %collective-permute-start.74 = (bf16[2,2,64,2048]{3,2,1,0:T(8,128)(2,1)}, bf16[2,2,64,2048]{3,2,1,0:T(8,128)(2,1)S(1)}, u32[]{:S(2)}, u32[]{:S(2)}) collective-permute-start(bf16[2,2,64,2048]{3,2,1,0:T(8,128)(2,1)} %get-tuple-element.420), channel_id=1, source_target_pairs={{0,2},{1,3},{2,0},{3,1},{4,6},{5,7},{6,4},{7,5},{8,10},{9,11},{10,... | collective-permute-start | bytes 3145736 | tf_op jit(solution)/shard_map/ppermute | solution.py:334
  537.5 30.9 %collective-permute-start.75 = (bf16[2,2,64,2048]{3,2,1,0:T(8,128)(2,1)}, bf16[2,2,64,2048]{3,2,1,0:T(8,128)(2,1)}, u32[]{:S(2)}, u32[]{:S(2)}) collective-permute-start(bf16[2,2,64,2048]{3,2,1,0:T(8,128)(2,1)} %get-tuple-element.421), channel_id=1, source_target_pairs={{0,1},{1,0},{2,3},{3,2},{4,5},{5,4},{6,7},{7,6},{8,9},{9,8},{10,11... | collective-permute-start | bytes 3145736 | tf_op jit(solution)/shard_map/ppermute | solution.py:334
  (176 other events, 2249.1 us)
Sparse Core Ops, SparseCore 0:
  266.9 106.0 reduce-scatter.3
  441.0 90.9 reduce-scatter.5
  534.5 77.2 reduce-scatter.7

commit v5 on v4

--- a/solution.py
+++ b/solution.py
@@ -924,9 +924,7 @@
     )
 
 
-def feed_forward(
-    tp_here, pieces, cot, up_weight, up_bias, down_weight, earlier, index, count, direct, after=()
-):
+def feed_inner(tp_here, pieces, cot, up_weight, up_bias, down_weight, with_grad, after=()):
     rows, width = cot.shape
     hidden = up_weight.shape[1]
     size = rows // 4
@@ -936,10 +934,9 @@
     def body(tp_ref, *rest):
         refs, rest = rest[: len(pieces)], rest[len(pieces) :]
         cot_ref, up_hbm, bias_ref, down_hbm = rest[:4]
-        rest = rest[4 + len(earlier) :]
-        norm_ref, act_ref, pre_ref, sum_ref, cot_sum_ref = rest[:5]
-        feed_outs, grad_outs = rest[5:9], rest[9:13]
-        up, down, held, sems = rest[13:]
+        norm_ref, act_ref, pre_ref, sum_ref, cot_sum_ref = rest[4:9]
+        grad_outs = rest[9:13] if with_grad else ()
+        up, down, held, sems = rest[-4:]
 
         def part(number):
             return pl.ds(pl.multiple_of(number * step, step), step)
@@ -975,42 +972,32 @@
             pre_ref[:, place] = grad_pre
             sum_ref[:, place] = jnp.sum(grad_pre.astype(F32), axis=0, keepdims=True)
 
-        @pl.loop(0, width // step)
-        def _(number):
-            place = part(number)
-            held[:, place] = dot_nt(pre_ref[...], up[place, :]).astype(BF)
-
-        emit_messages(lambda at: held[at, :], tp_ref[0], grad_outs, size)
-
-        @pl.loop(0, width // step)
-        def _(number):
-            place = part(number)
-            held[:, place] = dot(act_ref[...], down[:, place]).astype(BF)
-
-        emit_messages(lambda at: held[at, :], tp_ref[0], [ref.at[0] for ref in feed_outs], size)
-
-    message = (2, size // 2, width)
-    args = [tp_here, *pieces, cot, up_weight, up_bias, down_weight, *earlier]
-    first = len(args) - len(earlier)
+        if with_grad:
+
+            @pl.loop(0, width // step)
+            def _(number):
+                place = part(number)
+                held[:, place] = dot_nt(pre_ref[...], up[place, :]).astype(BF)
+
+            emit_messages(lambda at: held[at, :], tp_ref[0], grad_outs, size)
+
+    args = [tp_here, *pieces, cot, up_weight, up_bias, down_weight]
     outs = [
         sds((rows, width)),
         sds((rows, hidden)),
         sds((rows, hidden)),
         sds((1, hidden), F32),
         sds((1, width), F32),
-    ]
-    messages = message_shapes(size // 2, width, direct)
+    ] + (message_shapes(size // 2, width, True) if with_grad else [])
     return launch(
         body,
         operands_of(args),
         [pl.BlockSpec(memory_space=pltpu.SMEM)]
         + [whole_of(piece.shape) for piece in pieces]
-        + [cot.spec(), pl.BlockSpec(memory_space=pl.ANY), whole_of(up_bias.shape)]
-        + [pl.BlockSpec(memory_space=pl.ANY)] * (1 + len(earlier)),
-        outs + [sds((count,) + message)] * 4 + messages,
-        [whole_of(item.shape) for item in outs]
-        + [pl.BlockSpec((1,) + message, lambda i: (index, 0, 0, 0))] * 4
-        + [whole_of(item.shape) for item in messages],
+        + [cot.spec(), pl.BlockSpec(memory_space=HBM), whole_of(up_bias.shape)]
+        + [pl.BlockSpec(memory_space=HBM)],
+        outs,
+        [whole_of(item.shape) for item in outs],
         [
             pltpu.VMEM((width, hidden), BF),
             pltpu.VMEM((hidden, width), BF),
@@ -1018,11 +1005,90 @@
             pltpu.SemaphoreType.DMA((2, blocks)),
         ],
         50 << 20,
-        cost(8 * rows * width * hidden, 4 * width * hidden + 20 * rows * width),
-        "feed_forward",
+        cost(6 * rows * width * hidden, 4 * width * hidden + 20 * rows * width),
+        "feed_inner",
         after,
         grid=(1,),
-        aliases={first + number: 5 + number for number in range(len(earlier))},
+    )
+
+
+def feed_grad(tp_here, grad_pre, up_weight, after=()):
+    rows, hidden = grad_pre.shape
+    width = up_weight.shape[0]
+    size = rows // 4
+    step = 512
+    blocks = width // step
+
+    def body(tp_ref, pre_ref, up_ref, *rest):
+        outs, held = rest[:4], rest[4]
+        number = pl.program_id(0)
+        place = pl.ds(pl.multiple_of(number * step, step), step)
+        held[:, place] = dot_nt(pre_ref[...], up_ref[...]).astype(BF)
+
+        @pl.when(number == blocks - 1)
+        def _():
+            emit_messages(lambda at: held[at, :], tp_ref[0], outs, size)
+
+    outs = message_shapes(size // 2, width)
+    return launch(
+        body,
+        operands_of([tp_here, grad_pre, up_weight]),
+        [
+            pl.BlockSpec(memory_space=pltpu.SMEM),
+            whole_of(grad_pre.shape),
+            pl.BlockSpec((step, hidden), lambda i: (i, 0)),
+        ],
+        outs,
+        [whole_of(item.shape) for item in outs],
+        [pltpu.VMEM((rows, width), BF)],
+        24 << 20,
+        cost(2 * rows * width * hidden, 2 * width * hidden + 6 * rows * width),
+        "feed_grad",
+        after,
+        grid=(blocks,),
+    )
+
+
+def feed_out(tp_here, acts, down_weight, after=()):
+    count = len(acts)
+    rows, hidden = acts[0].shape
+    width = down_weight.shape[1]
+    size = rows // 4
+    step = 512
+    blocks = width // step
+
+    def body(tp_ref, *rest):
+        act_refs, down_ref, outs, held = rest[:count], rest[count], rest[-5:-1], rest[-1]
+        number = pl.program_id(0)
+        place = pl.ds(pl.multiple_of(number * step, step), step)
+        for index in range(count):
+            held[index, :, place] = dot(act_refs[index][...], down_ref[...]).astype(BF)
+
+        @pl.when(number == blocks - 1)
+        def _():
+            for index in range(count):
+                emit_messages(
+                    lambda at: held[index, at, :],
+                    tp_ref[0],
+                    [ref.at[index] for ref in outs],
+                    size,
+                )
+
+    outs = [sds((count,) + item.shape) for item in message_shapes(size // 2, width)]
+    return launch(
+        body,
+        operands_of([tp_here, *acts, down_weight]),
+        [pl.BlockSpec(memory_space=pltpu.SMEM)]
+        + [whole_of(act.shape) for act in acts]
+        + [pl.BlockSpec((hidden, step), lambda i: (0, i))],
+        outs,
+        [whole_of(item.shape) for item in outs],
+        [pltpu.VMEM((count, rows, width), BF)],
+        36 << 20,
+        cost(2 * count * rows * width * hidden, 2 * width * hidden + 12 * rows * width),
+        "feed_out",
+        after,
+        grid=(blocks,),
     )
 
 
@@ -1473,18 +1539,15 @@
 
     norm_two, acts, grad_pres, up_sums, cot_sums = [], [], [], [], []
 
-    def feed_micro(index, pieces, feeds, direct, done):
-        (normed, act, grad_pre, up_sum, cot_sum, *messages), done = feed_forward(
+    def feed_micro(index, pieces, with_grad, done):
+        (normed, act, grad_pre, up_sum, cot_sum, *messages), done = feed_inner(
             tp_here,
             pieces,
             cots[index],
             up_weight,
             high_bias,
             down_weight,
-            feeds,
-            index,
-            micro_count,
-            direct,
+            with_grad,
             after=done,
         )
         norm_two.append(normed)
@@ -1492,8 +1555,7 @@
         grad_pres.append(grad_pre)
         up_sums.append(up_sum)
         cot_sums.append(cot_sum)
-        messages, ours = messages[:4], messages[4:]
-        return messages, reduce_direct(ours) if direct else ours, done
+        return messages, done
 
     grad_resids, gain_twos, shift_twos = [], [], []
     grad_mixes, mix_sums, states = [], [], []
@@ -1548,15 +1610,17 @@
     sums_b, done = reduce_second(state_b, done)
     state_b, done = norm_micro(1, sums_b, True, done)
     pieces_b = gather_direct(state_b[0])
-    feeds, sums_a, done = feed_micro(0, pieces_a, [], True, done)
-    feeds, messages, done = feed_micro(1, pieces_b, feeds, False, done)
-
+    messages, done = feed_micro(0, pieces_a, True, done)
+    sums_a = reduce_direct(messages)
+    _, done = feed_micro(1, pieces_b, False, done)
+    (down_part,), done = weight_grad([(cots, acts)], after=done)
+    state_a, done = norm_back_micro(0, sums_a, done)
+    down_grad = scattered(until(down_part, done))
+    messages, done = feed_grad(tp_here, grad_pres[1], up_weight, after=done)
     state_b = reduce_first(messages)
-    state_a, done = norm_back_micro(0, sums_a, done)
-    (down_part,), done = weight_grad([(cots, acts)], after=done)
     pieces_a, done = gather_second(state_a, done)
+    feeds, done = feed_out(tp_here, acts, down_weight, after=done)
     sums_b, done = reduce_second(state_b, done)
-    down_grad = scattered(until(down_part, done))
     done = heads_back_micro(0, pieces_a, done)
     state_b, done = norm_back_micro(1, sums_b, done)
     pieces_b, done = gather_second(state_b, done)
@@ -1572,9 +1636,7 @@
     state_back = exchange_chips(*sent_back)
     halves, done = finish_outputs(sums_feed, resids, low_bias, after=done)
     (up_part,), done = add_halves(own, got_up, after=done)
-    pieces_out, done = gather_second(gather_first(halves), done)
     got, done = exchange_cores(state_back, done)
-    outputs, done = assemble_outputs(tp_here, pieces_out, BF, after=done)
     up_grad = scattered_chips(until(up_part, done))
     (*grad_projs, proj_sum, first, second, third, fourth), done = project_back(
         here, tp_here, got, weight_three, after=done
@@ -1584,12 +1646,14 @@
     (sent, own), done = weight_grad(last, here, after=done)
     sums_one, done = reduce_second(state_one, done)
     got_last = xor_permute(until(sent, done), "ctx", 1)
+    pieces_out, done = gather_second(gather_first(halves), done)
     (last_part,), done = add_halves(own, got_last, after=done)
     (gain_sum, shift_sum, *halves), done = first_norm_back(
         sums_one, x_mine, grad_resids, gain_one, after=done
     )
     last_grad = scattered_chips(until(last_part, done))
     pieces_in, done = gather_second(gather_first(halves), done)
+    outputs, done = assemble_outputs(tp_here, pieces_out, BF, after=done)
     gain_ones, shift_ones, proj_sums = [gain_sum], [shift_sum], [proj_sum]
     (down_grad,), done = widen(down_grad, True, after=done)
     input_grad, done = assemble_outputs(tp_here, pieces_in, F32, after=done)

time: 631 us -> 611 us (0.968)
  waiting for transfers between devices: 245 us -> 214 us
    reduce_scatter x2, waiting for transfers between devices: 36 us -> 0.01 us  [scattered_chips(): lax.psum_scatter(part, 'ctx', scatter_dimension=0, axis_index_groups=chip...]
    unnamed x232 -> x230, local copies, waits for them, and re-layouts: 42.6 us -> 47.4 us
    pallas_call x46 -> x48, Pallas kernels: 197 us -> 201 us  [launch(): pl.pallas_call(inner, grid_spec=pltpu.PrefetchScalarGridSpec(num_scalar_p...]
  transfers between devices with their start and end apart: 84 -> 84, of which waited for: 34 -> 33; matrix products, arithmetic and copies ran while one was open for 1% -> 1% of each run, Pallas kernels for 30% -> 31%
where the time goes in v5:
time: 611 us; the launch traced here: 601 us
  waiting for transfers between devices  214 us (35%)
  Pallas kernels  201 us (33%)
  starting transfers between devices  116 us (19%)
  local copies, waits for them, and re-layouts  53.8 us (9%)
  between operations  15.6 us (3%)
    ppermute x81, waiting for transfers between devices, xor_permute(): return lax.ppermute(values, axis, [(i, i ^ step) for i in range(count)])  214 us
    pallas_call x48, Pallas kernels, launch(): pl.pallas_call(inner, grid_spec=pltpu.PrefetchScalarGridSpec(num_scalar_p...  201 us
    ppermute x81, starting transfers between devices, xor_permute(): return lax.ppermute(values, axis, [(i, i ^ step) for i in range(count)])  116 us
    unnamed x230, local copies, waits for them, and re-layouts  47.4 us
  transfers between devices with their start and end apart: 84, of which 33 were waited for; matrix products, arithmetic and copies ran while one was open for 1% of the time, Pallas kernels for 31%

profile of v5, /device:TPU:0, one launch (start us, length us, event | category | flops | bytes accessed | tf_op | source)
XLA Modules:
  0.0 600.8 jit_solution(11246453014166523542)
XLA Ops:
  23.4 6.9 %project.3 = (bf16[512,2048]{1,0:T(8,128)(2,1)S(1)}, bf16[256,384]{1,0:T(8,128)(2,1)S(1)}, bf16[256,384]{1,0:T(8,128)(2,1)S(1)}, bf16[2,256,384]{2,1,0:T(8,128)(...) custom-call(f32[8,128]{1,0:T(8,128)S(1)} %get-tuple-element.228.refs_0_, ...), custom_call_target="tpu_custom_call" | custom-call | flops 3221225472 | bytes 3692544 | tf_op jit(solution)/shard_map/project/pallas_call | solution.py:374
  43.0 7.6 %collective-permute-done.1.refs_3_.refs_4_ = bf16[2,256,384]{2,1,0:T(8,128)(2,1)S(1)} collective-permute-done((bf16[2,256,384]{2,1,0:T(8,128)(2,1)S(1)}, bf16[2,256,384]{2,1,0:T(8,128)(2,1)S(1)}, u32[]{:S(2)}, u32[]{:S(2)}) %collective-permute-start.1) | collective-permute-done | bytes 393248 | tf_op jit(solution)/shard_map/ppermute | solution.py:334
  59.3 25.0 %collective-permute-done.5.refs_3_.refs_4_ = bf16[2,256,384]{2,1,0:T(8,128)(2,1)S(1)} collective-permute-done((bf16[2,256,384]{2,1,0:T(8,128)(2,1)S(1)}, bf16[2,256,384]{2,1,0:T(8,128)(2,1)S(1)}, u32[]{:S(2)}, u32[]{:S(2)}) %collective-permute-start.5) | collective-permute-done | bytes 393248 | tf_op jit(solution)/shard_map/ppermute | solution.py:334
  84.5 7.6 %collective-permute-start.8 = (bf16[2,256,128]{2,1,0:T(8,128)(2,1)S(1)}, bf16[2,256,128]{2,1,0:T(8,128)(2,1)S(1)}, u32[]{:S(2)}, u32[]{:S(2)}) collective-permute-start(bf16[2,256,128]{2,1,0:T(8,128)(2,1)S(1)} %get-tuple-element.247), channel_id=1, source_target_pairs={{0,8},{4,12},{8,0},{12,4},{16,24},{20,28},{24,16},{28,20},{1,9},{5... | collective-permute-start | bytes 393224 | tf_op jit(solution)/shard_map/ppermute | solution.py:334
  143.5 13.9 %collective-permute-done.20.refs_2_.refs_3_ = bf16[64,2048]{1,0:T(8,128)(2,1)S(1)} collective-permute-done((bf16[64,2048]{1,0:T(8,128)(2,1)S(1)}, bf16[64,2048]{1,0:T(8,128)(2,1)S(1)}, u32[]{:S(2)}, u32[]{:S(2)}) %collective-permute-start.20) | collective-permute-done | bytes 262176 | tf_op jit(solution)/shard_map/ppermute | solution.py:334
  165.4 11.7 %collective-permute-done.24.refs_2_ = bf16[64,2048]{1,0:T(8,128)(2,1)S(1)} collective-permute-done((bf16[64,2048]{1,0:T(8,128)(2,1)S(1)}, bf16[64,2048]{1,0:T(8,128)(2,1)S(1)}, u32[]{:S(2)}, u32[]{:S(2)}) %collective-permute-start.24) | collective-permute-done | bytes 262176 | tf_op jit(solution)/shard_map/ppermute | solution.py:334
  184.2 20.7 %feed_inner.2 = (bf16[512,2048]{1,0:T(8,128)(2,1)}, bf16[512,2048]{1,0:T(8,128)(2,1)}, bf16[512,2048]{1,0:T(8,128)(2,1)}, f32[1,2048]{1,0:T(1,128)S(1)}, f32[1,2...) custom-call(f32[8,128]{1,0:T(8,128)S(1)} %get-tuple-element.284.refs, ...), custom_call_target="tpu_custom_call" | custom-call | flops 12884901888 | bytes 37748736 | tf_op jit(solution)/shard_map/feed_inner/pallas_call | solution.py:374
  209.4 15.3 %feed_inner.3 = (bf16[512,2048]{1,0:T(8,128)(2,1)S(1)}, bf16[512,2048]{1,0:T(8,128)(2,1)}, bf16[512,2048]{1,0:T(8,128)(2,1)}, f32[1,2048]{1,0:T(1,128)S(1)}, f32...) custom-call(f32[8,128]{1,0:T(8,128)S(1)} %get-tuple-element.287.refs_0_, s32[1]{0:T(128)} %bitcast.9.refs_2_.refs_1_, ...), custom_call_target="tpu_custom_call" | custom-call | flops 12884901888 | bytes 37748736 | tf_op jit(solution)/shard_map/feed_inner/pallas_call | solution.py:374
  224.7 14.2 %weight_grad.3 = (bf16[2048,2048]{1,0:T(8,128)(2,1)}, f32[8,128]{1,0:T(8,128)S(1)}) custom-call(f32[8,128]{1,0:T(8,128)S(1)} %get-tuple-element.289.refs_0_, bf16[2,512,2048]{2,1,0:T(8,128)(2,1)} %bitcast.89, bf16[2,512,2048]{2,1,0:T(8,128)(2,1)} %bitcast.90, bf16[512,2048]{1,0:T(8,128)(2,1)} %get-tuple-element.290.refs_3_.refs_2_, ...), custom_call_target="tpu_custom_call" | custom-call | flops 8589934592 | bytes 16777216 | tf_op jit(solution)/shard_map/weight_grad/pallas_call | solution.py:374
  243.9 8.2 %feed_grad.1 = (bf16[2,64,2048]{2,1,0:T(8,128)(2,1)S(1)}, bf16[2,64,2048]{2,1,0:T(8,128)(2,1)S(1)}, bf16[2,64,2048]{2,1,0:T(8,128)(2,1)S(1)}, bf16[2,64,2048]{2,1,0:T(8,128)(2,1)S(1)}, f32[8,128]{1,0:T(8,128)S(1)}) custom-call(f32[8,128]{1,0:T(8,128)S(1)} %get-tuple-element.298.refs_0_, s32[1]{0:T(128)} %bitcast.9.refs_2_.refs_1_, ...), custom_call_target="tpu_custom_call" | custom-call | flops 4294967296 | bytes 14680064 | tf_op jit(solution)/shard_map/feed_grad/pallas_call | solution.py:374
  256.4 12.6 %feed_out.1 = (bf16[2,2,64,2048]{3,2,1,0:T(8,128)(2,1)S(1)}, bf16[2,2,64,2048]{3,2,1,0:T(8,128)(2,1)S(1)}, bf16[2,2,64,2048]{3,2,1,0:T(8,128)(2,1)S(1)}, bf16[2,...) custom-call(f32[8,128]{1,0:T(8,128)S(1)} %get-tuple-element.303.refs_0_, s32[1]{0:T(128)} %bitcast.9.refs_2_.refs_1_, ...), custom_call_target="tpu_custom_call" | custom-call | flops 8589934592 | bytes 20971520 | tf_op jit(solution)/shard_map/feed_out/pallas_call | solution.py:374
  294.9 14.6 %weight_grad.4 = (bf16[4,256,2048]{2,1,0:T(8,128)(2,1)}, bf16[4,256,2048]{2,1,0:T(8,128)(2,1)}, f32[8,128]{1,0:T(8,128)S(1)}) custom-call(s32[1]{0:T(128)} %bitcast.refs_0_.refs_1_, f32[8,128]{1,0:T(8,128)S(1)} %get-tuple-element.321.refs_1_, bf16[512,2048]{1,0:T(8,128)(2,1)} %get-tuple-element.322.refs_2_, bf16[512,2048]{1,0:T(8,128)(2,1)} %copy-done.101, ...), custom_call_target="tpu_custom_call" | custom-call | flops 8589934592 | bytes 16777216 | tf_op jit(solution)/shard_map/weight_grad/pallas_call | solution.py:374
  318.5 9.9 %attention_back.2 = (bf16[2,256,384]{2,1,0:T(8,128)(2,1)S(1)}, bf16[2,256,384]{2,1,0:T(8,128)(2,1)S(1)}, bf16[2,2,256,384]{3,2,1,0:T(8,128)(2,1)S(1)}, bf16[2,2,...) custom-call(f32[8,128]{1,0:T(8,128)S(1)} %get-tuple-element.333.refs_0_, ...), custom_call_target="tpu_custom_call" | custom-call | flops 2684354560 | bytes 3145728 | tf_op jit(solution)/shard_map/attention_back/pallas_call | solution.py:374
  345.5 11.2 %attention_back.3 = (bf16[2,256,384]{2,1,0:T(8,128)(2,1)}, bf16[2,256,384]{2,1,0:T(8,128)(2,1)}, bf16[2,2,256,384]{3,2,1,0:T(8,128)(2,1)}, bf16[2,2,256,384]{3,2...) custom-call(f32[8,128]{1,0:T(8,128)S(1)} %get-tuple-element.351.refs, ...), custom_call_target="tpu_custom_call", output_to_operand_aliasing={{0}: (15, {}), {1}: (16, {}), {2}: (17, {}), {3}: (18, {}),... | custom-call | flops 2684354560 | bytes 3145728 | tf_op jit(solution)/shard_map/attention_back/pallas_call | solution.py:374
  365.5 11.9 %collective-permute-done.57.refs_4_ = bf16[2,64,2048]{2,1,0:T(8,128)(2,1)S(1)} collective-permute-done((bf16[2,64,2048]{2,1,0:T(8,128)(2,1)S(1)}, bf16[2,64,2048]{2,1,0:T(8,128)(2,1)S(1)}, u32[]{:S(2)}, u32[]{:S(2)}) %collective-permute-start.57) | collective-permute-done | bytes 524320 | tf_op jit(solution)/shard_map/ppermute | solution.py:334
  385.7 9.9 %collective-permute-done.59.refs_2_.refs_4_ = bf16[2,2,256,384]{3,2,1,0:T(8,128)(2,1)S(1)} collective-permute-done((bf16[2,2,256,384]{3,2,1,0:T(8,128)(2,1)}, bf16[2,2,256,384]{3,2,1,0:T(8,128)(2,1)S(1)}, u32[]{:S(2)}, u32[]{:S(2)}) %collective-permute-start.59) | collective-permute-done | bytes 786464 | tf_op jit(solution)/shard_map/ppermute | solution.py:334
  395.6 20.9 %collective-permute-done.60.refs_3_.refs_5_ = bf16[2,2,256,384]{3,2,1,0:T(8,128)(2,1)S(1)} collective-permute-done((bf16[2,2,256,384]{3,2,1,0:T(8,128)(2,1)}, bf16[2,2,256,384]{3,2,1,0:T(8,128)(2,1)S(1)}, u32[]{:S(2)}, u32[]{:S(2)}) %collective-permute-start.60) | collective-permute-done | bytes 786464 | tf_op jit(solution)/shard_map/ppermute | solution.py:334
  430.4 7.7 %project_back.1 = (bf16[512,1536]{1,0:T(8,128)(2,1)S(1)}, bf16[512,1536]{1,0:T(8,128)(2,1)S(1)}, f32[1,1536]{1,0:T(1,128)S(1)}, bf16[2,2,64,2048]{3,2,1,0:T(8,12...) custom-call(f32[8,128]{1,0:T(8,128)S(1)} %get-tuple-element.374.refs, ...), custom_call_target="tpu_custom_call" | custom-call | flops 6442450944 | bytes 17963008 | tf_op jit(solution)/shard_map/project_back/pallas_call | solution.py:374
  442.6 15.5 %weight_grad.5 = (bf16[4,256,2048]{2,1,0:T(8,128)(2,1)}, bf16[4,256,2048]{2,1,0:T(8,128)(2,1)}, f32[8,128]{1,0:T(8,128)S(1)}) custom-call(s32[1]{0:T(128)} %bitcast.refs_0_.refs_1_, f32[8,128]{1,0:T(8,128)S(1)} %get-tuple-element.377.refs_1_, bf16[512,2048]{1,0:T(8,128)(2,1)} %copy-done.86, bf16[512,2048]{1,0:T(8,128)(2,1)} %copy-done.85, ...), custom_call_target="tpu_custom_call" | custom-call | flops 8589934592 | bytes 20971520 | tf_op jit(solution)/shard_map/weight_grad/pallas_call | solution.py:374
  458.1 7.6 %collective-permute-done.63.refs_2_ = bf16[2,2,64,2048]{3,2,1,0:T(8,128)(2,1)S(1)} collective-permute-done((bf16[2,2,64,2048]{3,2,1,0:T(8,128)(2,1)S(1)}, bf16[2,2,64,2048]{3,2,1,0:T(8,128)(2,1)S(1)}, u32[]{:S(2)}, u32[]{:S(2)}) %collective-permute-start.63) | collective-permute-done | bytes 1048608 | tf_op jit(solution)/shard_map/ppermute | solution.py:334
  471.5 10.7 %collective-permute-done.65.refs_2_.refs_3_ = bf16[2,64,2048]{2,1,0:T(8,128)(2,1)S(1)} collective-permute-done((bf16[2,64,2048]{2,1,0:T(8,128)(2,1)S(1)}, bf16[2,64,2048]{2,1,0:T(8,128)(2,1)S(1)}, u32[]{:S(2)}, u32[]{:S(2)}) %collective-permute-start.65) | collective-permute-done | bytes 524320 | tf_op jit(solution)/shard_map/ppermute | solution.py:334
  497.3 17.2 %collective-permute-start.76 = (f32[4,8,256]{2,1,0:T(8,128)S(1)}, f32[4,8,256]{2,1,0:T(8,128)S(1)}, u32[]{:S(2)}, u32[]{:S(2)}) collective-permute-start(f32[4,8,256]{2,1,0:T(8,128)S(1)} %dynamic-slice_bitcast_fusion.4), channel_id=1, source_target_pairs={{0,16},{4,20},{8,24},{12,28},{16,0},{20,4},{24,8},{28,12},{1,17},{... | collective-permute-start | bytes 98312 | tf_op jit(solution)/shard_map/ppermute | solution.py:334
  522.5 7.0 %collective-permute-done.70.refs_2_.refs_3_ = bf16[2,64,2048]{2,1,0:T(8,128)(2,1)} collective-permute-done((bf16[2,64,2048]{2,1,0:T(8,128)(2,1)S(1)}, bf16[2,64,2048]{2,1,0:T(8,128)(2,1)}, u32[]{:S(2)}, u32[]{:S(2)}) %collective-permute-start.70) | collective-permute-done | bytes 524320 | tf_op jit(solution)/shard_map/ppermute | solution.py:334
  536.8 36.1 %collective-permute-done.79 = f32[4,256]{1,0:T(4,128)S(1)} collective-permute-done((f32[4,256]{1,0:T(4,128)S(1)}, f32[4,256]{1,0:T(4,128)S(1)}, u32[]{:S(2)}, u32[]{:S(2)}) %collective-permute-start.79) | collective-permute-done | bytes 4128 | tf_op jit(solution)/shard_map/ppermute | solution.py:334
  (456 shorter events, 261.3 us)
Async XLA Ops:
  7.2 573.3 %reduce-scatter.4.cloned.1.call-start = ((), (), s32[]{:S(2)}) async-start(), calls=%async_computation.3 | async-start | bytes 9437184 | tf_op jit(solution)/shard_map/reduce_scatter | solution.py:1497
  20.8 29.8 %collective-permute-start.1 = (bf16[2,256,384]{2,1,0:T(8,128)(2,1)S(1)}, bf16[2,256,384]{2,1,0:T(8,128)(2,1)S(1)}, u32[]{:S(2)}, u32[]{:S(2)}) collective-permute-start(bf16[2,256,384]{2,1,0:T(8,128)(2,1)S(1)} %get-tuple-element.232), channel_id=1, source_target_pairs={{0,16},{4,20},{8,24},{12,28},{16,0},{20,4},{24,8},{28,12},{1,17},{... | collective-permute-start | bytes 1179656 | tf_op jit(solution)/shard_map/ppermute | solution.py:334
  23.4 27.2 %collective-permute-start.2 = (bf16[2,256,384]{2,1,0:T(8,128)(2,1)S(1)}, bf16[2,256,384]{2,1,0:T(8,128)(2,1)S(1)}, u32[]{:S(2)}, u32[]{:S(2)}) collective-permute-start(bf16[2,256,384]{2,1,0:T(8,128)(2,1)S(1)} %get-tuple-element.233), channel_id=1, source_target_pairs={{0,24},{4,28},{8,16},{12,20},{16,8},{20,12},{24,0},{28,4},{1,25},{... | collective-permute-start | bytes 1179656 | tf_op jit(solution)/shard_map/ppermute | solution.py:334
  31.6 27.7 %collective-permute-start.4 = (bf16[2,256,384]{2,1,0:T(8,128)(2,1)S(1)}, bf16[2,256,384]{2,1,0:T(8,128)(2,1)S(1)}, u32[]{:S(2)}, u32[]{:S(2)}) collective-permute-start(bf16[2,256,384]{2,1,0:T(8,128)(2,1)S(1)} %get-tuple-element.239), channel_id=1, source_target_pairs={{0,8},{4,12},{8,0},{12,4},{16,24},{20,28},{24,16},{28,20},{1,9},{5... | collective-permute-start | bytes 1179656 | tf_op jit(solution)/shard_map/ppermute | solution.py:334
  32.5 51.8 %collective-permute-start.5 = (bf16[2,256,384]{2,1,0:T(8,128)(2,1)S(1)}, bf16[2,256,384]{2,1,0:T(8,128)(2,1)S(1)}, u32[]{:S(2)}, u32[]{:S(2)}) collective-permute-start(bf16[2,256,384]{2,1,0:T(8,128)(2,1)S(1)} %get-tuple-element.240), channel_id=1, source_target_pairs={{0,16},{4,20},{8,24},{12,28},{16,0},{20,4},{24,8},{28,12},{1,17},{... | collective-permute-start | bytes 1179656 | tf_op jit(solution)/shard_map/ppermute | solution.py:334
  38.4 45.9 %collective-permute-start.6 = (bf16[2,256,384]{2,1,0:T(8,128)(2,1)S(1)}, bf16[2,256,384]{2,1,0:T(8,128)(2,1)S(1)}, u32[]{:S(2)}, u32[]{:S(2)}) collective-permute-start(bf16[2,256,384]{2,1,0:T(8,128)(2,1)S(1)} %get-tuple-element.241), channel_id=1, source_target_pairs={{0,24},{4,28},{8,16},{12,20},{16,8},{20,12},{24,0},{28,4},{1,25},{... | collective-permute-start | bytes 1179656 | tf_op jit(solution)/shard_map/ppermute | solution.py:334
  179.7 26.5 %collective-permute-start.30 = (bf16[128,2048]{1,0:T(8,128)(2,1)S(1)}, bf16[128,2048]{1,0:T(8,128)(2,1)S(1)}, u32[]{:S(2)}, u32[]{:S(2)}) collective-permute-start(bf16[128,2048]{1,0:T(8,128)(2,1)S(1)} %get-tuple-element.288.refs_2_), channel_id=1, source_target_pairs={{0,3},{1,2},{2,1},{3,0},{4,7},{5,6},{6,5},{7,4},{8,11},{9,10},{10,... | collective-permute-start | bytes 1572872 | tf_op jit(solution)/shard_map/ppermute | solution.py:334
  180.5 27.9 %collective-permute-start.29 = (bf16[128,2048]{1,0:T(8,128)(2,1)S(1)}, bf16[128,2048]{1,0:T(8,128)(2,1)S(1)}, u32[]{:S(2)}, u32[]{:S(2)}) collective-permute-start(bf16[128,2048]{1,0:T(8,128)(2,1)S(1)} %get-tuple-element.288.refs_2_), channel_id=1, source_target_pairs={{0,2},{1,3},{2,0},{3,1},{4,6},{5,7},{6,4},{7,5},{8,10},{9,11},{10,... | collective-permute-start | bytes 1572872 | tf_op jit(solution)/shard_map/ppermute | solution.py:334
  181.8 26.6 %collective-permute-start.28 = (bf16[128,2048]{1,0:T(8,128)(2,1)S(1)}, bf16[128,2048]{1,0:T(8,128)(2,1)S(1)}, u32[]{:S(2)}, u32[]{:S(2)}) collective-permute-start(bf16[128,2048]{1,0:T(8,128)(2,1)S(1)} %get-tuple-element.288.refs_2_), channel_id=1, source_target_pairs={{0,1},{1,0},{2,3},{3,2},{4,5},{5,4},{6,7},{7,6},{8,9},{9,8},{10,11... | collective-permute-start | bytes 1572872 | tf_op jit(solution)/shard_map/ppermute | solution.py:334
  204.9 34.1 %collective-permute-start.31 = (bf16[128,2048]{1,0:T(8,128)(2,1)S(1)}, bf16[128,2048]{1,0:T(8,128)(2,1)S(1)}, u32[]{:S(2)}, u32[]{:S(2)}) collective-permute-start(bf16[128,2048]{1,0:T(8,128)(2,1)S(1)} %get-tuple-element.294), channel_id=1, source_target_pairs={{0,1},{1,0},{2,3},{3,2},{4,5},{5,4},{6,7},{7,6},{8,9},{9,8},{10,11... | collective-permute-start | bytes 1572872 | tf_op jit(solution)/shard_map/ppermute | solution.py:334
  205.5 33.4 %collective-permute-start.32 = (bf16[128,2048]{1,0:T(8,128)(2,1)S(1)}, bf16[128,2048]{1,0:T(8,128)(2,1)S(1)}, u32[]{:S(2)}, u32[]{:S(2)}) collective-permute-start(bf16[128,2048]{1,0:T(8,128)(2,1)S(1)} %get-tuple-element.295), channel_id=1, source_target_pairs={{0,2},{1,3},{2,0},{3,1},{4,6},{5,7},{6,4},{7,5},{8,10},{9,11},{10,... | collective-permute-start | bytes 1572872 | tf_op jit(solution)/shard_map/ppermute | solution.py:334
  206.3 32.7 %collective-permute-start.33 = (bf16[128,2048]{1,0:T(8,128)(2,1)S(1)}, bf16[128,2048]{1,0:T(8,128)(2,1)S(1)}, u32[]{:S(2)}, u32[]{:S(2)}) collective-permute-start(bf16[128,2048]{1,0:T(8,128)(2,1)S(1)} %get-tuple-element.296), channel_id=1, source_target_pairs={{0,3},{1,2},{2,1},{3,0},{4,7},{5,6},{6,5},{7,4},{8,11},{9,10},{10,... | collective-permute-start | bytes 1572872 | tf_op jit(solution)/shard_map/ppermute | solution.py:334
  242.1 346.4 %reduce-scatter.6.cloned.1.call-start = ((), (), s32[]{:S(2)}) async-start(), calls=%async_computation.4 | async-start | bytes 5242880 | tf_op jit(solution)/shard_map/reduce_scatter | solution.py:1501
  337.2 40.5 %collective-permute-start.58 = (bf16[4,256,2048]{2,1,0:T(8,128)(2,1)S(1)}, bf16[4,256,2048]{2,1,0:T(8,128)(2,1)S(1)}, u32[]{:S(2)}, u32[]{:S(2)}) collective-permute-start(bf16[4,256,2048]{2,1,0:T(8,128)(2,1)S(1)} %copy-done.106), channel_id=1, source_target_pairs={{0,4},{4,0},{8,12},{12,8},{16,20},{20,16},{24,28},{28,24},{1,5},{5... | collective-permute-start | bytes 12582920 | tf_op jit(solution)/shard_map/ppermute | solution.py:334
  337.8 25.9 %collective-permute-start.56 = (bf16[2,64,2048]{2,1,0:T(8,128)(2,1)S(1)}, bf16[2,64,2048]{2,1,0:T(8,128)(2,1)S(1)}, u32[]{:S(2)}, u32[]{:S(2)}) collective-permute-start(bf16[2,64,2048]{2,1,0:T(8,128)(2,1)S(1)} %get-tuple-element.362), channel_id=1, source_target_pairs={{0,2},{1,3},{2,0},{3,1},{4,6},{5,7},{6,4},{7,5},{8,10},{9,11},{10,... | collective-permute-start | bytes 1572872 | tf_op jit(solution)/shard_map/ppermute | solution.py:334
  356.7 38.9 %collective-permute-start.59 = (bf16[2,2,256,384]{3,2,1,0:T(8,128)(2,1)}, bf16[2,2,256,384]{3,2,1,0:T(8,128)(2,1)S(1)}, u32[]{:S(2)}, u32[]{:S(2)}) collective-permute-start(bf16[2,2,256,384]{3,2,1,0:T(8,128)(2,1)} %get-tuple-element.371), channel_id=1, source_target_pairs={{0,8},{4,12},{8,0},{12,4},{16,24},{20,28},{24,16},{28,20},{1,9},{5... | collective-permute-start | bytes 2359304 | tf_op jit(solution)/shard_map/ppermute | solution.py:334
  361.3 55.2 %collective-permute-start.60 = (bf16[2,2,256,384]{3,2,1,0:T(8,128)(2,1)}, bf16[2,2,256,384]{3,2,1,0:T(8,128)(2,1)S(1)}, u32[]{:S(2)}, u32[]{:S(2)}) collective-permute-start(bf16[2,2,256,384]{3,2,1,0:T(8,128)(2,1)} %get-tuple-element.372), channel_id=1, source_target_pairs={{0,16},{4,20},{8,24},{12,28},{16,0},{20,4},{24,8},{28,12},{1,17},{... | collective-permute-start | bytes 2359304 | tf_op jit(solution)/shard_map/ppermute | solution.py:334
  362.1 54.4 %collective-permute-start.61 = (bf16[2,2,256,384]{3,2,1,0:T(8,128)(2,1)}, bf16[2,2,256,384]{3,2,1,0:T(8,128)(2,1)S(1)}, u32[]{:S(2)}, u32[]{:S(2)}) collective-permute-start(bf16[2,2,256,384]{3,2,1,0:T(8,128)(2,1)} %get-tuple-element.373), channel_id=1, source_target_pairs={{0,24},{4,28},{8,16},{12,20},{16,8},{20,12},{24,0},{28,4},{1,25},{... | collective-permute-start | bytes 2359304 | tf_op jit(solution)/shard_map/ppermute | solution.py:334
  419.5 171.7 %reduce-scatter.8.cloned.1.call-start = ((), (), s32[]{:S(2)}) async-start(), calls=%async_computation.5 | async-start | bytes 5242880 | tf_op jit(solution)/shard_map/reduce_scatter | solution.py:1501
  520.4 56.7 %collective-permute-start.72 = (bf16[2,2,64,2048]{3,2,1,0:T(8,128)(2,1)}, bf16[2,2,64,2048]{3,2,1,0:T(8,128)(2,1)}, u32[]{:S(2)}, u32[]{:S(2)}) collective-permute-start(bf16[2,2,64,2048]{3,2,1,0:T(8,128)(2,1)} %copy-done.68), channel_id=1, source_target_pairs={{0,2},{1,3},{2,0},{3,1},{4,6},{5,7},{6,4},{7,5},{8,10},{9,11},{10,... | collective-permute-start | bytes 3145736 | tf_op jit(solution)/shard_map/ppermute | solution.py:334
  522.2 54.9 %collective-permute-start.73 = (bf16[2,2,64,2048]{3,2,1,0:T(8,128)(2,1)}, bf16[2,2,64,2048]{3,2,1,0:T(8,128)(2,1)}, u32[]{:S(2)}, u32[]{:S(2)}) collective-permute-start(bf16[2,2,64,2048]{3,2,1,0:T(8,128)(2,1)} %copy-done.67), channel_id=1, source_target_pairs={{0,1},{1,0},{2,3},{3,2},{4,5},{5,4},{6,7},{7,6},{8,9},{9,8},{10,11... | collective-permute-start | bytes 3145736 | tf_op jit(solution)/shard_map/ppermute | solution.py:334
  533.8 49.5 %collective-permute-start.74 = (bf16[2,2,64,2048]{3,2,1,0:T(8,128)(2,1)}, bf16[2,2,64,2048]{3,2,1,0:T(8,128)(2,1)}, u32[]{:S(2)}, u32[]{:S(2)}) collective-permute-start(bf16[2,2,64,2048]{3,2,1,0:T(8,128)(2,1)} %get-tuple-element.416), channel_id=1, source_target_pairs={{0,2},{1,3},{2,0},{3,1},{4,6},{5,7},{6,4},{7,5},{8,10},{9,11},{10,... | collective-permute-start | bytes 3145736 | tf_op jit(solution)/shard_map/ppermute | solution.py:334
  534.1 49.2 %collective-permute-start.75 = (bf16[2,2,64,2048]{3,2,1,0:T(8,128)(2,1)}, bf16[2,2,64,2048]{3,2,1,0:T(8,128)(2,1)}, u32[]{:S(2)}, u32[]{:S(2)}) collective-permute-start(bf16[2,2,64,2048]{3,2,1,0:T(8,128)(2,1)} %get-tuple-element.417), channel_id=1, source_target_pairs={{0,1},{1,0},{2,3},{3,2},{4,5},{5,4},{6,7},{7,6},{8,9},{9,8},{10,11... | collective-permute-start | bytes 3145736 | tf_op jit(solution)/shard_map/ppermute | solution.py:334
  534.6 38.3 %collective-permute-start.79 = (f32[4,256]{1,0:T(4,128)S(1)}, f32[4,256]{1,0:T(4,128)S(1)}, u32[]{:S(2)}, u32[]{:S(2)}) collective-permute-start(f32[4,256]{1,0:T(4,128)S(1)} %slice_bitcast_fusion.4), channel_id=1, source_target_pairs={{0,1},{1,0},{2,3},{3,2},{4,5},{5,4},{6,7},{7,6},{8,9},{9,8},{10,11... | collective-permute-start | bytes 12296 | tf_op jit(solution)/shard_map/ppermute | solution.py:334
  (175 other events, 2281.7 us)
Sparse Core Ops, SparseCore 0:
  242.2 106.0 reduce-scatter.3
  419.6 90.5 reduce-scatter.5
  512.6 77.2 reduce-scatter.7

commit v6 on v5

--- a/solution.py
+++ b/solution.py
@@ -651,21 +651,36 @@
     heads = inner // HD
 
     def body(here_ref, x_ref, gain_ref, shift_ref, weight_hbm, bias_ref, *rest):
-        norm_ref, outs, (held, weight_ref, x_held, sems) = rest[0], rest[1:6], rest[6:]
-        fetch = pltpu.make_async_copy(x_ref.at[index], x_held, sems.at[3])
-        fetch.start()
+        norm_ref, outs = rest[0], rest[1:6]
+        held, weight_ref, x_held, gain_held, shift_held, bias_held, sems = rest[6:]
+        fetches = [
+            pltpu.make_async_copy(source, target, sems.at[3 + number])
+            for number, (source, target) in enumerate(
+                (
+                    (x_ref.at[index], x_held),
+                    (gain_ref, gain_held),
+                    (shift_ref, shift_held),
+                    (bias_ref, bias_held),
+                )
+            )
+        ]
+        for fetch in fetches:
+            fetch.start()
         copies = [
             pltpu.make_async_copy(weight_hbm.at[part], weight_ref.at[part], sems.at[part])
             for part in range(3)
         ]
         for copy in copies:
             copy.start()
-        fetch.wait()
+        for fetch in fetches:
+            fetch.wait()
         unit, _ = normalized(x_held[...].astype(F32))
-        norm_ref[...] = (unit * gain_ref[...] + shift_ref[...]).astype(BF)
+        norm_ref[...] = (unit * gain_held[...] + shift_held[...]).astype(BF)
         for part in range(3):
             copies[part].wait()
-            value = dot(norm_ref[...], weight_ref[part]) + bias_ref[part : part + 1]
+            value = dot(norm_ref[...], weight_ref[part])
+            if part != 1:
+                value += bias_held[part // 2 : part // 2 + 1]
             value = value.astype(BF)
             for head in range(heads):
                 held[head, :, part * HD : (part + 1) * HD] = value[:, head * HD : (head + 1) * HD]
@@ -684,12 +699,15 @@
             pltpu.VMEM((heads, rows, 3 * HD), BF),
             pltpu.VMEM(weight.shape, BF),
             pltpu.VMEM((rows, width), BF),
-            pltpu.SemaphoreType.DMA((4,)),
+            pltpu.VMEM(gain.shape, F32),
+            pltpu.VMEM(shift.shape, F32),
+            pltpu.VMEM(bias.shape, F32),
+            pltpu.SemaphoreType.DMA((7,)),
         ],
         name="project",
         limit=14,
         after=after,
-        in_hbm=(1, 4),
+        in_hbm=(1, 2, 3, 4, 5),
     )
 
 
@@ -924,7 +942,9 @@
     )
 
 
-def feed_inner(tp_here, pieces, cot, up_weight, up_bias, down_weight, with_grad, after=()):
+def feed_inner(
+    tp_here, pieces, cot, up_weight, up_bias, down_weight, earlier, index, with_grad, after=()
+):
     rows, width = cot.shape
     hidden = up_weight.shape[1]
     size = rows // 4
@@ -934,8 +954,10 @@
     def body(tp_ref, *rest):
         refs, rest = rest[: len(pieces)], rest[len(pieces) :]
         cot_ref, up_hbm, bias_ref, down_hbm = rest[:4]
-        norm_ref, act_ref, pre_ref, sum_ref, cot_sum_ref = rest[4:9]
-        grad_outs = rest[9:13] if with_grad else ()
+        rest = rest[4 + len(earlier) :]
+        norm_ref, act_ref, pre_ref = [ref.at[0] for ref in rest[:3]]
+        sum_ref, cot_sum_ref = rest[3:5]
+        grad_outs = rest[5:9] if with_grad else ()
         up, down, held, sems = rest[-4:]
 
         def part(number):
@@ -982,22 +1004,20 @@
             emit_messages(lambda at: held[at, :], tp_ref[0], grad_outs, size)
 
     args = [tp_here, *pieces, cot, up_weight, up_bias, down_weight]
-    outs = [
-        sds((rows, width)),
-        sds((rows, hidden)),
-        sds((rows, hidden)),
-        sds((1, hidden), F32),
-        sds((1, width), F32),
-    ] + (message_shapes(size // 2, width, True) if with_grad else [])
+    count = cot.array.shape[0]
+    wide = [(1, rows, width), (1, rows, hidden), (1, rows, hidden)]
+    outs = [sds((1, hidden), F32), sds((1, width), F32)]
+    outs += message_shapes(size // 2, width, True) if with_grad else []
     return launch(
         body,
-        operands_of(args),
+        operands_of(args) + list(earlier),
         [pl.BlockSpec(memory_space=pltpu.SMEM)]
         + [whole_of(piece.shape) for piece in pieces]
         + [cot.spec(), pl.BlockSpec(memory_space=HBM), whole_of(up_bias.shape)]
-        + [pl.BlockSpec(memory_space=HBM)],
-        outs,
-        [whole_of(item.shape) for item in outs],
+        + [pl.BlockSpec(memory_space=HBM)] * (1 + len(earlier)),
+        [HBM((count,) + shape[1:], BF) for shape in wide] + outs,
+        [pl.BlockSpec(shape, lambda i: (index, 0, 0)) for shape in wide]
+        + [whole_of(item.shape) for item in outs],
         [
             pltpu.VMEM((width, hidden), BF),
             pltpu.VMEM((hidden, width), BF),
@@ -1009,7 +1029,12 @@
         "feed_inner",
         after,
         grid=(1,),
-    )
+        aliases={len(args) + number: number for number in range(len(earlier))},
+    )
+
+
+def stacked(array):
+    return array.reshape((-1, array.shape[-1]))
 
 
 def feed_grad(tp_here, grad_pre, up_weight, after=()):
@@ -1035,7 +1060,7 @@
         operands_of([tp_here, grad_pre, up_weight]),
         [
             pl.BlockSpec(memory_space=pltpu.SMEM),
-            whole_of(grad_pre.shape),
+            grad_pre.spec(),
             pl.BlockSpec((step, hidden), lambda i: (i, 0)),
         ],
         outs,
@@ -1079,7 +1104,7 @@
         body,
         operands_of([tp_here, *acts, down_weight]),
         [pl.BlockSpec(memory_space=pltpu.SMEM)]
-        + [whole_of(act.shape) for act in acts]
+        + [act.spec() for act in acts]
         + [pl.BlockSpec((hidden, step), lambda i: (0, i))],
         outs,
         [whole_of(item.shape) for item in outs],
@@ -1225,13 +1250,19 @@
             proj_ref[number] = part_ref[:, place].astype(F32)
         mixer_ref[...] = part_ref[:, 3 * inner :].astype(F32).T
 
-    return run_kernel(
-        body,
-        [sds((3, rows, inner), F32), sds((inner, rows), F32)],
-        [part],
-        after=after,
-        name="widen",
-        limit=6,
+    outs = [sds((3, rows, inner), F32), sds((inner, rows), F32)]
+    return launch(
+        body,
+        operands_of([part]),
+        [whole_of(part.shape)],
+        outs,
+        [whole_of(item.shape) for item in outs],
+        (),
+        16 << 20,
+        cost(0, 16 * rows * inner),
+        "widen",
+        after,
+        grid=(1,),
     )
 
 
@@ -1472,7 +1503,6 @@
     here = lax.axis_index("ctx").astype(jnp.int32).reshape(1)
     tp_here = lax.axis_index("tp").astype(jnp.int32).reshape(1)
     weight_three = jnp.transpose(proj_weight, (1, 0, 2))
-    bias_three = jnp.stack([proj_bias[0], jnp.zeros_like(proj_bias[0]), proj_bias[1]])
     x_all = inputs.reshape(micro_count, rows, width)
     cot_all = out_cotangent.reshape(micro_count, rows, width)
     key_rows = jnp.where(keep_mask > 0, segments, -1)[:, :, None, :]
@@ -1510,7 +1540,7 @@
 
     def project_micro(index, done):
         (normed, *sent), done = project(
-            here, x_all, index, gain_one, shift_one, weight_three, bias_three, tok_len, after=done
+            here, x_all, index, gain_one, shift_one, weight_three, proj_bias, tok_len, after=done
         )
         norm_one.append(normed)
         return exchange_chips(*sent), done
@@ -1537,25 +1567,24 @@
         resids.append(resid)
         return shard if direct else gather_first(shard), done
 
-    norm_two, acts, grad_pres, up_sums, cot_sums = [], [], [], [], []
-
-    def feed_micro(index, pieces, with_grad, done):
-        (normed, act, grad_pre, up_sum, cot_sum, *messages), done = feed_inner(
+    up_sums, cot_sums = [], []
+
+    def feed_micro(index, pieces, earlier, with_grad, done):
+        (norms, acts, pres, up_sum, cot_sum, *messages), done = feed_inner(
             tp_here,
             pieces,
             cots[index],
             up_weight,
             high_bias,
             down_weight,
+            earlier,
+            index,
             with_grad,
             after=done,
         )
-        norm_two.append(normed)
-        acts.append(act)
-        grad_pres.append(grad_pre)
         up_sums.append(up_sum)
         cot_sums.append(cot_sum)
-        return messages, done
+        return (norms, acts, pres), messages, done
 
     grad_resids, gain_twos, shift_twos = [], [], []
     grad_mixes, mix_sums, states = [], [], []
@@ -1610,29 +1639,32 @@
     sums_b, done = reduce_second(state_b, done)
     state_b, done = norm_micro(1, sums_b, True, done)
     pieces_b = gather_direct(state_b[0])
-    messages, done = feed_micro(0, pieces_a, True, done)
+    kept, messages, done = feed_micro(0, pieces_a, (), True, done)
     sums_a = reduce_direct(messages)
-    _, done = feed_micro(1, pieces_b, False, done)
-    (down_part,), done = weight_grad([(cots, acts)], after=done)
+    (norm_two, acts, grad_pres), _, done = feed_micro(1, pieces_b, kept, False, done)
+    (down_part,), done = weight_grad([([stacked(cot_all)], [stacked(acts)])], after=done)
     state_a, done = norm_back_micro(0, sums_a, done)
     down_grad = scattered(until(down_part, done))
-    messages, done = feed_grad(tp_here, grad_pres[1], up_weight, after=done)
+    messages, done = feed_grad(tp_here, Part(grad_pres, 1), up_weight, after=done)
     state_b = reduce_first(messages)
     pieces_a, done = gather_second(state_a, done)
+    acts = [Part(acts, index) for index in micro]
     feeds, done = feed_out(tp_here, acts, down_weight, after=done)
     sums_b, done = reduce_second(state_b, done)
     done = heads_back_micro(0, pieces_a, done)
     state_b, done = norm_back_micro(1, sums_b, done)
     pieces_b, done = gather_second(state_b, done)
-    (sent, own), done = weight_grad([(norm_two, grad_pres)], here, after=done)
+    (sent, own), done = weight_grad(
+        [([stacked(norm_two)], [stacked(grad_pres)])], here, after=done
+    )
     got_a, done = exchange_cores(states[0], done)
     done = heads_back_micro(1, pieces_b, done)
     state_feed = reduce_first(until(feeds, done))
     sent_back, done = attend_back_micro(0, got_a, [], done)
     got_b, done = exchange_cores(states[1], done)
     sums_feed, done = reduce_second(state_feed, done)
+    sent_back, done = attend_back_micro(1, got_b, sent_back, done)
     got_up = xor_permute(until(sent, done), "ctx", 1)
-    sent_back, done = attend_back_micro(1, got_b, sent_back, done)
     state_back = exchange_chips(*sent_back)
     halves, done = finish_outputs(sums_feed, resids, low_bias, after=done)
     (up_part,), done = add_halves(own, got_up, after=done)

time: 611 us -> 597 us (0.977)
  waiting for transfers between devices: 214 us -> 204 us
  local copies, waits for them, and re-layouts: 53.8 us -> 44.6 us
    ppermute x81, waiting for transfers between devices: 214 us -> 203 us  [xor_permute(): return lax.ppermute(values, axis, [(i, i ^ step) for i in range(count)])]
    unnamed x230 -> x202, local copies, waits for them, and re-layouts: 47.4 us -> 39 us
  transfers between devices with their start and end apart: 84 -> 84, of which waited for: 33 -> 36; matrix products, arithmetic and copies ran while one was open for 1% -> 1% of each run, Pallas kernels for 31% -> 32%
where the time goes in v6:
time: 597 us; the launch traced here: 588 us
  waiting for transfers between devices  204 us (34%)
  Pallas kernels  202 us (34%)
  starting transfers between devices  121 us (20%)
  local copies, waits for them, and re-layouts  44.6 us (7%)
  between operations  15.5 us (3%)
    ppermute x81, waiting for transfers between devices, xor_permute(): return lax.ppermute(values, axis, [(i, i ^ step) for i in range(count)])  203 us
    pallas_call x48, Pallas kernels, launch(): pl.pallas_call(inner, grid_spec=pltpu.PrefetchScalarGridSpec(num_scalar_p...  202 us
    ppermute x81, starting transfers between devices, xor_permute(): return lax.ppermute(values, axis, [(i, i ^ step) for i in range(count)])  121 us
    unnamed x202, local copies, waits for them, and re-layouts  39 us
  transfers between devices with their start and end apart: 84, of which 36 were waited for; matrix products, arithmetic and copies ran while one was open for 1% of the time, Pallas kernels for 32%

profile of v6, /device:TPU:0, one launch (start us, length us, event | category | flops | bytes accessed | tf_op | source)
XLA Modules:
  0.0 587.8 jit_solution(8600547304509237745)
XLA Ops:
  7.2 6.9 %project.2 = (bf16[512,2048]{1,0:T(8,128)(2,1)S(1)}, bf16[256,384]{1,0:T(8,128)(2,1)S(1)}, bf16[256,384]{1,0:T(8,128)(2,1)S(1)}, bf16[2,256,384]{2,1,0:T(8,128)(...) custom-call(s32[1]{0:T(128)} %bitcast.refs_0_.refs_1_, ...), custom_call_target="tpu_custom_call" | custom-call | flops 3221225472 | bytes 3670016 | tf_op jit(solution)/shard_map/project/pallas_call | solution.py:374
  21.1 6.9 %project.3 = (bf16[512,2048]{1,0:T(8,128)(2,1)S(1)}, bf16[256,384]{1,0:T(8,128)(2,1)S(1)}, bf16[256,384]{1,0:T(8,128)(2,1)S(1)}, bf16[2,256,384]{2,1,0:T(8,128)(...) custom-call(f32[8,128]{1,0:T(8,128)S(1)} %get-tuple-element.228.refs_0_, ...), custom_call_target="tpu_custom_call" | custom-call | flops 3221225472 | bytes 3670016 | tf_op jit(solution)/shard_map/project/pallas_call | solution.py:374
  40.7 7.6 %collective-permute-done.1.refs_3_.refs_4_ = bf16[2,256,384]{2,1,0:T(8,128)(2,1)S(1)} collective-permute-done((bf16[2,256,384]{2,1,0:T(8,128)(2,1)S(1)}, bf16[2,256,384]{2,1,0:T(8,128)(2,1)S(1)}, u32[]{:S(2)}, u32[]{:S(2)}) %collective-permute-start.1) | collective-permute-done | bytes 393248 | tf_op jit(solution)/shard_map/ppermute | solution.py:334
  58.1 23.9 %collective-permute-done.5.refs_3_.refs_4_ = bf16[2,256,384]{2,1,0:T(8,128)(2,1)S(1)} collective-permute-done((bf16[2,256,384]{2,1,0:T(8,128)(2,1)S(1)}, bf16[2,256,384]{2,1,0:T(8,128)(2,1)S(1)}, u32[]{:S(2)}, u32[]{:S(2)}) %collective-permute-start.5) | collective-permute-done | bytes 393248 | tf_op jit(solution)/shard_map/ppermute | solution.py:334
  82.3 7.6 %collective-permute-start.8 = (bf16[2,256,128]{2,1,0:T(8,128)(2,1)S(1)}, bf16[2,256,128]{2,1,0:T(8,128)(2,1)S(1)}, u32[]{:S(2)}, u32[]{:S(2)}) collective-permute-start(bf16[2,256,128]{2,1,0:T(8,128)(2,1)S(1)} %get-tuple-element.247), channel_id=1, source_target_pairs={{0,8},{4,12},{8,0},{12,4},{16,24},{20,28},{24,16},{28,20},{1,9},{5... | collective-permute-start | bytes 393224 | tf_op jit(solution)/shard_map/ppermute | solution.py:334
  92.4 6.7 %attention.3 = (bf16[256,128]{1,0:T(8,128)(2,1)S(1)}, bf16[256,128]{1,0:T(8,128)(2,1)S(1)}, bf16[2,256,128]{2,1,0:T(8,128)(2,1)}, bf16[2,256,128]{2,1,0:T(8,128)...) custom-call(f32[8,128]{1,0:T(8,128)S(1)} %get-tuple-element.242.refs_0_, ...), custom_call_target="tpu_custom_call" | custom-call | flops 2147483648 | bytes 2727936 | tf_op jit(solution)/shard_map/attention/pallas_call | solution.py:374
  137.9 13.6 %collective-permute-done.20.refs_2_.refs_3_ = bf16[64,2048]{1,0:T(8,128)(2,1)S(1)} collective-permute-done((bf16[64,2048]{1,0:T(8,128)(2,1)S(1)}, bf16[64,2048]{1,0:T(8,128)(2,1)S(1)}, u32[]{:S(2)}, u32[]{:S(2)}) %collective-permute-start.20) | collective-permute-done | bytes 262176 | tf_op jit(solution)/shard_map/ppermute | solution.py:334
  159.3 11.4 %collective-permute-done.24.refs_2_ = bf16[64,2048]{1,0:T(8,128)(2,1)S(1)} collective-permute-done((bf16[64,2048]{1,0:T(8,128)(2,1)S(1)}, bf16[64,2048]{1,0:T(8,128)(2,1)S(1)}, u32[]{:S(2)}, u32[]{:S(2)}) %collective-permute-start.24) | collective-permute-done | bytes 262176 | tf_op jit(solution)/shard_map/ppermute | solution.py:334
  177.8 20.7 %feed_inner.2 = (bf16[2,512,2048]{2,1,0:T(8,128)(2,1)}, bf16[2,512,2048]{2,1,0:T(8,128)(2,1)}, bf16[2,512,2048]{2,1,0:T(8,128)(2,1)}, f32[1,2048]{1,0:T(1,128)S(...) custom-call(f32[8,128]{1,0:T(8,128)S(1)} %get-tuple-element.284.refs, ...), custom_call_target="tpu_custom_call" | custom-call | flops 12884901888 | bytes 37748736 | tf_op jit(solution)/shard_map/feed_inner/pallas_call | solution.py:374
  203.0 15.3 %feed_inner.3 = (bf16[2,512,2048]{2,1,0:T(8,128)(2,1)}, bf16[2,512,2048]{2,1,0:T(8,128)(2,1)}, bf16[2,512,2048]{2,1,0:T(8,128)(2,1)}, f32[1,2048]{1,0:T(1,128)S(...) custom-call(f32[8,128]{1,0:T(8,128)S(1)} %get-tuple-element.287.refs, ...), custom_call_target="tpu_custom_call", output_to_operand_aliasing={{0}: (10, {}), {1}: (11, {}), {2}: (12, {})} | custom-call | flops 12884901888 | bytes 37748736 | tf_op jit(solution)/shard_map/feed_inner/pallas_call | solution.py:374
  218.3 13.4 %weight_grad.3 = (bf16[2048,2048]{1,0:T(8,128)(2,1)}, f32[8,128]{1,0:T(8,128)S(1)}) custom-call(f32[8,128]{1,0:T(8,128)S(1)} %get-tuple-element.292.refs_0_, bf16[1024,2048]{1,0:T(8,128)(2,1)} %bitcast.90, bf16[1024,2048]{1,0:T(8,128)(2,1)} %bitcast.114), custom_call_target="tpu_custom_call" | custom-call | flops 8589934592 | bytes 16777216 | tf_op jit(solution)/shard_map/weight_grad/pallas_call | solution.py:374
  236.6 8.2 %feed_grad.1 = (bf16[2,64,2048]{2,1,0:T(8,128)(2,1)S(1)}, bf16[2,64,2048]{2,1,0:T(8,128)(2,1)S(1)}, bf16[2,64,2048]{2,1,0:T(8,128)(2,1)S(1)}, bf16[2,64,2048]{2,1,0:T(8,128)(2,1)S(1)}, f32[8,128]{1,0:T(8,128)S(1)}) custom-call(f32[8,128]{1,0:T(8,128)S(1)} %get-tuple-element.300.refs_0_, s32[1]{0:T(128)} %bitcast.9.refs_2_.refs_1_, ...), custom_call_target="tpu_custom_call" | custom-call | flops 4294967296 | bytes 14680064 | tf_op jit(solution)/shard_map/feed_grad/pallas_call | solution.py:374
  249.1 12.6 %feed_out.1 = (bf16[2,2,64,2048]{3,2,1,0:T(8,128)(2,1)S(1)}, bf16[2,2,64,2048]{3,2,1,0:T(8,128)(2,1)S(1)}, bf16[2,2,64,2048]{3,2,1,0:T(8,128)(2,1)S(1)}, bf16[2,...) custom-call(f32[8,128]{1,0:T(8,128)S(1)} %get-tuple-element.305.refs_0_, s32[1]{0:T(128)} %bitcast.9.refs_2_.refs_1_, ...), custom_call_target="tpu_custom_call" | custom-call | flops 8589934592 | bytes 20971520 | tf_op jit(solution)/shard_map/feed_out/pallas_call | solution.py:374
  287.6 14.7 %weight_grad.4 = (bf16[4,256,2048]{2,1,0:T(8,128)(2,1)}, bf16[4,256,2048]{2,1,0:T(8,128)(2,1)}, f32[8,128]{1,0:T(8,128)S(1)}) custom-call(s32[1]{0:T(128)} %bitcast.refs_0_.refs_1_, f32[8,128]{1,0:T(8,128)S(1)} %get-tuple-element.323.refs_1_, bf16[1024,2048]{1,0:T(8,128)(2,1)} %bitcast.113, bf16[1024,2048]{1,0:T(8,128)(2,1)} %bitcast.115), custom_call_target="tpu_custom_call" | custom-call | flops 8589934592 | bytes 16777216 | tf_op jit(solution)/shard_map/weight_grad/pallas_call | solution.py:374
  311.2 9.9 %attention_back.2 = (bf16[2,256,384]{2,1,0:T(8,128)(2,1)S(1)}, bf16[2,256,384]{2,1,0:T(8,128)(2,1)S(1)}, bf16[2,2,256,384]{3,2,1,0:T(8,128)(2,1)S(1)}, bf16[2,2,...) custom-call(f32[8,128]{1,0:T(8,128)S(1)} %get-tuple-element.333.refs_0_, ...), custom_call_target="tpu_custom_call" | custom-call | flops 2684354560 | bytes 3145728 | tf_op jit(solution)/shard_map/attention_back/pallas_call | solution.py:374
  331.8 11.3 %attention_back.3 = (bf16[2,256,384]{2,1,0:T(8,128)(2,1)}, bf16[2,256,384]{2,1,0:T(8,128)(2,1)}, bf16[2,2,256,384]{3,2,1,0:T(8,128)(2,1)}, bf16[2,2,256,384]{3,2...) custom-call(f32[8,128]{1,0:T(8,128)S(1)} %get-tuple-element.351.refs, ...), custom_call_target="tpu_custom_call", output_to_operand_aliasing={{0}: (15, {}), {1}: (16, {}), {2}: (17, {}), {3}: (18, {}),... | custom-call | flops 2684354560 | bytes 3145728 | tf_op jit(solution)/shard_map/attention_back/pallas_call | solution.py:374
  350.6 6.8 %collective-permute-done.56.refs_2_ = bf16[2,64,2048]{2,1,0:T(8,128)(2,1)S(1)} collective-permute-done((bf16[2,64,2048]{2,1,0:T(8,128)(2,1)S(1)}, bf16[2,64,2048]{2,1,0:T(8,128)(2,1)S(1)}, u32[]{:S(2)}, u32[]{:S(2)}) %collective-permute-start.56) | collective-permute-done | bytes 524320 | tf_op jit(solution)/shard_map/ppermute | solution.py:334
  359.2 11.6 %collective-permute-done.57.refs_4_ = bf16[2,64,2048]{2,1,0:T(8,128)(2,1)S(1)} collective-permute-done((bf16[2,64,2048]{2,1,0:T(8,128)(2,1)S(1)}, bf16[2,64,2048]{2,1,0:T(8,128)(2,1)S(1)}, u32[]{:S(2)}, u32[]{:S(2)}) %collective-permute-start.57) | collective-permute-done | bytes 524320 | tf_op jit(solution)/shard_map/ppermute | solution.py:334
  382.2 20.8 %collective-permute-done.60.refs_3_.refs_5_ = bf16[2,2,256,384]{3,2,1,0:T(8,128)(2,1)S(1)} collective-permute-done((bf16[2,2,256,384]{3,2,1,0:T(8,128)(2,1)}, bf16[2,2,256,384]{3,2,1,0:T(8,128)(2,1)S(1)}, u32[]{:S(2)}, u32[]{:S(2)}) %collective-permute-start.60) | collective-permute-done | bytes 786464 | tf_op jit(solution)/shard_map/ppermute | solution.py:334
  415.7 7.7 %project_back.1 = (bf16[512,1536]{1,0:T(8,128)(2,1)S(1)}, bf16[512,1536]{1,0:T(8,128)(2,1)S(1)}, f32[1,1536]{1,0:T(1,128)S(1)}, bf16[2,2,64,2048]{3,2,1,0:T(8,12...) custom-call(f32[8,128]{1,0:T(8,128)S(1)} %get-tuple-element.374.refs, ...), custom_call_target="tpu_custom_call" | custom-call | flops 6442450944 | bytes 17963008 | tf_op jit(solution)/shard_map/project_back/pallas_call | solution.py:374
  428.8 15.5 %weight_grad.5 = (bf16[4,256,2048]{2,1,0:T(8,128)(2,1)}, bf16[4,256,2048]{2,1,0:T(8,128)(2,1)}, f32[8,128]{1,0:T(8,128)S(1)}) custom-call(s32[1]{0:T(128)} %bitcast.refs_0_.refs_1_, f32[8,128]{1,0:T(8,128)S(1)} %get-tuple-element.377.refs_1_, bf16[512,2048]{1,0:T(8,128)(2,1)} %copy-done.75, bf16[512,2048]{1,0:T(8,128)(2,1)} %copy-done.74, ...), custom_call_target="tpu_custom_call" | custom-call | flops 8589934592 | bytes 20971520 | tf_op jit(solution)/shard_map/weight_grad/pallas_call | solution.py:374
  456.8 10.7 %collective-permute-done.65.refs_2_.refs_3_ = bf16[2,64,2048]{2,1,0:T(8,128)(2,1)S(1)} collective-permute-done((bf16[2,64,2048]{2,1,0:T(8,128)(2,1)S(1)}, bf16[2,64,2048]{2,1,0:T(8,128)(2,1)S(1)}, u32[]{:S(2)}, u32[]{:S(2)}) %collective-permute-start.65) | collective-permute-done | bytes 524320 | tf_op jit(solution)/shard_map/ppermute | solution.py:334
  482.6 18.4 %collective-permute-start.76 = (f32[4,8,256]{2,1,0:T(8,128)S(1)}, f32[4,8,256]{2,1,0:T(8,128)S(1)}, u32[]{:S(2)}, u32[]{:S(2)}) collective-permute-start(f32[4,8,256]{2,1,0:T(8,128)S(1)} %dynamic-slice_bitcast_fusion.4), channel_id=1, source_target_pairs={{0,16},{4,20},{8,24},{12,28},{16,0},{20,4},{24,8},{28,12},{1,17},{... | collective-permute-start | bytes 98312 | tf_op jit(solution)/shard_map/ppermute | solution.py:334
  524.4 34.7 %collective-permute-done.79 = f32[4,256]{1,0:T(4,128)S(1)} collective-permute-done((f32[4,256]{1,0:T(4,128)S(1)}, f32[4,256]{1,0:T(4,128)S(1)}, u32[]{:S(2)}, u32[]{:S(2)}) %collective-permute-start.79) | collective-permute-done | bytes 4128 | tf_op jit(solution)/shard_map/ppermute | solution.py:334
  (425 shorter events, 255.4 us)
Async XLA Ops:
  7.2 559.5 %reduce-scatter.4.cloned.1.call-start = ((), (), s32[]{:S(2)}) async-start(), calls=%async_computation.3 | async-start | bytes 9437184 | tf_op jit(solution)/shard_map/reduce_scatter | solution.py:1527
  18.5 29.8 %collective-permute-start.1 = (bf16[2,256,384]{2,1,0:T(8,128)(2,1)S(1)}, bf16[2,256,384]{2,1,0:T(8,128)(2,1)S(1)}, u32[]{:S(2)}, u32[]{:S(2)}) collective-permute-start(bf16[2,256,384]{2,1,0:T(8,128)(2,1)S(1)} %get-tuple-element.232), channel_id=1, source_target_pairs={{0,16},{4,20},{8,24},{12,28},{16,0},{20,4},{24,8},{28,12},{1,17},{... | collective-permute-start | bytes 1179656 | tf_op jit(solution)/shard_map/ppermute | solution.py:334
  21.1 27.3 %collective-permute-start.2 = (bf16[2,256,384]{2,1,0:T(8,128)(2,1)S(1)}, bf16[2,256,384]{2,1,0:T(8,128)(2,1)S(1)}, u32[]{:S(2)}, u32[]{:S(2)}) collective-permute-start(bf16[2,256,384]{2,1,0:T(8,128)(2,1)S(1)} %get-tuple-element.233), channel_id=1, source_target_pairs={{0,24},{4,28},{8,16},{12,20},{16,8},{20,12},{24,0},{28,4},{1,25},{... | collective-permute-start | bytes 1179656 | tf_op jit(solution)/shard_map/ppermute | solution.py:334
  28.1 30.0 %collective-permute-start.4 = (bf16[2,256,384]{2,1,0:T(8,128)(2,1)S(1)}, bf16[2,256,384]{2,1,0:T(8,128)(2,1)S(1)}, u32[]{:S(2)}, u32[]{:S(2)}) collective-permute-start(bf16[2,256,384]{2,1,0:T(8,128)(2,1)S(1)} %get-tuple-element.239), channel_id=1, source_target_pairs={{0,8},{4,12},{8,0},{12,4},{16,24},{20,28},{24,16},{28,20},{1,9},{5... | collective-permute-start | bytes 1179656 | tf_op jit(solution)/shard_map/ppermute | solution.py:334
  29.0 53.0 %collective-permute-start.5 = (bf16[2,256,384]{2,1,0:T(8,128)(2,1)S(1)}, bf16[2,256,384]{2,1,0:T(8,128)(2,1)S(1)}, u32[]{:S(2)}, u32[]{:S(2)}) collective-permute-start(bf16[2,256,384]{2,1,0:T(8,128)(2,1)S(1)} %get-tuple-element.240), channel_id=1, source_target_pairs={{0,16},{4,20},{8,24},{12,28},{16,0},{20,4},{24,8},{28,12},{1,17},{... | collective-permute-start | bytes 1179656 | tf_op jit(solution)/shard_map/ppermute | solution.py:334
  36.1 45.9 %collective-permute-start.6 = (bf16[2,256,384]{2,1,0:T(8,128)(2,1)S(1)}, bf16[2,256,384]{2,1,0:T(8,128)(2,1)S(1)}, u32[]{:S(2)}, u32[]{:S(2)}) collective-permute-start(bf16[2,256,384]{2,1,0:T(8,128)(2,1)S(1)} %get-tuple-element.241), channel_id=1, source_target_pairs={{0,24},{4,28},{8,16},{12,20},{16,8},{20,12},{24,0},{28,4},{1,25},{... | collective-permute-start | bytes 1179656 | tf_op jit(solution)/shard_map/ppermute | solution.py:334
  173.3 26.5 %collective-permute-start.30 = (bf16[128,2048]{1,0:T(8,128)(2,1)S(1)}, bf16[128,2048]{1,0:T(8,128)(2,1)S(1)}, u32[]{:S(2)}, u32[]{:S(2)}) collective-permute-start(bf16[128,2048]{1,0:T(8,128)(2,1)S(1)} %get-tuple-element.288.refs_2_), channel_id=1, source_target_pairs={{0,3},{1,2},{2,1},{3,0},{4,7},{5,6},{6,5},{7,4},{8,11},{9,10},{10,... | collective-permute-start | bytes 1572872 | tf_op jit(solution)/shard_map/ppermute | solution.py:334
  174.1 27.9 %collective-permute-start.29 = (bf16[128,2048]{1,0:T(8,128)(2,1)S(1)}, bf16[128,2048]{1,0:T(8,128)(2,1)S(1)}, u32[]{:S(2)}, u32[]{:S(2)}) collective-permute-start(bf16[128,2048]{1,0:T(8,128)(2,1)S(1)} %get-tuple-element.288.refs_2_), channel_id=1, source_target_pairs={{0,2},{1,3},{2,0},{3,1},{4,6},{5,7},{6,4},{7,5},{8,10},{9,11},{10,... | collective-permute-start | bytes 1572872 | tf_op jit(solution)/shard_map/ppermute | solution.py:334
  175.4 26.6 %collective-permute-start.28 = (bf16[128,2048]{1,0:T(8,128)(2,1)S(1)}, bf16[128,2048]{1,0:T(8,128)(2,1)S(1)}, u32[]{:S(2)}, u32[]{:S(2)}) collective-permute-start(bf16[128,2048]{1,0:T(8,128)(2,1)S(1)} %get-tuple-element.288.refs_2_), channel_id=1, source_target_pairs={{0,1},{1,0},{2,3},{3,2},{4,5},{5,4},{6,7},{7,6},{8,9},{9,8},{10,11... | collective-permute-start | bytes 1572872 | tf_op jit(solution)/shard_map/ppermute | solution.py:334
  198.4 33.2 %collective-permute-start.31 = (bf16[128,2048]{1,0:T(8,128)(2,1)S(1)}, bf16[128,2048]{1,0:T(8,128)(2,1)S(1)}, u32[]{:S(2)}, u32[]{:S(2)}) collective-permute-start(bf16[128,2048]{1,0:T(8,128)(2,1)S(1)} %get-tuple-element.296), channel_id=1, source_target_pairs={{0,1},{1,0},{2,3},{3,2},{4,5},{5,4},{6,7},{7,6},{8,9},{9,8},{10,11... | collective-permute-start | bytes 1572872 | tf_op jit(solution)/shard_map/ppermute | solution.py:334
  199.1 32.5 %collective-permute-start.32 = (bf16[128,2048]{1,0:T(8,128)(2,1)S(1)}, bf16[128,2048]{1,0:T(8,128)(2,1)S(1)}, u32[]{:S(2)}, u32[]{:S(2)}) collective-permute-start(bf16[128,2048]{1,0:T(8,128)(2,1)S(1)} %get-tuple-element.297), channel_id=1, source_target_pairs={{0,2},{1,3},{2,0},{3,1},{4,6},{5,7},{6,4},{7,5},{8,10},{9,11},{10,... | collective-permute-start | bytes 1572872 | tf_op jit(solution)/shard_map/ppermute | solution.py:334
  199.8 31.8 %collective-permute-start.33 = (bf16[128,2048]{1,0:T(8,128)(2,1)S(1)}, bf16[128,2048]{1,0:T(8,128)(2,1)S(1)}, u32[]{:S(2)}, u32[]{:S(2)}) collective-permute-start(bf16[128,2048]{1,0:T(8,128)(2,1)S(1)} %get-tuple-element.298), channel_id=1, source_target_pairs={{0,3},{1,2},{2,1},{3,0},{4,7},{5,6},{6,5},{7,4},{8,11},{9,10},{10,... | collective-permute-start | bytes 1572872 | tf_op jit(solution)/shard_map/ppermute | solution.py:334
  234.8 339.9 %reduce-scatter.6.cloned.1.call-start = ((), (), s32[]{:S(2)}) async-start(), calls=%async_computation.4 | async-start | bytes 5242880 | tf_op jit(solution)/shard_map/reduce_scatter | solution.py:1531
  276.4 25.8 %collective-permute-start.44 = (bf16[2,256,128]{2,1,0:T(8,128)(2,1)S(1)}, bf16[2,256,128]{2,1,0:T(8,128)(2,1)S(1)}, u32[]{:S(2)}, u32[]{:S(2)}) collective-permute-start(bf16[2,256,128]{2,1,0:T(8,128)(2,1)S(1)} %get-tuple-element.327), channel_id=1, source_target_pairs={{0,8},{4,12},{8,0},{12,4},{16,24},{20,28},{24,16},{28,20},{1,9},{5... | collective-permute-start | bytes 393224 | tf_op jit(solution)/shard_map/ppermute | solution.py:334
  343.0 28.1 %collective-permute-start.58 = (bf16[4,256,2048]{2,1,0:T(8,128)(2,1)S(1)}, bf16[4,256,2048]{2,1,0:T(8,128)(2,1)S(1)}, u32[]{:S(2)}, u32[]{:S(2)}) collective-permute-start(bf16[4,256,2048]{2,1,0:T(8,128)(2,1)S(1)} %copy-done.92), channel_id=1, source_target_pairs={{0,4},{4,0},{8,12},{12,8},{16,20},{20,16},{24,28},{28,24},{1,5},{5... | collective-permute-start | bytes 12582920 | tf_op jit(solution)/shard_map/ppermute | solution.py:334
  343.8 38.4 %collective-permute-start.59 = (bf16[2,2,256,384]{3,2,1,0:T(8,128)(2,1)}, bf16[2,2,256,384]{3,2,1,0:T(8,128)(2,1)S(1)}, u32[]{:S(2)}, u32[]{:S(2)}) collective-permute-start(bf16[2,2,256,384]{3,2,1,0:T(8,128)(2,1)} %get-tuple-element.371), channel_id=1, source_target_pairs={{0,8},{4,12},{8,0},{12,4},{16,24},{20,28},{24,16},{28,20},{1,9},{5... | collective-permute-start | bytes 2359304 | tf_op jit(solution)/shard_map/ppermute | solution.py:334
  347.7 55.2 %collective-permute-start.60 = (bf16[2,2,256,384]{3,2,1,0:T(8,128)(2,1)}, bf16[2,2,256,384]{3,2,1,0:T(8,128)(2,1)S(1)}, u32[]{:S(2)}, u32[]{:S(2)}) collective-permute-start(bf16[2,2,256,384]{3,2,1,0:T(8,128)(2,1)} %get-tuple-element.372), channel_id=1, source_target_pairs={{0,16},{4,20},{8,24},{12,28},{16,0},{20,4},{24,8},{28,12},{1,17},{... | collective-permute-start | bytes 2359304 | tf_op jit(solution)/shard_map/ppermute | solution.py:334
  349.1 53.9 %collective-permute-start.61 = (bf16[2,2,256,384]{3,2,1,0:T(8,128)(2,1)}, bf16[2,2,256,384]{3,2,1,0:T(8,128)(2,1)S(1)}, u32[]{:S(2)}, u32[]{:S(2)}) collective-permute-start(bf16[2,2,256,384]{3,2,1,0:T(8,128)(2,1)} %get-tuple-element.373), channel_id=1, source_target_pairs={{0,24},{4,28},{8,16},{12,20},{16,8},{20,12},{24,0},{28,4},{1,25},{... | collective-permute-start | bytes 2359304 | tf_op jit(solution)/shard_map/ppermute | solution.py:334
  405.9 172.2 %reduce-scatter.8.cloned.1.call-start = ((), (), s32[]{:S(2)}) async-start(), calls=%async_computation.5 | async-start | bytes 5242880 | tf_op jit(solution)/shard_map/reduce_scatter | solution.py:1531
  508.0 55.3 %collective-permute-start.72 = (bf16[2,2,64,2048]{3,2,1,0:T(8,128)(2,1)}, bf16[2,2,64,2048]{3,2,1,0:T(8,128)(2,1)}, u32[]{:S(2)}, u32[]{:S(2)}) collective-permute-start(bf16[2,2,64,2048]{3,2,1,0:T(8,128)(2,1)} %copy-done.62), channel_id=1, source_target_pairs={{0,2},{1,3},{2,0},{3,1},{4,6},{5,7},{6,4},{7,5},{8,10},{9,11},{10,... | collective-permute-start | bytes 3145736 | tf_op jit(solution)/shard_map/ppermute | solution.py:334
  508.5 54.8 %collective-permute-start.73 = (bf16[2,2,64,2048]{3,2,1,0:T(8,128)(2,1)}, bf16[2,2,64,2048]{3,2,1,0:T(8,128)(2,1)}, u32[]{:S(2)}, u32[]{:S(2)}) collective-permute-start(bf16[2,2,64,2048]{3,2,1,0:T(8,128)(2,1)} %copy-done.61), channel_id=1, source_target_pairs={{0,1},{1,0},{2,3},{3,2},{4,5},{5,4},{6,7},{7,6},{8,9},{9,8},{10,11... | collective-permute-start | bytes 3145736 | tf_op jit(solution)/shard_map/ppermute | solution.py:334
  520.2 49.4 %collective-permute-start.74 = (bf16[2,2,64,2048]{3,2,1,0:T(8,128)(2,1)}, bf16[2,2,64,2048]{3,2,1,0:T(8,128)(2,1)}, u32[]{:S(2)}, u32[]{:S(2)}) collective-permute-start(bf16[2,2,64,2048]{3,2,1,0:T(8,128)(2,1)} %get-tuple-element.416), channel_id=1, source_target_pairs={{0,2},{1,3},{2,0},{3,1},{4,6},{5,7},{6,4},{7,5},{8,10},{9,11},{10,... | collective-permute-start | bytes 3145736 | tf_op jit(solution)/shard_map/ppermute | solution.py:334
  521.8 47.8 %collective-permute-start.75 = (bf16[2,2,64,2048]{3,2,1,0:T(8,128)(2,1)}, bf16[2,2,64,2048]{3,2,1,0:T(8,128)(2,1)}, u32[]{:S(2)}, u32[]{:S(2)}) collective-permute-start(bf16[2,2,64,2048]{3,2,1,0:T(8,128)(2,1)} %get-tuple-element.417), channel_id=1, source_target_pairs={{0,1},{1,0},{2,3},{3,2},{4,5},{5,4},{6,7},{7,6},{8,9},{9,8},{10,11... | collective-permute-start | bytes 3145736 | tf_op jit(solution)/shard_map/ppermute | solution.py:334
  522.1 37.0 %collective-permute-start.79 = (f32[4,256]{1,0:T(4,128)S(1)}, f32[4,256]{1,0:T(4,128)S(1)}, u32[]{:S(2)}, u32[]{:S(2)}) collective-permute-start(f32[4,256]{1,0:T(4,128)S(1)} %slice_bitcast_fusion.4), channel_id=1, source_target_pairs={{0,1},{1,0},{2,3},{3,2},{4,5},{5,4},{6,7},{7,6},{8,9},{9,8},{10,11... | collective-permute-start | bytes 12296 | tf_op jit(solution)/shard_map/ppermute | solution.py:334
  (161 other events, 2142.2 us)
Sparse Core Ops, SparseCore 0:
  234.9 106.0 reduce-scatter.3
  406.0 92.3 reduce-scatter.5
  500.8 77.2 reduce-scatter.7

commit v7 on v6

--- a/solution.py
+++ b/solution.py
@@ -674,16 +674,21 @@
             copy.start()
         for fetch in fetches:
             fetch.wait()
-        unit, _ = normalized(x_held[...].astype(F32))
-        norm_ref[...] = (unit * gain_held[...] + shift_held[...]).astype(BF)
-        for part in range(3):
-            copies[part].wait()
-            value = dot(norm_ref[...], weight_ref[part])
-            if part != 1:
-                value += bias_held[part // 2 : part // 2 + 1]
-            value = value.astype(BF)
-            for head in range(heads):
-                held[head, :, part * HD : (part + 1) * HD] = value[:, head * HD : (head + 1) * HD]
+        for start in range(0, rows, tok_len):
+            place = slice(start, start + tok_len)
+            unit, _ = normalized(x_held[place].astype(F32))
+            norm_ref[place] = (unit * gain_held[...] + shift_held[...]).astype(BF)
+            for part in range(3):
+                if start == 0:
+                    copies[part].wait()
+                value = dot(norm_ref[place], weight_ref[part])
+                if part != 1:
+                    value += bias_held[part // 2 : part // 2 + 1]
+                value = value.astype(BF)
+                for head in range(heads):
+                    held[head, place, part * HD : (part + 1) * HD] = value[
+                        :, head * HD : (head + 1) * HD
+                    ]
 
         def load(unit_id):
             return held[unit_id % heads, rows_at(unit_id // heads * tok_len, tok_len), :]

time: 597 us -> 597 us (level)
  no operation moved by 1% of the time
where the time goes in v7:
time: 597 us; the launch traced here: 587 us
  waiting for transfers between devices  205 us (34%)
  Pallas kernels  201 us (34%)
  starting transfers between devices  121 us (20%)
  local copies, waits for them, and re-layouts  44.6 us (7%)
  between operations  15.5 us (3%)
    ppermute x81, waiting for transfers between devices, xor_permute(): return lax.ppermute(values, axis, [(i, i ^ step) for i in range(count)])  204 us
    pallas_call x48, Pallas kernels, launch(): pl.pallas_call(inner, grid_spec=pltpu.PrefetchScalarGridSpec(num_scalar_p...  201 us
    ppermute x81, starting transfers between devices, xor_permute(): return lax.ppermute(values, axis, [(i, i ^ step) for i in range(count)])  121 us
    unnamed x202, local copies, waits for them, and re-layouts  39 us
  transfers between devices with their start and end apart: 84, of which 36 were waited for; matrix products, arithmetic and copies ran while one was open for 1% of the time, Pallas kernels for 32%

profile of v7, /device:TPU:0, one launch (start us, length us, event | category | flops | bytes accessed | tf_op | source)
XLA Modules:
  0.0 587.4 jit_solution(8788868031487282818)
XLA Ops:
  7.2 6.6 %project.2 = (bf16[512,2048]{1,0:T(8,128)(2,1)S(1)}, bf16[256,384]{1,0:T(8,128)(2,1)S(1)}, bf16[256,384]{1,0:T(8,128)(2,1)S(1)}, bf16[2,256,384]{2,1,0:T(8,128)(...) custom-call(s32[1]{0:T(128)} %bitcast.refs_0_.refs_1_, ...), custom_call_target="tpu_custom_call" | custom-call | flops 3221225472 | bytes 3670016 | tf_op jit(solution)/shard_map/project/pallas_call | solution.py:374
  40.4 7.7 %collective-permute-done.1.refs_3_.refs_4_ = bf16[2,256,384]{2,1,0:T(8,128)(2,1)S(1)} collective-permute-done((bf16[2,256,384]{2,1,0:T(8,128)(2,1)S(1)}, bf16[2,256,384]{2,1,0:T(8,128)(2,1)S(1)}, u32[]{:S(2)}, u32[]{:S(2)}) %collective-permute-start.1) | collective-permute-done | bytes 393248 | tf_op jit(solution)/shard_map/ppermute | solution.py:334
  57.8 23.9 %collective-permute-done.5.refs_3_.refs_4_ = bf16[2,256,384]{2,1,0:T(8,128)(2,1)S(1)} collective-permute-done((bf16[2,256,384]{2,1,0:T(8,128)(2,1)S(1)}, bf16[2,256,384]{2,1,0:T(8,128)(2,1)S(1)}, u32[]{:S(2)}, u32[]{:S(2)}) %collective-permute-start.5) | collective-permute-done | bytes 393248 | tf_op jit(solution)/shard_map/ppermute | solution.py:334
  81.9 7.6 %collective-permute-start.8 = (bf16[2,256,128]{2,1,0:T(8,128)(2,1)S(1)}, bf16[2,256,128]{2,1,0:T(8,128)(2,1)S(1)}, u32[]{:S(2)}, u32[]{:S(2)}) collective-permute-start(bf16[2,256,128]{2,1,0:T(8,128)(2,1)S(1)} %get-tuple-element.247), channel_id=1, source_target_pairs={{0,8},{4,12},{8,0},{12,4},{16,24},{20,28},{24,16},{28,20},{1,9},{5... | collective-permute-start | bytes 393224 | tf_op jit(solution)/shard_map/ppermute | solution.py:334
  92.1 6.7 %attention.3 = (bf16[256,128]{1,0:T(8,128)(2,1)S(1)}, bf16[256,128]{1,0:T(8,128)(2,1)S(1)}, bf16[2,256,128]{2,1,0:T(8,128)(2,1)}, bf16[2,256,128]{2,1,0:T(8,128)...) custom-call(f32[8,128]{1,0:T(8,128)S(1)} %get-tuple-element.242.refs_0_, ...), custom_call_target="tpu_custom_call" | custom-call | flops 2147483648 | bytes 2727936 | tf_op jit(solution)/shard_map/attention/pallas_call | solution.py:374
  137.8 13.3 %collective-permute-done.20.refs_2_.refs_3_ = bf16[64,2048]{1,0:T(8,128)(2,1)S(1)} collective-permute-done((bf16[64,2048]{1,0:T(8,128)(2,1)S(1)}, bf16[64,2048]{1,0:T(8,128)(2,1)S(1)}, u32[]{:S(2)}, u32[]{:S(2)}) %collective-permute-start.20) | collective-permute-done | bytes 262176 | tf_op jit(solution)/shard_map/ppermute | solution.py:334
  158.7 11.6 %collective-permute-done.24.refs_2_ = bf16[64,2048]{1,0:T(8,128)(2,1)S(1)} collective-permute-done((bf16[64,2048]{1,0:T(8,128)(2,1)S(1)}, bf16[64,2048]{1,0:T(8,128)(2,1)S(1)}, u32[]{:S(2)}, u32[]{:S(2)}) %collective-permute-start.24) | collective-permute-done | bytes 262176 | tf_op jit(solution)/shard_map/ppermute | solution.py:334
  177.4 20.7 %feed_inner.2 = (bf16[2,512,2048]{2,1,0:T(8,128)(2,1)}, bf16[2,512,2048]{2,1,0:T(8,128)(2,1)}, bf16[2,512,2048]{2,1,0:T(8,128)(2,1)}, f32[1,2048]{1,0:T(1,128)S(...) custom-call(f32[8,128]{1,0:T(8,128)S(1)} %get-tuple-element.284.refs, ...), custom_call_target="tpu_custom_call" | custom-call | flops 12884901888 | bytes 37748736 | tf_op jit(solution)/shard_map/feed_inner/pallas_call | solution.py:374
  202.6 15.3 %feed_inner.3 = (bf16[2,512,2048]{2,1,0:T(8,128)(2,1)}, bf16[2,512,2048]{2,1,0:T(8,128)(2,1)}, bf16[2,512,2048]{2,1,0:T(8,128)(2,1)}, f32[1,2048]{1,0:T(1,128)S(...) custom-call(f32[8,128]{1,0:T(8,128)S(1)} %get-tuple-element.287.refs, ...), custom_call_target="tpu_custom_call", output_to_operand_aliasing={{0}: (10, {}), {1}: (11, {}), {2}: (12, {})} | custom-call | flops 12884901888 | bytes 37748736 | tf_op jit(solution)/shard_map/feed_inner/pallas_call | solution.py:374
  217.9 13.4 %weight_grad.3 = (bf16[2048,2048]{1,0:T(8,128)(2,1)}, f32[8,128]{1,0:T(8,128)S(1)}) custom-call(f32[8,128]{1,0:T(8,128)S(1)} %get-tuple-element.292.refs_0_, bf16[1024,2048]{1,0:T(8,128)(2,1)} %bitcast.90, bf16[1024,2048]{1,0:T(8,128)(2,1)} %bitcast.114), custom_call_target="tpu_custom_call" | custom-call | flops 8589934592 | bytes 16777216 | tf_op jit(solution)/shard_map/weight_grad/pallas_call | solution.py:374
  236.3 8.2 %feed_grad.1 = (bf16[2,64,2048]{2,1,0:T(8,128)(2,1)S(1)}, bf16[2,64,2048]{2,1,0:T(8,128)(2,1)S(1)}, bf16[2,64,2048]{2,1,0:T(8,128)(2,1)S(1)}, bf16[2,64,2048]{2,1,0:T(8,128)(2,1)S(1)}, f32[8,128]{1,0:T(8,128)S(1)}) custom-call(f32[8,128]{1,0:T(8,128)S(1)} %get-tuple-element.300.refs_0_, s32[1]{0:T(128)} %bitcast.9.refs_2_.refs_1_, ...), custom_call_target="tpu_custom_call" | custom-call | flops 4294967296 | bytes 14680064 | tf_op jit(solution)/shard_map/feed_grad/pallas_call | solution.py:374
  248.7 12.6 %feed_out.1 = (bf16[2,2,64,2048]{3,2,1,0:T(8,128)(2,1)S(1)}, bf16[2,2,64,2048]{3,2,1,0:T(8,128)(2,1)S(1)}, bf16[2,2,64,2048]{3,2,1,0:T(8,128)(2,1)S(1)}, bf16[2,...) custom-call(f32[8,128]{1,0:T(8,128)S(1)} %get-tuple-element.305.refs_0_, s32[1]{0:T(128)} %bitcast.9.refs_2_.refs_1_, ...), custom_call_target="tpu_custom_call" | custom-call | flops 8589934592 | bytes 20971520 | tf_op jit(solution)/shard_map/feed_out/pallas_call | solution.py:374
  287.2 14.7 %weight_grad.4 = (bf16[4,256,2048]{2,1,0:T(8,128)(2,1)}, bf16[4,256,2048]{2,1,0:T(8,128)(2,1)}, f32[8,128]{1,0:T(8,128)S(1)}) custom-call(s32[1]{0:T(128)} %bitcast.refs_0_.refs_1_, f32[8,128]{1,0:T(8,128)S(1)} %get-tuple-element.323.refs_1_, bf16[1024,2048]{1,0:T(8,128)(2,1)} %bitcast.113, bf16[1024,2048]{1,0:T(8,128)(2,1)} %bitcast.115), custom_call_target="tpu_custom_call" | custom-call | flops 8589934592 | bytes 16777216 | tf_op jit(solution)/shard_map/weight_grad/pallas_call | solution.py:374
  310.8 9.9 %attention_back.2 = (bf16[2,256,384]{2,1,0:T(8,128)(2,1)S(1)}, bf16[2,256,384]{2,1,0:T(8,128)(2,1)S(1)}, bf16[2,2,256,384]{3,2,1,0:T(8,128)(2,1)S(1)}, bf16[2,2,...) custom-call(f32[8,128]{1,0:T(8,128)S(1)} %get-tuple-element.333.refs_0_, ...), custom_call_target="tpu_custom_call" | custom-call | flops 2684354560 | bytes 3145728 | tf_op jit(solution)/shard_map/attention_back/pallas_call | solution.py:374
  331.4 11.3 %attention_back.3 = (bf16[2,256,384]{2,1,0:T(8,128)(2,1)}, bf16[2,256,384]{2,1,0:T(8,128)(2,1)}, bf16[2,2,256,384]{3,2,1,0:T(8,128)(2,1)}, bf16[2,2,256,384]{3,2...) custom-call(f32[8,128]{1,0:T(8,128)S(1)} %get-tuple-element.351.refs, ...), custom_call_target="tpu_custom_call", output_to_operand_aliasing={{0}: (15, {}), {1}: (16, {}), {2}: (17, {}), {3}: (18, {}),... | custom-call | flops 2684354560 | bytes 3145728 | tf_op jit(solution)/shard_map/attention_back/pallas_call | solution.py:374
  350.1 6.9 %collective-permute-done.56.refs_2_ = bf16[2,64,2048]{2,1,0:T(8,128)(2,1)S(1)} collective-permute-done((bf16[2,64,2048]{2,1,0:T(8,128)(2,1)S(1)}, bf16[2,64,2048]{2,1,0:T(8,128)(2,1)S(1)}, u32[]{:S(2)}, u32[]{:S(2)}) %collective-permute-start.56) | collective-permute-done | bytes 524320 | tf_op jit(solution)/shard_map/ppermute | solution.py:334
  358.8 11.6 %collective-permute-done.57.refs_4_ = bf16[2,64,2048]{2,1,0:T(8,128)(2,1)S(1)} collective-permute-done((bf16[2,64,2048]{2,1,0:T(8,128)(2,1)S(1)}, bf16[2,64,2048]{2,1,0:T(8,128)(2,1)S(1)}, u32[]{:S(2)}, u32[]{:S(2)}) %collective-permute-start.57) | collective-permute-done | bytes 524320 | tf_op jit(solution)/shard_map/ppermute | solution.py:334
  381.8 20.9 %collective-permute-done.60.refs_3_.refs_5_ = bf16[2,2,256,384]{3,2,1,0:T(8,128)(2,1)S(1)} collective-permute-done((bf16[2,2,256,384]{3,2,1,0:T(8,128)(2,1)}, bf16[2,2,256,384]{3,2,1,0:T(8,128)(2,1)S(1)}, u32[]{:S(2)}, u32[]{:S(2)}) %collective-permute-start.60) | collective-permute-done | bytes 786464 | tf_op jit(solution)/shard_map/ppermute | solution.py:334
  415.4 7.7 %project_back.1 = (bf16[512,1536]{1,0:T(8,128)(2,1)S(1)}, bf16[512,1536]{1,0:T(8,128)(2,1)S(1)}, f32[1,1536]{1,0:T(1,128)S(1)}, bf16[2,2,64,2048]{3,2,1,0:T(8,12...) custom-call(f32[8,128]{1,0:T(8,128)S(1)} %get-tuple-element.374.refs, ...), custom_call_target="tpu_custom_call" | custom-call | flops 6442450944 | bytes 17963008 | tf_op jit(solution)/shard_map/project_back/pallas_call | solution.py:374
  428.5 15.5 %weight_grad.5 = (bf16[4,256,2048]{2,1,0:T(8,128)(2,1)}, bf16[4,256,2048]{2,1,0:T(8,128)(2,1)}, f32[8,128]{1,0:T(8,128)S(1)}) custom-call(s32[1]{0:T(128)} %bitcast.refs_0_.refs_1_, f32[8,128]{1,0:T(8,128)S(1)} %get-tuple-element.377.refs_1_, bf16[512,2048]{1,0:T(8,128)(2,1)} %copy-done.75, bf16[512,2048]{1,0:T(8,128)(2,1)} %copy-done.74, ...), custom_call_target="tpu_custom_call" | custom-call | flops 8589934592 | bytes 20971520 | tf_op jit(solution)/shard_map/weight_grad/pallas_call | solution.py:374
  444.0 6.7 %collective-permute-done.63.refs_2_ = bf16[2,2,64,2048]{3,2,1,0:T(8,128)(2,1)S(1)} collective-permute-done((bf16[2,2,64,2048]{3,2,1,0:T(8,128)(2,1)S(1)}, bf16[2,2,64,2048]{3,2,1,0:T(8,128)(2,1)S(1)}, u32[]{:S(2)}, u32[]{:S(2)}) %collective-permute-start.63) | collective-permute-done | bytes 1048608 | tf_op jit(solution)/shard_map/ppermute | solution.py:334
  456.4 10.7 %collective-permute-done.65.refs_2_.refs_3_ = bf16[2,64,2048]{2,1,0:T(8,128)(2,1)S(1)} collective-permute-done((bf16[2,64,2048]{2,1,0:T(8,128)(2,1)S(1)}, bf16[2,64,2048]{2,1,0:T(8,128)(2,1)S(1)}, u32[]{:S(2)}, u32[]{:S(2)}) %collective-permute-start.65) | collective-permute-done | bytes 524320 | tf_op jit(solution)/shard_map/ppermute | solution.py:334
  482.3 18.3 %collective-permute-start.76 = (f32[4,8,256]{2,1,0:T(8,128)S(1)}, f32[4,8,256]{2,1,0:T(8,128)S(1)}, u32[]{:S(2)}, u32[]{:S(2)}) collective-permute-start(f32[4,8,256]{2,1,0:T(8,128)S(1)} %dynamic-slice_bitcast_fusion.4), channel_id=1, source_target_pairs={{0,16},{4,20},{8,24},{12,28},{16,0},{20,4},{24,8},{28,12},{1,17},{... | collective-permute-start | bytes 98312 | tf_op jit(solution)/shard_map/ppermute | solution.py:334
  524.1 34.7 %collective-permute-done.79 = f32[4,256]{1,0:T(4,128)S(1)} collective-permute-done((f32[4,256]{1,0:T(4,128)S(1)}, f32[4,256]{1,0:T(4,128)S(1)}, u32[]{:S(2)}, u32[]{:S(2)}) %collective-permute-start.79) | collective-permute-done | bytes 4128 | tf_op jit(solution)/shard_map/ppermute | solution.py:334
  (425 shorter events, 255.6 us)
Async XLA Ops:
  7.2 559.1 %reduce-scatter.4.cloned.1.call-start = ((), (), s32[]{:S(2)}) async-start(), calls=%async_computation.3 | async-start | bytes 9437184 | tf_op jit(solution)/shard_map/reduce_scatter | solution.py:1532
  18.2 29.8 %collective-permute-start.1 = (bf16[2,256,384]{2,1,0:T(8,128)(2,1)S(1)}, bf16[2,256,384]{2,1,0:T(8,128)(2,1)S(1)}, u32[]{:S(2)}, u32[]{:S(2)}) collective-permute-start(bf16[2,256,384]{2,1,0:T(8,128)(2,1)S(1)} %get-tuple-element.232), channel_id=1, source_target_pairs={{0,16},{4,20},{8,24},{12,28},{16,0},{20,4},{24,8},{28,12},{1,17},{... | collective-permute-start | bytes 1179656 | tf_op jit(solution)/shard_map/ppermute | solution.py:334
  20.8 27.3 %collective-permute-start.2 = (bf16[2,256,384]{2,1,0:T(8,128)(2,1)S(1)}, bf16[2,256,384]{2,1,0:T(8,128)(2,1)S(1)}, u32[]{:S(2)}, u32[]{:S(2)}) collective-permute-start(bf16[2,256,384]{2,1,0:T(8,128)(2,1)S(1)} %get-tuple-element.233), channel_id=1, source_target_pairs={{0,24},{4,28},{8,16},{12,20},{16,8},{20,12},{24,0},{28,4},{1,25},{... | collective-permute-start | bytes 1179656 | tf_op jit(solution)/shard_map/ppermute | solution.py:334
  27.4 30.4 %collective-permute-start.4 = (bf16[2,256,384]{2,1,0:T(8,128)(2,1)S(1)}, bf16[2,256,384]{2,1,0:T(8,128)(2,1)S(1)}, u32[]{:S(2)}, u32[]{:S(2)}) collective-permute-start(bf16[2,256,384]{2,1,0:T(8,128)(2,1)S(1)} %get-tuple-element.239), channel_id=1, source_target_pairs={{0,8},{4,12},{8,0},{12,4},{16,24},{20,28},{24,16},{28,20},{1,9},{5... | collective-permute-start | bytes 1179656 | tf_op jit(solution)/shard_map/ppermute | solution.py:334
  28.4 53.4 %collective-permute-start.5 = (bf16[2,256,384]{2,1,0:T(8,128)(2,1)S(1)}, bf16[2,256,384]{2,1,0:T(8,128)(2,1)S(1)}, u32[]{:S(2)}, u32[]{:S(2)}) collective-permute-start(bf16[2,256,384]{2,1,0:T(8,128)(2,1)S(1)} %get-tuple-element.240), channel_id=1, source_target_pairs={{0,16},{4,20},{8,24},{12,28},{16,0},{20,4},{24,8},{28,12},{1,17},{... | collective-permute-start | bytes 1179656 | tf_op jit(solution)/shard_map/ppermute | solution.py:334
  35.8 46.0 %collective-permute-start.6 = (bf16[2,256,384]{2,1,0:T(8,128)(2,1)S(1)}, bf16[2,256,384]{2,1,0:T(8,128)(2,1)S(1)}, u32[]{:S(2)}, u32[]{:S(2)}) collective-permute-start(bf16[2,256,384]{2,1,0:T(8,128)(2,1)S(1)} %get-tuple-element.241), channel_id=1, source_target_pairs={{0,24},{4,28},{8,16},{12,20},{16,8},{20,12},{24,0},{28,4},{1,25},{... | collective-permute-start | bytes 1179656 | tf_op jit(solution)/shard_map/ppermute | solution.py:334
  173.0 26.5 %collective-permute-start.30 = (bf16[128,2048]{1,0:T(8,128)(2,1)S(1)}, bf16[128,2048]{1,0:T(8,128)(2,1)S(1)}, u32[]{:S(2)}, u32[]{:S(2)}) collective-permute-start(bf16[128,2048]{1,0:T(8,128)(2,1)S(1)} %get-tuple-element.288.refs_2_), channel_id=1, source_target_pairs={{0,3},{1,2},{2,1},{3,0},{4,7},{5,6},{6,5},{7,4},{8,11},{9,10},{10,... | collective-permute-start | bytes 1572872 | tf_op jit(solution)/shard_map/ppermute | solution.py:334
  173.7 27.9 %collective-permute-start.29 = (bf16[128,2048]{1,0:T(8,128)(2,1)S(1)}, bf16[128,2048]{1,0:T(8,128)(2,1)S(1)}, u32[]{:S(2)}, u32[]{:S(2)}) collective-permute-start(bf16[128,2048]{1,0:T(8,128)(2,1)S(1)} %get-tuple-element.288.refs_2_), channel_id=1, source_target_pairs={{0,2},{1,3},{2,0},{3,1},{4,6},{5,7},{6,4},{7,5},{8,10},{9,11},{10,... | collective-permute-start | bytes 1572872 | tf_op jit(solution)/shard_map/ppermute | solution.py:334
  175.0 26.6 %collective-permute-start.28 = (bf16[128,2048]{1,0:T(8,128)(2,1)S(1)}, bf16[128,2048]{1,0:T(8,128)(2,1)S(1)}, u32[]{:S(2)}, u32[]{:S(2)}) collective-permute-start(bf16[128,2048]{1,0:T(8,128)(2,1)S(1)} %get-tuple-element.288.refs_2_), channel_id=1, source_target_pairs={{0,1},{1,0},{2,3},{3,2},{4,5},{5,4},{6,7},{7,6},{8,9},{9,8},{10,11... | collective-permute-start | bytes 1572872 | tf_op jit(solution)/shard_map/ppermute | solution.py:334
  198.1 33.2 %collective-permute-start.31 = (bf16[128,2048]{1,0:T(8,128)(2,1)S(1)}, bf16[128,2048]{1,0:T(8,128)(2,1)S(1)}, u32[]{:S(2)}, u32[]{:S(2)}) collective-permute-start(bf16[128,2048]{1,0:T(8,128)(2,1)S(1)} %get-tuple-element.296), channel_id=1, source_target_pairs={{0,1},{1,0},{2,3},{3,2},{4,5},{5,4},{6,7},{7,6},{8,9},{9,8},{10,11... | collective-permute-start | bytes 1572872 | tf_op jit(solution)/shard_map/ppermute | solution.py:334
  198.8 32.5 %collective-permute-start.32 = (bf16[128,2048]{1,0:T(8,128)(2,1)S(1)}, bf16[128,2048]{1,0:T(8,128)(2,1)S(1)}, u32[]{:S(2)}, u32[]{:S(2)}) collective-permute-start(bf16[128,2048]{1,0:T(8,128)(2,1)S(1)} %get-tuple-element.297), channel_id=1, source_target_pairs={{0,2},{1,3},{2,0},{3,1},{4,6},{5,7},{6,4},{7,5},{8,10},{9,11},{10,... | collective-permute-start | bytes 1572872 | tf_op jit(solution)/shard_map/ppermute | solution.py:334
  199.5 31.8 %collective-permute-start.33 = (bf16[128,2048]{1,0:T(8,128)(2,1)S(1)}, bf16[128,2048]{1,0:T(8,128)(2,1)S(1)}, u32[]{:S(2)}, u32[]{:S(2)}) collective-permute-start(bf16[128,2048]{1,0:T(8,128)(2,1)S(1)} %get-tuple-element.298), channel_id=1, source_target_pairs={{0,3},{1,2},{2,1},{3,0},{4,7},{5,6},{6,5},{7,4},{8,11},{9,10},{10,... | collective-permute-start | bytes 1572872 | tf_op jit(solution)/shard_map/ppermute | solution.py:334
  234.5 339.8 %reduce-scatter.6.cloned.1.call-start = ((), (), s32[]{:S(2)}) async-start(), calls=%async_computation.4 | async-start | bytes 5242880 | tf_op jit(solution)/shard_map/reduce_scatter | solution.py:1536
  276.1 25.8 %collective-permute-start.44 = (bf16[2,256,128]{2,1,0:T(8,128)(2,1)S(1)}, bf16[2,256,128]{2,1,0:T(8,128)(2,1)S(1)}, u32[]{:S(2)}, u32[]{:S(2)}) collective-permute-start(bf16[2,256,128]{2,1,0:T(8,128)(2,1)S(1)} %get-tuple-element.327), channel_id=1, source_target_pairs={{0,8},{4,12},{8,0},{12,4},{16,24},{20,28},{24,16},{28,20},{1,9},{5... | collective-permute-start | bytes 393224 | tf_op jit(solution)/shard_map/ppermute | solution.py:334
  342.7 28.1 %collective-permute-start.58 = (bf16[4,256,2048]{2,1,0:T(8,128)(2,1)S(1)}, bf16[4,256,2048]{2,1,0:T(8,128)(2,1)S(1)}, u32[]{:S(2)}, u32[]{:S(2)}) collective-permute-start(bf16[4,256,2048]{2,1,0:T(8,128)(2,1)S(1)} %copy-done.92), channel_id=1, source_target_pairs={{0,4},{4,0},{8,12},{12,8},{16,20},{20,16},{24,28},{28,24},{1,5},{5... | collective-permute-start | bytes 12582920 | tf_op jit(solution)/shard_map/ppermute | solution.py:334
  343.4 38.5 %collective-permute-start.59 = (bf16[2,2,256,384]{3,2,1,0:T(8,128)(2,1)}, bf16[2,2,256,384]{3,2,1,0:T(8,128)(2,1)S(1)}, u32[]{:S(2)}, u32[]{:S(2)}) collective-permute-start(bf16[2,2,256,384]{3,2,1,0:T(8,128)(2,1)} %get-tuple-element.371), channel_id=1, source_target_pairs={{0,8},{4,12},{8,0},{12,4},{16,24},{20,28},{24,16},{28,20},{1,9},{5... | collective-permute-start | bytes 2359304 | tf_op jit(solution)/shard_map/ppermute | solution.py:334
  347.4 55.2 %collective-permute-start.60 = (bf16[2,2,256,384]{3,2,1,0:T(8,128)(2,1)}, bf16[2,2,256,384]{3,2,1,0:T(8,128)(2,1)S(1)}, u32[]{:S(2)}, u32[]{:S(2)}) collective-permute-start(bf16[2,2,256,384]{3,2,1,0:T(8,128)(2,1)} %get-tuple-element.372), channel_id=1, source_target_pairs={{0,16},{4,20},{8,24},{12,28},{16,0},{20,4},{24,8},{28,12},{1,17},{... | collective-permute-start | bytes 2359304 | tf_op jit(solution)/shard_map/ppermute | solution.py:334
  348.7 54.0 %collective-permute-start.61 = (bf16[2,2,256,384]{3,2,1,0:T(8,128)(2,1)}, bf16[2,2,256,384]{3,2,1,0:T(8,128)(2,1)S(1)}, u32[]{:S(2)}, u32[]{:S(2)}) collective-permute-start(bf16[2,2,256,384]{3,2,1,0:T(8,128)(2,1)} %get-tuple-element.373), channel_id=1, source_target_pairs={{0,24},{4,28},{8,16},{12,20},{16,8},{20,12},{24,0},{28,4},{1,25},{... | collective-permute-start | bytes 2359304 | tf_op jit(solution)/shard_map/ppermute | solution.py:334
  405.6 172.1 %reduce-scatter.8.cloned.1.call-start = ((), (), s32[]{:S(2)}) async-start(), calls=%async_computation.5 | async-start | bytes 5242880 | tf_op jit(solution)/shard_map/reduce_scatter | solution.py:1536
  507.7 55.3 %collective-permute-start.72 = (bf16[2,2,64,2048]{3,2,1,0:T(8,128)(2,1)}, bf16[2,2,64,2048]{3,2,1,0:T(8,128)(2,1)}, u32[]{:S(2)}, u32[]{:S(2)}) collective-permute-start(bf16[2,2,64,2048]{3,2,1,0:T(8,128)(2,1)} %copy-done.62), channel_id=1, source_target_pairs={{0,2},{1,3},{2,0},{3,1},{4,6},{5,7},{6,4},{7,5},{8,10},{9,11},{10,... | collective-permute-start | bytes 3145736 | tf_op jit(solution)/shard_map/ppermute | solution.py:334
  508.1 54.8 %collective-permute-start.73 = (bf16[2,2,64,2048]{3,2,1,0:T(8,128)(2,1)}, bf16[2,2,64,2048]{3,2,1,0:T(8,128)(2,1)}, u32[]{:S(2)}, u32[]{:S(2)}) collective-permute-start(bf16[2,2,64,2048]{3,2,1,0:T(8,128)(2,1)} %copy-done.61), channel_id=1, source_target_pairs={{0,1},{1,0},{2,3},{3,2},{4,5},{5,4},{6,7},{7,6},{8,9},{9,8},{10,11... | collective-permute-start | bytes 3145736 | tf_op jit(solution)/shard_map/ppermute | solution.py:334
  519.8 49.4 %collective-permute-start.74 = (bf16[2,2,64,2048]{3,2,1,0:T(8,128)(2,1)}, bf16[2,2,64,2048]{3,2,1,0:T(8,128)(2,1)}, u32[]{:S(2)}, u32[]{:S(2)}) collective-permute-start(bf16[2,2,64,2048]{3,2,1,0:T(8,128)(2,1)} %get-tuple-element.416), channel_id=1, source_target_pairs={{0,2},{1,3},{2,0},{3,1},{4,6},{5,7},{6,4},{7,5},{8,10},{9,11},{10,... | collective-permute-start | bytes 3145736 | tf_op jit(solution)/shard_map/ppermute | solution.py:334
  521.4 47.8 %collective-permute-start.75 = (bf16[2,2,64,2048]{3,2,1,0:T(8,128)(2,1)}, bf16[2,2,64,2048]{3,2,1,0:T(8,128)(2,1)}, u32[]{:S(2)}, u32[]{:S(2)}) collective-permute-start(bf16[2,2,64,2048]{3,2,1,0:T(8,128)(2,1)} %get-tuple-element.417), channel_id=1, source_target_pairs={{0,1},{1,0},{2,3},{3,2},{4,5},{5,4},{6,7},{7,6},{8,9},{9,8},{10,11... | collective-permute-start | bytes 3145736 | tf_op jit(solution)/shard_map/ppermute | solution.py:334
  521.7 37.0 %collective-permute-start.79 = (f32[4,256]{1,0:T(4,128)S(1)}, f32[4,256]{1,0:T(4,128)S(1)}, u32[]{:S(2)}, u32[]{:S(2)}) collective-permute-start(f32[4,256]{1,0:T(4,128)S(1)} %slice_bitcast_fusion.4), channel_id=1, source_target_pairs={{0,1},{1,0},{2,3},{3,2},{4,5},{5,4},{6,7},{7,6},{8,9},{9,8},{10,11... | collective-permute-start | bytes 12296 | tf_op jit(solution)/shard_map/ppermute | solution.py:334
  (161 other events, 2142.4 us)
Sparse Core Ops, SparseCore 0:
  234.6 106.0 reduce-scatter.3
  405.7 92.2 reduce-scatter.5
  500.4 77.2 reduce-scatter.7
